TPU v7x, 256 devices: a whole 4x4x8 slice. The times are simulated.
256 devices in a mesh: frame: 16 (over y, z_hi, core), patch: 16 (over x, z_lo).
Axes of the slice: x: 4, y: 4, z: 8 (z_hi: 2, z_lo: 4; z = z_hi * 4 + z_lo), core: 2. Of those that a mesh axis runs over, the one named last changes fastest.
Arguments:
- q_space: bfloat16 [128, 8, 1024, 128], P('frame', None, 'patch'), may hold values from -8 to 8
- k_space: bfloat16 [128, 8, 1024, 128], P('frame', None, 'patch'), may hold values from -8 to 8
- v_space: bfloat16 [128, 8, 1024, 128], P('frame', None, 'patch'), may hold values from -6 to 6
- d_out_space: bfloat16 [128, 8, 1024, 128], P('frame', None, 'patch'), may hold values from -6 to 6
- q_time: bfloat16 [128, 8, 1024, 128], P('frame', None, 'patch'), may hold values from -8 to 8
- k_time: bfloat16 [128, 8, 1024, 128], P('frame', None, 'patch'), may hold values from -8 to 8
- v_time: bfloat16 [128, 8, 1024, 128], P('frame', None, 'patch'), may hold values from -6 to 6
- d_out_time: bfloat16 [128, 8, 1024, 128], P('frame', None, 'patch'), may hold values from -6 to 6
Outputs:
- grad_q_space: bfloat16 [128, 8, 1024, 128], P('frame', None, 'patch')
- grad_k_space: bfloat16 [128, 8, 1024, 128], P('frame', None, 'patch')
- grad_v_space: bfloat16 [128, 8, 1024, 128], P('frame', None, 'patch')
- grad_q_time: bfloat16 [128, 8, 1024, 128], P('frame', None, 'patch')
- grad_k_time: bfloat16 [128, 8, 1024, 128], P('frame', None, 'patch')
- grad_v_time: bfloat16 [128, 8, 1024, 128], P('frame', None, 'patch')
All inputs are finite; a program needn't handle non-finite values.
Results may differ from a plain program's by a relative error of at most 0.0071.
Values may be sent and summed in bfloat16 or wider, within the bound.
No kernel may reach another device: no remote copies, remote signals or barrier semaphores. Data moves between devices by JAX's collectives and lax.ppermute only.
A program may use at most 128 MiB of HBM per device.

v0:
```python
import math

import jax
import jax.numpy as jnp
from jax import lax
from jax.sharding import PartitionSpec as P

SPACE_FORM = ("giqd", "gikd", "giqk")
TIME_FORM = ("qhpd", "khpd", "hpqk")


def contract(first_form, second_form, result_form, left, right):
    return jnp.einsum(
        first_form + "," + second_form + "->" + result_form,
        left,
        right,
        preferred_element_type=jnp.float32,
    )


def forward_pass(queries, key_rows, values, layout, causal):
    inverse_root_scale = 1.0 / math.sqrt(queries.shape[-1])
    score_logits = contract(layout[0], layout[1], layout[2], queries, key_rows) * inverse_root_scale
    if causal:
        length = score_logits.shape[-1]
        allowed = jnp.arange(length)[:, None] >= jnp.arange(length)[None, :]
        score_logits = jnp.where(allowed, score_logits, -1e30)
    row_max = jnp.max(score_logits, axis=-1, keepdims=True)
    raised = jnp.exp(score_logits - row_max)
    softmax_rows = raised / jnp.sum(raised, axis=-1, keepdims=True)
    weight_probabilities = softmax_rows.astype(jnp.bfloat16)
    output_tensor = contract(layout[2], layout[1], layout[0], weight_probabilities, values)
    return (softmax_rows, weight_probabilities, output_tensor)


def backward_pass(queries, key_rows, values, out_grad, state, layout):
    softmax_rows, weight_probabilities, output_tensor = state
    inverse_root_scale = 1.0 / math.sqrt(queries.shape[-1])
    delta_rows = jnp.einsum(
        layout[0] + "," + layout[0] + "->" + layout[2][:-1],
        out_grad.astype(jnp.float32),
        output_tensor,
    )
    value_gradient = contract(
        layout[2], layout[0], layout[1], weight_probabilities, out_grad
    ).astype(jnp.bfloat16)
    probability_gradient = contract(layout[0], layout[1], layout[2], out_grad, values)
    logit_gradient = (softmax_rows * (probability_gradient - delta_rows[..., None])).astype(
        jnp.bfloat16
    )
    query_gradient = (
        contract(layout[2], layout[1], layout[0], logit_gradient, key_rows) * inverse_root_scale
    ).astype(jnp.bfloat16)
    key_gradient = (
        contract(layout[2], layout[0], layout[1], logit_gradient, queries) * inverse_root_scale
    ).astype(jnp.bfloat16)
    return (query_gradient, key_gradient, value_gradient)


def attention_grads(queries, key_rows, values, out_grad, layout, causal):
    state = forward_pass(queries, key_rows, values, layout, causal)
    return backward_pass(queries, key_rows, values, out_grad, state, layout)


def space_items(parts):
    return attention_grads(parts[0], parts[1], parts[2], parts[3], SPACE_FORM, False)


def time_items(parts):
    return attention_grads(parts[0], parts[1], parts[2], parts[3], TIME_FORM, True)


def per_device(q_space, k_space, v_space, d_out_space, q_time, k_time, v_time, d_out_time):
    frame_dev, head_count, patch_dev, head_dim = q_space.shape
    patch_devices = lax.axis_size("patch")
    per_group = frame_dev * head_count // patch_devices

    def regroup(block):
        return block.reshape(patch_devices, per_group, patch_dev, head_dim)

    space_grads = space_items(
        (
            lax.all_to_all(regroup(q_space), "patch", split_axis=0, concat_axis=2, tiled=True),
            lax.all_to_all(regroup(k_space), "patch", split_axis=0, concat_axis=2, tiled=True),
            lax.all_to_all(regroup(v_space), "patch", split_axis=0, concat_axis=2, tiled=True),
            lax.all_to_all(regroup(d_out_space), "patch", split_axis=0, concat_axis=2, tiled=True),
        )
    )
    time_grads = time_items(
        (
            lax.all_to_all(q_time, "frame", split_axis=2, concat_axis=0, tiled=True),
            lax.all_to_all(k_time, "frame", split_axis=2, concat_axis=0, tiled=True),
            lax.all_to_all(v_time, "frame", split_axis=2, concat_axis=0, tiled=True),
            lax.all_to_all(d_out_time, "frame", split_axis=2, concat_axis=0, tiled=True),
        )
    )
    space_back = (
        lax.all_to_all(space_grads[0], "patch", split_axis=2, concat_axis=0, tiled=True),
        lax.all_to_all(space_grads[1], "patch", split_axis=2, concat_axis=0, tiled=True),
        lax.all_to_all(space_grads[2], "patch", split_axis=2, concat_axis=0, tiled=True),
    )
    time_back = (
        lax.all_to_all(time_grads[0], "frame", split_axis=0, concat_axis=2, tiled=True),
        lax.all_to_all(time_grads[1], "frame", split_axis=0, concat_axis=2, tiled=True),
        lax.all_to_all(time_grads[2], "frame", split_axis=0, concat_axis=2, tiled=True),
    )
    shape_dev = (frame_dev, head_count, patch_dev, head_dim)
    return (
        space_back[0].reshape(shape_dev),
        space_back[1].reshape(shape_dev),
        space_back[2].reshape(shape_dev),
        time_back[0],
        time_back[1],
        time_back[2],
    )


def solution(mesh):
    in_specs = (
        P("frame", None, "patch", None),
        P("frame", None, "patch", None),
        P("frame", None, "patch", None),
        P("frame", None, "patch", None),
        P("frame", None, "patch", None),
        P("frame", None, "patch", None),
        P("frame", None, "patch", None),
        P("frame", None, "patch", None),
    )
    out_specs = (
        P("frame", None, "patch", None),
        P("frame", None, "patch", None),
        P("frame", None, "patch", None),
        P("frame", None, "patch", None),
        P("frame", None, "patch", None),
        P("frame", None, "patch", None),
    )
    return jax.shard_map(
        per_device, mesh=mesh, in_specs=in_specs, out_specs=out_specs, check_vma=False
    )
```

profile of v0, /device:TPU:68, one launch (start us, length us, event | category | flops | bytes accessed | tf_op | source)
XLA Modules:
  0.0 460.2 jit_solution(12879932563144421262)
XLA Ops:
  0.7 31.7 %all_to_all.231 = bf16[16,4,64,128]{3,2,1,0:T(8,128)(2,1)S(1)} all-to-all(bf16[16,4,64,128]{3,2,1,0:T(8,128)(2,1)} %bitcast.140), channel_id=1, replica_groups=mesh['frame'=16,'patch'=16] {'patch'}, dimensions={0} | all-to-all | bytes 2097152 | tf_op jit(solution)/shard_map/all_to_all | solution.py:86
  32.4 30.2 %all_to_all.232 = bf16[16,4,64,128]{3,2,1,0:T(8,128)(2,1)S(1)} all-to-all(bf16[16,4,64,128]{3,2,1,0:T(8,128)(2,1)S(1)} %bitcast.141), channel_id=1, replica_groups=mesh['frame'=16,'patch'=16] {'patch'}, dimensions={0} | all-to-all | bytes 2097152 | tf_op jit(solution)/shard_map/all_to_all | solution.py:85
  62.6 30.3 %all_to_all.233 = bf16[16,4,64,128]{3,2,1,0:T(8,128)(2,1)} all-to-all(bf16[16,4,64,128]{3,2,1,0:T(8,128)(2,1)S(1)} %bitcast.142), channel_id=1, replica_groups=mesh['frame'=16,'patch'=16] {'patch'}, dimensions={0} | all-to-all | bytes 2097152 | tf_op jit(solution)/shard_map/all_to_all | solution.py:83
  92.9 7.7 %all-to-all-start.1 = ((bf16[16,4,64,128]{3,2,1,0:T(8,128)(2,1)}), bf16[16,4,64,128]{3,2,1,0:T(8,128)(2,1)S(1)}, u32[]{:S(2)}, u32[]{:S(2)}) async-start(bf16[16,4,64,128]{3,2,1,0:T(8,128)(2,1)} %bitcast.143), calls=%async_computation.1 | async-start | bytes 2097152 | tf_op jit(solution)/shard_map/all_to_all | solution.py:84
  103.5 19.0 %all-to-all-done.1 = bf16[16,4,64,128]{3,2,1,0:T(8,128)(2,1)S(1)} async-done(((bf16[16,4,64,128]{3,2,1,0:T(8,128)(2,1)}), bf16[16,4,64,128]{3,2,1,0:T(8,128)(2,1)S(1)}, u32[]{:S(2)}, u32[]{:S(2)}) %all-to-all-start.1) | async-done | bytes 1048608 | tf_op jit(solution)/shard_map/all_to_all | solution.py:84
  122.5 8.6 %all-to-all-start.10 = ((bf16[8,8,64,128]{3,1,0,2:T(8,128)(2,1)}), bf16[8,8,64,128]{3,1,0,2:T(8,128)(2,1)}, u32[]{:S(2)}, u32[]{:S(2)}) async-start(bf16[8,8,64,128]{3,1,0,2:T(8,128)(2,1)} %copy.99), calls=%async_computation.10 | async-start | bytes 2097152 | tf_op jit(solution)/shard_map/all_to_all | solution.py:93
  133.9 27.8 %all-to-all-done.10 = bf16[8,8,64,128]{3,1,0,2:T(8,128)(2,1)} async-done(((bf16[8,8,64,128]{3,1,0,2:T(8,128)(2,1)}), bf16[8,8,64,128]{3,1,0,2:T(8,128)(2,1)}, u32[]{:S(2)}, u32[]{:S(2)}) %all-to-all-start.10) | async-done | bytes 1048608 | tf_op jit(solution)/shard_map/all_to_all | solution.py:93
  161.8 4.3 all-to-all-start.9
  172.9 9.9 %fusion.54 = (f32[4,1024]{1,0:T(4,128)S(1)}, f32[4,1024,1024]{1,2,0:T(8,128)}) fusion(bf16[4,1024,128]{2,1,0:T(8,128)(2,1)} %bitcast.144, bf16[4,1024,128]{2,1,0:T(8,128)(2,1)} %bitcast.149), kind=kOutput, calls=%fused_computation.54 | convolution fusion | flops 1086325760 | bytes 18890752 | tf_op jit(solution)/shard_map/sub | solution.py:29
  182.8 14.9 %all-to-all-done.9 = bf16[8,8,64,128]{3,1,0,2:T(8,128)(2,1)} async-done(((bf16[8,8,64,128]{3,1,0,2:T(8,128)(2,1)}), bf16[8,8,64,128]{3,1,0,2:T(8,128)(2,1)}, u32[]{:S(2)}, u32[]{:S(2)}) %all-to-all-start.9) | async-done | bytes 1048608 | tf_op jit(solution)/shard_map/all_to_all | solution.py:94
  197.7 3.7 all-to-all-start.8
  201.4 6.8 %fusion.6 = bf16[4,1024,1024]{1,2,0:T(8,128)(2,1)S(1)} fusion(f32[4,1024,1024]{1,2,0:T(8,128)} %get-tuple-element.19, f32[4,1024]{1,0:T(4,128)S(1)} %get-tuple-element.18), kind=kLoop, calls=%fused_computation.8 | loop fusion | flops 8388608 | bytes 25182208 | tf_op jit(solution)/shard_map/convert_element_type | solution.py:31
  215.5 14.7 %all-to-all-done.8 = bf16[8,8,64,128]{3,1,0,2:T(8,128)(2,1)S(1)} async-done(((bf16[8,8,64,128]{3,1,0,2:T(8,128)(2,1)}), bf16[8,8,64,128]{3,1,0,2:T(8,128)(2,1)S(1)}, u32[]{:S(2)}, u32[]{:S(2)}) %all-to-all-start.8) | async-done | bytes 1048608 | tf_op jit(solution)/shard_map/all_to_all | solution.py:92
  230.2 3.8 all-to-all-start.7
  234.0 9.9 %multiply_convert_fusion = bf16[4,1024,1024]{1,2,0:T(8,128)(2,1)} fusion(bf16[4,1024,128]{2,1,0:T(8,128)(2,1)S(1)} %bitcast.148, bf16[4,1024,128]{2,1,0:T(8,128)(2,1)} %bitcast.155, f32[4,1024]{1,0:T(4,128)S(1)} %multiply_reduce_fusion.2, f32[4,1024,1024]{1,2,0:T(8,128)} %get-tuple-element.19, f32[4,1024]{1,0:T(4,128)S(1)} %get-tuple-element.18), kind=kOutput, calls=%fused_computation.2 | convolution fusion | flops 1090519040 | bytes 27295744 | tf_op jit(solution)/shard_map/giqd,gikd->giqk/dot_general | solution.py:13
  244.0 6.4 %fusion.10 = bf16[1,4,1024,128]{3,2,1,0:T(8,128)(2,1)S(1)} fusion(bf16[4,1024,1024]{1,2,0:T(8,128)(2,1)} %multiply_convert_fusion, bf16[4,1024,128]{2,1,0:T(8,128)(2,1)S(1)} %bitcast.150), kind=kOutput, calls=%fused_computation.23 | convolution fusion | flops 1074790400 | bytes 10485760 | tf_op jit(solution)/shard_map/giqk,gikd->giqd/dot_general | solution.py:13
  252.1 4.4 all-to-all-done.7
  256.5 11.7 %all-to-all-start.4 = ((bf16[1,4,1024,128]{3,1,0,2:T(4,128)(2,1)}), bf16[1,4,1024,128]{3,1,0,2:T(4,128)(2,1)S(1)}, u32[]{:S(2)}, u32[]{:S(2)}) async-start(bf16[1,4,1024,128]{3,1,0,2:T(4,128)(2,1)} %copy.87), calls=%async_computation.4 | async-start | bytes 2097152 | tf_op jit(solution)/shard_map/all_to_all | solution.py:98
  268.3 5.9 %fusion.11 = bf16[1,4,1024,128]{3,2,1,0:T(8,128)(2,1)S(1)} fusion(bf16[4,1024,1024]{1,2,0:T(8,128)(2,1)} %multiply_convert_fusion, bf16[4,1024,128]{2,1,0:T(8,128)(2,1)} %bitcast.145), kind=kOutput, calls=%fused_computation.24 | convolution fusion | flops 1074790400 | bytes 10485760 | tf_op jit(solution)/shard_map/giqk,giqd->gikd/dot_general | solution.py:13
  276.0 15.2 %all-to-all-done.4 = bf16[1,4,1024,128]{3,1,0,2:T(4,128)(2,1)S(1)} async-done(((bf16[1,4,1024,128]{3,1,0,2:T(4,128)(2,1)}), bf16[1,4,1024,128]{3,1,0,2:T(4,128)(2,1)S(1)}, u32[]{:S(2)}, u32[]{:S(2)}) %all-to-all-start.4) | async-done | bytes 1048608 | tf_op jit(solution)/shard_map/all_to_all | solution.py:98
  291.1 9.3 %all-to-all-start.5 = ((bf16[1,4,1024,128]{3,1,0,2:T(4,128)(2,1)}), bf16[1,4,1024,128]{3,1,0,2:T(4,128)(2,1)}, u32[]{:S(2)}, u32[]{:S(2)}) async-start(bf16[1,4,1024,128]{3,1,0,2:T(4,128)(2,1)} %copy.89), calls=%async_computation.5 | async-start | bytes 2097152 | tf_op jit(solution)/shard_map/all_to_all | solution.py:99
  300.5 5.9 %fusion.8 = bf16[1,4,1024,128]{3,2,1,0:T(8,128)(2,1)S(1)} fusion(bf16[4,1024,1024]{1,2,0:T(8,128)(2,1)} %copy-done, bf16[4,1024,128]{2,1,0:T(8,128)(2,1)} %bitcast.147), kind=kOutput, calls=%fused_computation.21 | convolution fusion | flops 1074266112 | bytes 10485760 | tf_op jit(solution)/shard_map/giqk,giqd->gikd/dot_general | solution.py:13
  308.2 14.5 %all-to-all-done.5 = bf16[1,4,1024,128]{3,1,0,2:T(4,128)(2,1)} async-done(((bf16[1,4,1024,128]{3,1,0,2:T(4,128)(2,1)}), bf16[1,4,1024,128]{3,1,0,2:T(4,128)(2,1)}, u32[]{:S(2)}, u32[]{:S(2)}) %all-to-all-start.5) | async-done | bytes 1048608 | tf_op jit(solution)/shard_map/all_to_all | solution.py:99
  322.7 9.3 %all-to-all-start.6 = ((bf16[1,4,1024,128]{3,1,0,2:T(4,128)(2,1)}), bf16[1,4,1024,128]{3,1,0,2:T(4,128)(2,1)}, u32[]{:S(2)}, u32[]{:S(2)}) async-start(bf16[1,4,1024,128]{3,1,0,2:T(4,128)(2,1)} %copy.91), calls=%async_computation.6 | async-start | bytes 2097152 | tf_op jit(solution)/shard_map/all_to_all | solution.py:100
  334.5 3.3 multiply_reduce_fusion.1
  344.4 9.8 %all-to-all-done.6 = bf16[1,4,1024,128]{3,1,0,2:T(4,128)(2,1)} async-done(((bf16[1,4,1024,128]{3,1,0,2:T(4,128)(2,1)}), bf16[1,4,1024,128]{3,1,0,2:T(4,128)(2,1)}, u32[]{:S(2)}, u32[]{:S(2)}) %all-to-all-start.6) | async-done | bytes 1048608 | tf_op jit(solution)/shard_map/all_to_all | solution.py:100
  354.2 4.3 all-to-all-start.11
  361.1 28.0 %all-to-all-done.11 = bf16[128,8,4,128]{3,2,1,0:T(4,128)(2,1)} async-done(((bf16[128,8,4,128]{3,2,1,0:T(4,128)(2,1)}), bf16[128,8,4,128]{3,2,1,0:T(4,128)(2,1)}, u32[]{:S(2)}, u32[]{:S(2)}) %all-to-all-start.11) | async-done | bytes 1048608 | tf_op jit(solution)/shard_map/all_to_all | solution.py:103
  389.1 3.7 all-to-all-start.12
  396.9 26.5 %all-to-all-done.12 = bf16[128,8,4,128]{3,2,1,0:T(4,128)(2,1)S(1)} async-done(((bf16[128,8,4,128]{3,2,1,0:T(4,128)(2,1)}), bf16[128,8,4,128]{3,2,1,0:T(4,128)(2,1)S(1)}, u32[]{:S(2)}, u32[]{:S(2)}) %all-to-all-start.12) | async-done | bytes 1048608 | tf_op jit(solution)/shard_map/all_to_all | solution.py:104
  423.4 3.7 all-to-all-start.13
  437.6 21.1 %all-to-all-done.13 = bf16[128,8,4,128]{3,2,1,0:T(4,128)(2,1)S(1)} async-done(((bf16[128,8,4,128]{3,2,1,0:T(4,128)(2,1)}), bf16[128,8,4,128]{3,2,1,0:T(4,128)(2,1)S(1)}, u32[]{:S(2)}, u32[]{:S(2)}) %all-to-all-start.13) | async-done | bytes 1048608 | tf_op jit(solution)/shard_map/all_to_all | solution.py:105
  (55 shorter events, 52.9 us)
Async XLA Ops:
  0.6 31.7 %copy-start.4 = (bf16[8,8,64,128]{3,2,1,0:T(8,128)(2,1)S(1)}, bf16[8,8,64,128]{3,2,1,0:T(8,128)(2,1)}, u32[]{:S(2)}) copy-start(bf16[8,8,64,128]{3,2,1,0:T(8,128)(2,1)} %param.10) | copy-start | bytes 3145732
  0.6 62.0 %copy-start.5 = (bf16[8,8,64,128]{3,2,1,0:T(8,128)(2,1)S(1)}, bf16[8,8,64,128]{3,2,1,0:T(8,128)(2,1)}, u32[]{:S(2)}) copy-start(bf16[8,8,64,128]{3,2,1,0:T(8,128)(2,1)} %param.8) | copy-start | bytes 3145732
  92.9 29.6 %all-to-all-start.1 = ((bf16[16,4,64,128]{3,2,1,0:T(8,128)(2,1)}), bf16[16,4,64,128]{3,2,1,0:T(8,128)(2,1)S(1)}, u32[]{:S(2)}, u32[]{:S(2)}) async-start(bf16[16,4,64,128]{3,2,1,0:T(8,128)(2,1)} %bitcast.143), calls=%async_computation.1 | async-start | bytes 2097152 | tf_op jit(solution)/shard_map/all_to_all | solution.py:84
  122.5 39.3 %all-to-all-start.10 = ((bf16[8,8,64,128]{3,1,0,2:T(8,128)(2,1)}), bf16[8,8,64,128]{3,1,0,2:T(8,128)(2,1)}, u32[]{:S(2)}, u32[]{:S(2)}) async-start(bf16[8,8,64,128]{3,1,0,2:T(8,128)(2,1)} %copy.99), calls=%async_computation.10 | async-start | bytes 2097152 | tf_op jit(solution)/shard_map/all_to_all | solution.py:93
  161.8 36.0 %all-to-all-start.9 = ((bf16[8,8,64,128]{3,1,0,2:T(8,128)(2,1)}), bf16[8,8,64,128]{3,1,0,2:T(8,128)(2,1)}, u32[]{:S(2)}, u32[]{:S(2)}) async-start(bf16[8,8,64,128]{3,1,0,2:T(8,128)(2,1)} %copy.97), calls=%async_computation.9 | async-start | bytes 2097152 | tf_op jit(solution)/shard_map/all_to_all | solution.py:94
  166.1 3.0 copy-start.6
  166.1 4.7 %copy-start.3 = (bf16[16,4,64,128]{3,2,1,0:T(8,128)(2,1)S(1)}, bf16[16,4,64,128]{3,2,1,0:T(8,128)(2,1)}, u32[]{:S(2)}) copy-start(bf16[16,4,64,128]{3,2,1,0:T(8,128)(2,1)} %all_to_all.233) | copy-start | bytes 3145732
  197.7 32.4 %all-to-all-start.8 = ((bf16[8,8,64,128]{3,1,0,2:T(8,128)(2,1)}), bf16[8,8,64,128]{3,1,0,2:T(8,128)(2,1)S(1)}, u32[]{:S(2)}, u32[]{:S(2)}) async-start(bf16[8,8,64,128]{3,1,0,2:T(8,128)(2,1)} %copy.95), calls=%async_computation.8 | async-start | bytes 2097152 | tf_op jit(solution)/shard_map/all_to_all | solution.py:92
  208.2 3.2 copy-start
  208.3 3.6 copy-start.7
  208.4 3.8 copy-start.10
  215.5 18.6 %copy-start.8 = (bf16[1,4,16,64,128]{4,3,2,1,0:T(8,128)(2,1)S(1)}, bf16[1,4,16,64,128]{4,3,2,1,0:T(8,128)(2,1)}, u32[]{:S(2)}) copy-start(bf16[1,4,16,64,128]{4,3,2,1,0:T(8,128)(2,1)} %copy-done.7) | copy-start | bytes 3145732
  230.2 26.3 %all-to-all-start.7 = ((bf16[8,8,64,128]{3,1,0,2:T(8,128)(2,1)}), bf16[8,8,64,128]{3,1,0,2:T(8,128)(2,1)S(1)}, u32[]{:S(2)}, u32[]{:S(2)}) async-start(bf16[8,8,64,128]{3,1,0,2:T(8,128)(2,1)} %copy.93), calls=%async_computation.7 | async-start | bytes 2097152 | tf_op jit(solution)/shard_map/all_to_all | solution.py:91
  234.0 10.0 %copy-start.9 = (bf16[1,4,16,64,128]{4,3,2,1,0:T(8,128)(2,1)S(1)}, bf16[1,4,16,64,128]{4,3,2,1,0:T(8,128)(2,1)}, u32[]{:S(2)}) copy-start(bf16[1,4,16,64,128]{4,3,2,1,0:T(8,128)(2,1)} %copy.81) | copy-start | bytes 3145732
  256.5 34.6 %all-to-all-start.4 = ((bf16[1,4,1024,128]{3,1,0,2:T(4,128)(2,1)}), bf16[1,4,1024,128]{3,1,0,2:T(4,128)(2,1)S(1)}, u32[]{:S(2)}, u32[]{:S(2)}) async-start(bf16[1,4,1024,128]{3,1,0,2:T(4,128)(2,1)} %copy.87), calls=%async_computation.4 | async-start | bytes 2097152 | tf_op jit(solution)/shard_map/all_to_all | solution.py:98
  291.1 15.3 %copy-start.1 = (bf16[1,4,1024,128]{3,1,0,2:T(4,128)(2,1)}, bf16[1,4,1024,128]{3,1,0,2:T(4,128)(2,1)S(1)}, u32[]{:S(2)}) copy-start(bf16[1,4,1024,128]{3,1,0,2:T(4,128)(2,1)S(1)} %all-to-all-done.4) | copy-start | bytes 3145732
  291.1 31.5 %all-to-all-start.5 = ((bf16[1,4,1024,128]{3,1,0,2:T(4,128)(2,1)}), bf16[1,4,1024,128]{3,1,0,2:T(4,128)(2,1)}, u32[]{:S(2)}, u32[]{:S(2)}) async-start(bf16[1,4,1024,128]{3,1,0,2:T(4,128)(2,1)} %copy.89), calls=%async_computation.5 | async-start | bytes 2097152 | tf_op jit(solution)/shard_map/all_to_all | solution.py:99
  322.7 31.5 %all-to-all-start.6 = ((bf16[1,4,1024,128]{3,1,0,2:T(4,128)(2,1)}), bf16[1,4,1024,128]{3,1,0,2:T(4,128)(2,1)}, u32[]{:S(2)}, u32[]{:S(2)}) async-start(bf16[1,4,1024,128]{3,1,0,2:T(4,128)(2,1)} %copy.91), calls=%async_computation.6 | async-start | bytes 2097152 | tf_op jit(solution)/shard_map/all_to_all | solution.py:100
  334.5 3.3 copy-start.11
  354.2 34.9 %all-to-all-start.11 = ((bf16[128,8,4,128]{3,2,1,0:T(4,128)(2,1)}), bf16[128,8,4,128]{3,2,1,0:T(4,128)(2,1)}, u32[]{:S(2)}, u32[]{:S(2)}) async-start(bf16[128,8,4,128]{3,2,1,0:T(4,128)(2,1)} %copy.105), calls=%async_computation.11 | async-start | bytes 2097152 | tf_op jit(solution)/shard_map/all_to_all | solution.py:103
  389.1 34.3 %all-to-all-start.12 = ((bf16[128,8,4,128]{3,2,1,0:T(4,128)(2,1)}), bf16[128,8,4,128]{3,2,1,0:T(4,128)(2,1)S(1)}, u32[]{:S(2)}, u32[]{:S(2)}) async-start(bf16[128,8,4,128]{3,2,1,0:T(4,128)(2,1)} %copy.109), calls=%async_computation.12 | async-start | bytes 2097152 | tf_op jit(solution)/shard_map/all_to_all | solution.py:104
  395.1 32.0 %copy-start.2 = (bf16[1,4,1024,128]{3,1,0,2:T(4,128)(2,1)S(1)}, bf16[1,4,1024,128]{3,1,0,2:T(4,128)(2,1)}, u32[]{:S(2)}) copy-start(bf16[1,4,1024,128]{3,1,0,2:T(4,128)(2,1)} %copy-done.1) | copy-start | bytes 3145732
  423.4 35.2 %all-to-all-start.13 = ((bf16[128,8,4,128]{3,2,1,0:T(4,128)(2,1)}), bf16[128,8,4,128]{3,2,1,0:T(4,128)(2,1)S(1)}, u32[]{:S(2)}, u32[]{:S(2)}) async-start(bf16[128,8,4,128]{3,2,1,0:T(4,128)(2,1)} %copy.112), calls=%async_computation.13 | async-start | bytes 2097152 | tf_op jit(solution)/shard_map/all_to_all | solution.py:105
where the time goes:
time: 462 us; the launch traced here: 460 us
  waiting for transfers between devices  196 us (42%)
  blocking collectives  92.3 us (20%)
  starting transfers between devices  70.1 us (15%)
  matrix products  54.2 us (12%)
  local copies, waits for them, and re-layouts  40.1 us (9%)
  other arithmetic  6.86 us (1%)
    dot_general x10, matrix products, contract(): jnp.einsum(first_form + ',' + second_form + '->' + result_form, left, rig...  41.8 us
    all_to_all x1, blocking collectives, per_device(): lax.all_to_all(regroup(d_out_space), 'patch', split_axis=0, concat_axis=2...  31.7 us
    all_to_all x1, blocking collectives, per_device(): lax.all_to_all(regroup(q_space), 'patch', split_axis=0, concat_axis=2, ti...  30.3 us
    all_to_all x1, blocking collectives, per_device(): lax.all_to_all(regroup(v_space), 'patch', split_axis=0, concat_axis=2, ti...  30.2 us
    all_to_all x1, waiting for transfers between devices, per_device(): lax.all_to_all(time_grads[0], 'frame', split_axis=0, concat_axis=2, tiled...  28 us
    all_to_all x1, waiting for transfers between devices, per_device(): lax.all_to_all(v_time, 'frame', split_axis=2, concat_axis=0, tiled=True)  27.8 us
    all_to_all x1, waiting for transfers between devices, per_device(): lax.all_to_all(time_grads[1], 'frame', split_axis=0, concat_axis=2, tiled...  26.5 us
    all_to_all x1, waiting for transfers between devices, per_device(): lax.all_to_all(time_grads[2], 'frame', split_axis=0, concat_axis=2, tiled...  21.1 us
  transfers between devices with their start and end apart: 11, of which 11 were waited for; matrix products, arithmetic and copies ran while one was open for 21% of the time, Pallas kernels for 0%

commit v1 on v0

v1 whole, which is shorter than its diff:
```python
import functools
import math

import jax
import jax.numpy as jnp
from jax import lax
from jax.experimental import pallas as pl
from jax.experimental.pallas import tpu as pltpu
from jax.sharding import PartitionSpec as P

F32 = jnp.float32
BF16 = jnp.bfloat16
LOG2E = 1.4426950408889634
MASKED = -1e30
VMEM_LIMIT = 40 * 1024 * 1024

CORE_BIT = 1
ZHI_BIT = 2
Y_BIT = 4
FRAME_DEVICES = 16
PATCH_DEVICES = 16
CHUNKS = 2


def dot(a, b, dims):
    return lax.dot_general(a, b, (dims, ((), ())), preferred_element_type=F32)


NT = ((1,), (1,))
NN = ((1,), (0,))
TN = ((0,), (0,))


def space_kernel(x_ref, o_ref, dk_acc, dv_acc, *, block, scale):
    peers, _, _, rows, dim = x_ref.shape
    length = peers * rows
    k = x_ref[:, 0, 1].reshape(length, dim)
    v = x_ref[:, 0, 2].reshape(length, dim)
    per = block // rows
    for b in range(length // block):
        q = x_ref[b * per : (b + 1) * per, 0, 0].reshape(block, dim)
        g = x_ref[b * per : (b + 1) * per, 0, 3].reshape(block, dim)
        s = dot(k, q, NT) * (scale * LOG2E)
        top = jnp.max(s, axis=0, keepdims=True)
        e = jnp.exp2(s - top)
        p = e * (1.0 / jnp.sum(e, axis=0, keepdims=True))
        w = p.astype(BF16)
        gv = dot(v, g, NT)
        delta = jnp.sum(p * gv, axis=0, keepdims=True)
        ds = (p * (gv - delta)).astype(BF16)
        dv = dot(w, g, NN)
        dk = dot(ds, q, NN)
        if b == 0:
            dv_acc[...] = dv
            dk_acc[...] = dk
        else:
            dv_acc[...] += dv
            dk_acc[...] += dk
        dq = dot(ds, k, TN) * scale
        o_ref[b * per : (b + 1) * per, 0, 0] = dq.astype(BF16).reshape(per, rows, dim)
    o_ref[:, 0, 1] = (dk_acc[...] * scale).astype(BF16).reshape(peers, rows, dim)
    o_ref[:, 0, 2] = dv_acc[...].astype(BF16).reshape(peers, rows, dim)


def space_grads(x):
    peers, seqs, _, rows, dim = x.shape
    length = peers * rows
    flops = seqs * 5 * 2 * length * length * dim
    return pl.pallas_call(
        functools.partial(space_kernel, block=256, scale=1.0 / math.sqrt(dim)),
        grid=(seqs,),
        in_specs=[pl.BlockSpec((peers, 1, 4, rows, dim), lambda j: (0, j, 0, 0, 0))],
        out_specs=pl.BlockSpec((peers, 1, 3, rows, dim), lambda j: (0, j, 0, 0, 0)),
        out_shape=jax.ShapeDtypeStruct((peers, seqs, 3, rows, dim), BF16),
        scratch_shapes=[pltpu.VMEM((length, dim), F32), pltpu.VMEM((length, dim), F32)],
        cost_estimate=pl.CostEstimate(
            flops=flops, bytes_accessed=x.size * 2 * 2, transcendentals=seqs * length * length
        ),
        compiler_params=pltpu.CompilerParams(vmem_limit_bytes=VMEM_LIMIT),
        name="space_grads",
    )(x)


def frame_rows(side, count, rows, dim_of):
    i = lax.broadcasted_iota(jnp.int32, *dim_of)
    return (2 * (i // rows) + side) * rows + i % rows


def time_scores(side, qg_ref, rb_ref, ra_ref, kv_ref, p, scale):
    slots, _, _, rows, dim = qg_ref.shape
    half = slots * rows
    k = kv_ref[:, 0, p].reshape(half, dim)
    v = kv_ref[:, 1, p].reshape(half, dim)
    q = jnp.concatenate(
        [qg_ref[:, 0, p].reshape(half, dim), rb_ref[0, p], ra_ref[:, 0, p].reshape(half - rows, dim)]
    )
    g = jnp.concatenate(
        [qg_ref[:, 1, p].reshape(half, dim), rb_ref[1, p], ra_ref[:, 1, p].reshape(half - rows, dim)]
    )
    s = dot(k, q, NT) * (scale * LOG2E)
    gv = dot(v, g, NT)
    return q, g, k, s, gv


def time_allowed(side, slots, rows):
    half = slots * rows
    shape = (half, 2 * half)
    ki = lax.broadcasted_iota(jnp.int32, shape, 0)
    qi = lax.broadcasted_iota(jnp.int32, shape, 1)
    remote = qi // half
    qj = qi % half
    key_frame = (2 * (ki // rows) + side) * rows + ki % rows
    query_side = jnp.where(remote == 0, side, 1 - side)
    query_frame = (2 * (qj // rows) + query_side) * rows + qj % rows
    return key_frame <= query_frame


def time_stats_kernel(side_ref, qg_ref, rb_ref, ra_ref, kv_ref, st_ref, *, scale):
    slots, _, count, rows, _ = qg_ref.shape
    side = side_ref[0]
    allowed = time_allowed(side, slots, rows)
    for p in range(count):
        _, _, _, s, gv = time_scores(side, qg_ref, rb_ref, ra_ref, kv_ref, p, scale)
        s = jnp.where(allowed, s, MASKED)
        top = jnp.max(s, axis=0, keepdims=True)
        e = jnp.exp2(s - top)
        total = jnp.sum(e, axis=0, keepdims=True)
        st_ref[0, pl.ds(p, 1)] = top + jnp.log2(total)
        st_ref[1, pl.ds(p, 1)] = jnp.sum(e * gv, axis=0, keepdims=True) / total


def time_grads_kernel(
    side_ref, qg_ref, rb_ref, ra_ref, kv_ref, mine_ref, other_ref, dq_ref, db_ref, da_ref, dkv_ref, *, scale
):
    slots, _, count, rows, dim = qg_ref.shape
    half = slots * rows
    side = side_ref[0]
    allowed = time_allowed(side, slots, rows)
    lse_a, lse_b = mine_ref[0], other_ref[0]
    top = jnp.maximum(lse_a, lse_b)
    lse = top + jnp.log2(jnp.exp2(lse_a - top) + jnp.exp2(lse_b - top))
    delta = jnp.exp2(lse_a - lse) * mine_ref[1] + jnp.exp2(lse_b - lse) * other_ref[1]
    for p in range(count):
        q, g, k, s, gv = time_scores(side, qg_ref, rb_ref, ra_ref, kv_ref, p, scale)
        w = jnp.where(allowed, jnp.exp2(jnp.where(allowed, s - lse[p : p + 1], 0.0)), 0.0)
        ds = (w * (gv - delta[p : p + 1])).astype(BF16)
        w = w.astype(BF16)
        dkv_ref[:, 1, p] = dot(w, g, NN).astype(BF16).reshape(slots, rows, dim)
        dkv_ref[:, 0, p] = (dot(ds, q, NN) * scale).astype(BF16).reshape(slots, rows, dim)
        dq = dot(ds, k, TN) * scale
        dq_ref[:, p] = dq[:half].reshape(slots, rows, dim)
        db_ref[p] = dq[half : half + rows].astype(BF16)
        da_ref[:, p] = dq[half + rows :].astype(BF16).reshape(slots - 1, rows, dim)


def time_specs(group, slots, rows, dim):
    return [
        pl.BlockSpec(memory_space=pltpu.SMEM),
        pl.BlockSpec((slots, 2, group, rows, dim), lambda i: (0, 0, i, 0, 0)),
        pl.BlockSpec((2, group, rows, dim), lambda i: (0, i, 0, 0)),
        pl.BlockSpec((slots - 1, 2, group, rows, dim), lambda i: (0, 0, i, 0, 0)),
        pl.BlockSpec((slots, 2, group, rows, dim), lambda i: (0, 0, i, 0, 0)),
    ]


def time_stats(side, qg, rb, ra, kv, group=8):
    slots, _, count, rows, dim = qg.shape
    half = slots * rows
    return pl.pallas_call(
        functools.partial(time_stats_kernel, scale=1.0 / math.sqrt(dim)),
        grid=(count // group,),
        in_specs=time_specs(group, slots, rows, dim),
        out_specs=pl.BlockSpec((2, group, 2 * half), lambda i: (0, i, 0)),
        out_shape=jax.ShapeDtypeStruct((2, count, 2 * half), F32),
        cost_estimate=pl.CostEstimate(
            flops=count * 2 * 2 * half * 2 * half * dim,
            bytes_accessed=qg.size * 2 * 3,
            transcendentals=count * half * 2 * half,
        ),
        compiler_params=pltpu.CompilerParams(vmem_limit_bytes=VMEM_LIMIT),
        name="time_stats",
    )(side, qg, rb, ra, kv)


def time_grads(side, qg, rb, ra, kv, mine, other, group=8):
    slots, _, count, rows, dim = qg.shape
    half = slots * rows
    stat = pl.BlockSpec((2, group, 2 * half), lambda i: (0, i, 0))
    return pl.pallas_call(
        functools.partial(time_grads_kernel, scale=1.0 / math.sqrt(dim)),
        grid=(count // group,),
        in_specs=time_specs(group, slots, rows, dim) + [stat, stat],
        out_specs=[
            pl.BlockSpec((slots, group, rows, dim), lambda i: (0, i, 0, 0)),
            pl.BlockSpec((group, rows, dim), lambda i: (i, 0, 0)),
            pl.BlockSpec((slots - 1, group, rows, dim), lambda i: (0, i, 0, 0)),
            pl.BlockSpec((slots, 2, group, rows, dim), lambda i: (0, 0, i, 0, 0)),
        ],
        out_shape=[
            jax.ShapeDtypeStruct((slots, count, rows, dim), F32),
            jax.ShapeDtypeStruct((count, rows, dim), BF16),
            jax.ShapeDtypeStruct((slots - 1, count, rows, dim), BF16),
            jax.ShapeDtypeStruct((slots, 2, count, rows, dim), BF16),
        ],
        cost_estimate=pl.CostEstimate(
            flops=count * 5 * 2 * half * 2 * half * dim,
            bytes_accessed=qg.size * 2 * 5,
            transcendentals=count * half * 2 * half,
        ),
        compiler_params=pltpu.CompilerParams(vmem_limit_bytes=VMEM_LIMIT),
        name="time_grads",
    )(side, qg, rb, ra, kv, mine, other)


def swap(x, bits):
    return lax.ppermute(x, "frame", [(i, i ^ bits) for i in range(FRAME_DEVICES)])


def from_side(x, side):
    pairs = [(i, i ^ ZHI_BIT) for i in range(FRAME_DEVICES) if (i // ZHI_BIT) % 2 == side]
    return lax.ppermute(x, "frame", pairs)


def pick(x, i):
    return lax.dynamic_index_in_dim(x, i, 0, keepdims=False)


def y_exchange(u, y):
    got = [swap(pick(u, y ^ j), j * Y_BIT) for j in range(1, 4)]
    for j in range(1, 4):
        u = lax.dynamic_update_index_in_dim(u, got[j - 1], y ^ j, 0)
    return u


def gather_frames(arrays, y, core):
    t = jnp.stack([jnp.transpose(a, (1, 2, 0, 3)) for a in arrays], 1)
    t = t.reshape((2, t.shape[0] // 2) + t.shape[1:])
    keep, got = pick(t, core), swap(pick(t, 1 - core), CORE_BIT)
    first = core == 0
    u = jnp.concatenate([jnp.where(first, keep, got), jnp.where(first, got, keep)], axis=-2)
    return y_exchange(u, y)


def scatter_frames(u, y, core):
    v = y_exchange(u, y)
    half = v.shape[-2] // 2
    low, high = v[..., :half, :], v[..., half:, :]
    first = core == 0
    keep = jnp.where(first, low, high)
    got = swap(jnp.where(first, high, low), CORE_BIT)
    t = jnp.concatenate([jnp.where(first, keep, got), jnp.where(first, got, keep)], axis=0)
    return [jnp.transpose(t[:, i], (2, 0, 1, 3)) for i in range(t.shape[1])]


def exchange_patches(x):
    return lax.all_to_all(x, "patch", split_axis=0, concat_axis=0, tiled=True)


def per_device(q_space, k_space, v_space, d_out_space, q_time, k_time, v_time, d_out_time):
    frames, heads, rows, dim = q_space.shape
    seqs = frames * heads
    f = lax.axis_index("frame")
    y, side, core = f // Y_BIT, (f // ZHI_BIT) % 2, f % 2
    side_arr = jnp.reshape(side, (1,)).astype(jnp.int32)

    space = [a.reshape(seqs, rows, dim) for a in (q_space, k_space, v_space, d_out_space)]
    width = seqs // CHUNKS
    arrived = []
    for c in range(CHUNKS):
        x = jnp.stack([a[c * width : (c + 1) * width] for a in space], 1)
        arrived.append(exchange_patches(x.reshape(PATCH_DEVICES, width // PATCH_DEVICES, 4, rows, dim)))

    qg = gather_frames((q_time, d_out_time), y, core)
    ra = swap(qg[1:], ZHI_BIT)
    rb = from_side(qg[0], 1)
    kv = gather_frames((k_time, v_time), y, core)

    back = [exchange_patches(space_grads(x)).reshape(width, 3, rows, dim) for x in arrived]

    mine = time_stats(side_arr, qg, rb, ra, kv)
    other = swap(mine, ZHI_BIT)
    other = jnp.roll(other, other.shape[-1] // 2, axis=-1)
    dq, db, da, dkv = time_grads(side_arr, qg, rb, ra, kv, mine, other)
    da = swap(da, ZHI_BIT)
    db = from_side(db, 0)
    dq = (dq + jnp.concatenate([db[None], da]).astype(F32)).astype(BF16)
    dk_time, dv_time = scatter_frames(dkv, y, core)
    (dq_time,) = scatter_frames(dq[:, None], y, core)

    shape = (frames, heads, rows, dim)
    out = [jnp.concatenate([b[:, i] for b in back]).reshape(shape) for i in range(3)]
    return (out[0], out[1], out[2], dq_time, dk_time, dv_time)


def solution(mesh):
    spec = P("frame", None, "patch", None)
    return jax.shard_map(
        per_device, mesh=mesh, in_specs=(spec,) * 8, out_specs=(spec,) * 6, check_vma=False
    )
```

time: 462 us -> 346 us (0.75)
  the two profiles are of different devices: /device:TPU:68 before, /device:TPU:1 now
where the time goes in v1:
time: 346 us; the launch traced here: 345 us
  waiting for transfers between devices  171 us (49%)
  starting transfers between devices  74 us (21%)
  Pallas kernels  45.8 us (13%)
  local copies, waits for them, and re-layouts  35.2 us (10%)
  other arithmetic  17.6 us (5%)
    all_to_all x4, waiting for transfers between devices, exchange_patches(): return lax.all_to_all(x, 'patch', split_axis=0, concat_axis=0, tiled=True)  113 us
    ppermute x19, waiting for transfers between devices, swap(): lax.ppermute(x, 'frame', [(i, i ^ bits) for i in range(FRAME_DEVICES)])  47.5 us
    ppermute x19, starting transfers between devices, swap(): lax.ppermute(x, 'frame', [(i, i ^ bits) for i in range(FRAME_DEVICES)])  43.2 us
    all_to_all x4, starting transfers between devices, exchange_patches(): return lax.all_to_all(x, 'patch', split_axis=0, concat_axis=0, tiled=True)  23.9 us
    pallas_call x2, Pallas kernels, space_grads(): pl.pallas_call(functools.partial(space_kernel, block=256, scale=1.0 / mat...  21.9 us
    pallas_call x1, Pallas kernels, time_grads(): pl.pallas_call(functools.partial(time_grads_kernel, scale=1.0 / math.sqrt...  16.9 us
    unnamed x39, local copies, waits for them, and re-layouts  11.3 us
    ppermute x2, waiting for transfers between devices, from_side(): return lax.ppermute(x, 'frame', pairs)  10.7 us
  transfers between devices with their start and end apart: 25, of which 12 were waited for; matrix products, arithmetic and copies ran while one was open for 12% of the time, Pallas kernels for 13%

profile of v1, /device:TPU:1, one launch (start us, length us, event | category | flops | bytes accessed | tf_op | source)
XLA Modules:
  0.0 344.8 jit_solution(15311605359165634663)
XLA Ops:
  5.9 9.0 %all-to-all-start = ((bf16[16,2,4,64,128]{4,3,2,1,0:T(8,128)(2,1)}), bf16[16,2,4,64,128]{4,3,2,1,0:T(8,128)(2,1)S(1)}, u32[]{:S(2)}, u32[]{:S(2)}) async-start(bf16[16,2,4,64,128]{4,3,2,1,0:T(8,128)(2,1)} %pad_maximum_fusion.2), calls=%async_computation | async-start | bytes 4194304 | tf_op jit(solution)/shard_map/all_to_all | solution.py:256
  15.0 2.0 copy_dynamic-update-slice_fusion.3
  22.8 41.9 %all-to-all-done.x_ref = bf16[16,2,4,64,128]{4,3,2,1,0:T(8,128)(2,1)S(1)} async-done(((bf16[16,2,4,64,128]{4,3,2,1,0:T(8,128)(2,1)}), bf16[16,2,4,64,128]{4,3,2,1,0:T(8,128)(2,1)S(1)}, u32[]{:S(2)}, u32[]{:S(2)}) %all-to-all-start) | async-done | bytes 2097184 | tf_op jit(solution)/shard_map/all_to_all | solution.py:256
  64.8 4.4 %all-to-all-start.2 = ((bf16[16,2,4,64,128]{4,3,2,1,0:T(8,128)(2,1)}), bf16[16,2,4,64,128]{4,3,2,1,0:T(8,128)(2,1)}, u32[]{:S(2)}, u32[]{:S(2)}) async-start(bf16[16,2,4,64,128]{4,3,2,1,0:T(8,128)(2,1)} %pad_maximum_fusion.3), calls=%async_computation.2 | async-start | bytes 4194304 | tf_op jit(solution)/shard_map/all_to_all | solution.py:256
  77.2 2.6 collective-permute-start.2
  81.6 7.9 %collective-permute-done.1 = bf16[2,64,16,128]{3,2,1,0:T(8,128)(2,1)S(1)} collective-permute-done((bf16[2,64,16,128]{3,2,1,0:T(8,128)(2,1)S(1)}, bf16[2,64,16,128]{3,2,1,0:T(8,128)(2,1)S(1)}, u32[]{:S(2)}, u32[]{:S(2)}) %collective-permute-start.1) | collective-permute-done | bytes 524320 | tf_op jit(solution)/shard_map/ppermute | solution.py:216
  89.5 13.6 %collective-permute-done.2 = bf16[2,64,16,128]{3,2,1,0:T(8,128)(2,1)S(1)} collective-permute-done((bf16[2,64,16,128]{3,2,1,0:T(8,128)(2,1)S(1)}, bf16[2,64,16,128]{3,2,1,0:T(8,128)(2,1)S(1)}, u32[]{:S(2)}, u32[]{:S(2)}) %collective-permute-start.2) | collective-permute-done | bytes 524320 | tf_op jit(solution)/shard_map/ppermute | solution.py:216
  103.2 1.9 collective-permute-done.3
  106.6 4.2 %collective-permute-start.5 = (bf16[3,2,64,16,128]{4,3,2,1,0:T(8,128)(2,1)}, bf16[3,2,64,16,128]{4,3,2,1,0:T(8,128)(2,1)}, u32[]{:S(2)}, u32[]{:S(2)}) collective-permute-start(bf16[3,2,64,16,128]{4,3,2,1,0:T(8,128)(2,1)} %slice.113), channel_id=1, source_target_pairs={{0,32},{16,48},{32,0},{48,16},{64,96},{80,112},{96,64},{112,80},{1... | collective-permute-start | bytes 4718600 | tf_op jit(solution)/shard_map/ppermute | solution.py:216
  113.4 2.5 collective-permute-start.9
  115.9 3.0 pad_maximum_fusion.1
  120.4 3.6 %collective-permute-done.7 = bf16[2,64,16,128]{3,2,1,0:T(8,128)(2,1)} collective-permute-done((bf16[2,64,16,128]{3,2,1,0:T(8,128)(2,1)}, bf16[2,64,16,128]{3,2,1,0:T(8,128)(2,1)}, u32[]{:S(2)}, u32[]{:S(2)}) %collective-permute-start.7) | collective-permute-done | bytes 524320 | tf_op jit(solution)/shard_map/ppermute | solution.py:216
  125.9 10.0 %space_grads.2 = bf16[16,2,3,64,128]{4,3,2,1,0:T(8,128)(2,1)S(1)} custom-call(bf16[16,2,4,64,128]{4,3,2,1,0:T(8,128)(2,1)S(1)} %copy-done.1), custom_call_target="tpu_custom_call" | custom-call | flops 2684354560 | bytes 4194304 | tf_op jit(solution)/shard_map/space_grads/pallas_call | solution.py:69
  137.0 51.3 %all-to-all-done.2.x_ref = bf16[16,2,4,64,128]{4,3,2,1,0:T(8,128)(2,1)} async-done(((bf16[16,2,4,64,128]{4,3,2,1,0:T(8,128)(2,1)}), bf16[16,2,4,64,128]{4,3,2,1,0:T(8,128)(2,1)}, u32[]{:S(2)}, u32[]{:S(2)}) %all-to-all-start.2) | async-done | bytes 2097184 | tf_op jit(solution)/shard_map/all_to_all | solution.py:256
  188.3 4.4 %all-to-all-start.1 = ((bf16[16,2,3,64,128]{4,3,2,1,0:T(8,128)(2,1)}), bf16[16,2,3,64,128]{4,3,2,1,0:T(8,128)(2,1)}, u32[]{:S(2)}, u32[]{:S(2)}) async-start(bf16[16,2,3,64,128]{4,3,2,1,0:T(8,128)(2,1)} %copy-done.2), calls=%async_computation.1 | async-start | bytes 3145728 | tf_op jit(solution)/shard_map/all_to_all | solution.py:256
  192.7 1.9 bitcast_dynamic-update-slice_fusion.4
  194.6 1.9 bitcast_dynamic-update-slice_fusion.3.kv_ref
  196.6 7.0 %time_stats.1.mine_ref = f32[2,64,128]{2,1,0:T(8,128)S(1)} custom-call(s32[1]{0:T(128)} %bitcast.19.side_ref, bf16[4,2,64,16,128]{4,3,2,1,0:T(8,128)(2,1)S(1)} %bitcast_dynamic-update-slice_fusion.6.qg_ref, bf16[2,64,16,128]{3,2,1,0:T(8,128)(2,1)S(1)} %collective-permute-done.4.rb_ref, bf16[3,2,64,16,128]{4,3,2,1,0:T(8,128)(2,1)} %collective-permute-done.5.ra_ref, ...), custom_call_target="tpu_custom_call" | custom-call | flops 268435456 | bytes 6291456 | tf_op jit(solution)/shard_map/time_stats/pallas_call | solution.py:169
  203.6 13.6 %collective-permute-start.10 = (f32[2,64,128]{2,1,0:T(8,128)S(1)}, f32[2,64,128]{2,1,0:T(8,128)S(1)}, u32[]{:S(2)}, u32[]{:S(2)}) collective-permute-start(f32[2,64,128]{2,1,0:T(8,128)S(1)} %time_stats.1.mine_ref), channel_id=1, source_target_pairs={{0,32},{16,48},{32,0},{48,16},{64,96},{80,112},{96,64},{112,80},{1... | collective-permute-start | bytes 196616 | tf_op jit(solution)/shard_map/ppermute | solution.py:216
  217.2 16.5 %collective-permute-done.10 = f32[2,64,128]{2,1,0:T(8,128)S(1)} collective-permute-done((f32[2,64,128]{2,1,0:T(8,128)S(1)}, f32[2,64,128]{2,1,0:T(8,128)S(1)}, u32[]{:S(2)}, u32[]{:S(2)}) %collective-permute-start.10) | collective-permute-done | bytes 65568 | tf_op jit(solution)/shard_map/ppermute | solution.py:216
  233.8 16.9 %time_grads.1 = (f32[4,64,16,128]{3,2,1,0:T(8,128)S(1)}, bf16[64,16,128]{2,1,0:T(8,128)(2,1)S(1)}, bf16[3,64,16,128]{3,2,1,0:T(8,128)(2,1)S(1)}, bf16[4,2,64,16,128]{4,3,2,1,0:T(8,128)(2,1)}) custom-call(s32[1]{0:T(128)} %bitcast.19.side_ref, bf16[4,2,64,16,128]{4,3,2,1,0:T(8,128)(2,1)S(1)} %bitcast_dynamic-update-slice_fusion.6.qg_ref, ...), custom_call_target="tpu_custom_call" | custom-call | flops 671088640 | bytes 10485760 | tf_op jit(solution)/shard_map/time_grads/pallas_call | solution.py:189
  255.1 5.5 %collective-permute-start.11 = (bf16[64,16,128]{2,1,0:T(8,128)(2,1)S(1)}, bf16[64,16,128]{2,1,0:T(8,128)(2,1)S(1)}, u32[]{:S(2)}, u32[]{:S(2)}) collective-permute-start(bf16[64,16,128]{2,1,0:T(8,128)(2,1)S(1)} %get-tuple-element.11), channel_id=1, source_target_pairs={{0,32},{16,48},{64,96},{80,112},{128,160},{144,176},{192,224},{208... | collective-permute-start | bytes 786440 | tf_op jit(solution)/shard_map/ppermute | solution.py:221
  260.6 2.2 collective-permute-done.17
  262.8 2.3 dynamic-slice_bitcast_fusion.2
  265.1 3.1 collective-permute-start.18
  269.0 11.9 %space_grads.3 = bf16[16,2,3,64,128]{4,3,2,1,0:T(8,128)(2,1)} custom-call(bf16[16,2,4,64,128]{4,3,2,1,0:T(8,128)(2,1)} %all-to-all-done.2.x_ref), custom_call_target="tpu_custom_call" | custom-call | flops 2684354560 | bytes 4194304 | tf_op jit(solution)/shard_map/space_grads/pallas_call | solution.py:69
  280.9 10.7 %collective-permute-done.11 = bf16[64,16,128]{2,1,0:T(8,128)(2,1)S(1)} collective-permute-done((bf16[64,16,128]{2,1,0:T(8,128)(2,1)S(1)}, bf16[64,16,128]{2,1,0:T(8,128)(2,1)S(1)}, u32[]{:S(2)}, u32[]{:S(2)}) %collective-permute-start.11) | collective-permute-done | bytes 262176 | tf_op jit(solution)/shard_map/ppermute | solution.py:221
  292.8 3.0 collective-permute-start.14
  297.9 6.0 %all-to-all-start.3 = ((bf16[16,2,3,64,128]{4,3,2,1,0:T(8,128)(2,1)}), bf16[16,2,3,64,128]{4,3,2,1,0:T(8,128)(2,1)S(1)}, u32[]{:S(2)}, u32[]{:S(2)}) async-start(bf16[16,2,3,64,128]{4,3,2,1,0:T(8,128)(2,1)} %space_grads.3), calls=%async_computation.3 | async-start | bytes 3145728 | tf_op jit(solution)/shard_map/all_to_all | solution.py:256
  305.6 3.2 collective-permute-start.20
  320.0 2.3 slice_bitcast_fusion.2
  322.3 19.8 %all-to-all-done.3 = bf16[16,2,3,64,128]{4,3,2,1,0:T(8,128)(2,1)S(1)} async-done(((bf16[16,2,3,64,128]{4,3,2,1,0:T(8,128)(2,1)}), bf16[16,2,3,64,128]{4,3,2,1,0:T(8,128)(2,1)S(1)}, u32[]{:S(2)}, u32[]{:S(2)}) %all-to-all-start.3) | async-done | bytes 1572896 | tf_op jit(solution)/shard_map/all_to_all | solution.py:256
  (106 shorter events, 53.7 us)
Async XLA Ops:
  5.9 58.8 %all-to-all-start = ((bf16[16,2,4,64,128]{4,3,2,1,0:T(8,128)(2,1)}), bf16[16,2,4,64,128]{4,3,2,1,0:T(8,128)(2,1)S(1)}, u32[]{:S(2)}, u32[]{:S(2)}) async-start(bf16[16,2,4,64,128]{4,3,2,1,0:T(8,128)(2,1)} %pad_maximum_fusion.2), calls=%async_computation | async-start | bytes 4194304 | tf_op jit(solution)/shard_map/all_to_all | solution.py:256
  17.0 4.2 %copy-start.8 = (bf16[4,8,64,128]{3,2,1,0:T(8,128)(2,1)S(1)}, bf16[4,8,64,128]{3,2,1,0:T(8,128)(2,1)}, u32[]{:S(2)}) copy-start(bf16[4,8,64,128]{3,2,1,0:T(8,128)(2,1)} %get-tuple-element.53) | copy-start | bytes 1572868
  17.0 4.2 %copy-start.9 = (bf16[4,8,64,128]{3,2,1,0:T(8,128)(2,1)S(1)}, bf16[4,8,64,128]{3,2,1,0:T(8,128)(2,1)}, u32[]{:S(2)}) copy-start(bf16[4,8,64,128]{3,2,1,0:T(8,128)(2,1)} %get-tuple-element.55) | copy-start | bytes 1572868
  20.3 53.9 %collective-permute-start = (bf16[4,2,64,8,128]{4,3,2,1,0:T(8,128)(2,1)}, bf16[4,2,64,8,128]{4,3,2,1,0:T(8,128)(2,1)}, u32[]{:S(2)}, u32[]{:S(2)}) collective-permute-start(bf16[4,2,64,8,128]{4,3,2,1,0:T(8,128)(2,1)} %dynamic-slice_bitcast_fusion.1), channel_id=1, source_target_pairs={{0,16},{16,0},{32,48},{48,32},{64,80},{80,64},{96,112},{112,96},{1... | collective-permute-start | bytes 3145736 | tf_op jit(solution)/shard_map/ppermute | solution.py:216
  22.8 46.4 %copy-start.15 = (bf16[8,8,64,128]{3,2,1,0:T(8,128)(2,1)S(1)}, bf16[8,8,64,128]{3,2,1,0:T(8,128)(2,1)}, u32[]{:S(2)}) copy-start(bf16[8,8,64,128]{3,2,1,0:T(8,128)(2,1)} %param.13) | copy-start | bytes 3145732
  64.8 4.5 %copy-start = (bf16[16,2,4,64,128]{4,3,2,1,0:T(8,128)(2,1)}, bf16[16,2,4,64,128]{4,3,2,1,0:T(8,128)(2,1)S(1)}, u32[]{:S(2)}) copy-start(bf16[16,2,4,64,128]{4,3,2,1,0:T(8,128)(2,1)S(1)} %all-to-all-done.x_ref) | copy-start | bytes 6291460
  64.8 123.6 %all-to-all-start.2 = ((bf16[16,2,4,64,128]{4,3,2,1,0:T(8,128)(2,1)}), bf16[16,2,4,64,128]{4,3,2,1,0:T(8,128)(2,1)}, u32[]{:S(2)}, u32[]{:S(2)}) async-start(bf16[16,2,4,64,128]{4,3,2,1,0:T(8,128)(2,1)} %pad_maximum_fusion.3), calls=%async_computation.2 | async-start | bytes 4194304 | tf_op jit(solution)/shard_map/all_to_all | solution.py:256
  72.6 7.2 %collective-permute-start.6 = (bf16[4,2,64,8,128]{4,3,2,1,0:T(8,128)(2,1)S(1)}, bf16[4,2,64,8,128]{4,3,2,1,0:T(8,128)(2,1)}, u32[]{:S(2)}, u32[]{:S(2)}) collective-permute-start(bf16[4,2,64,8,128]{4,3,2,1,0:T(8,128)(2,1)S(1)} %dynamic-slice_bitcast_fusion), channel_id=1, source_target_pairs={{0,16},{16,0},{32,48},{48,32},{64,80},{80,64},{96,112},{112,96},{1... | collective-permute-start | bytes 3145736 | tf_op jit(solution)/shard_map/ppermute | solution.py:216
  75.5 4.3 %copy-start.7 = (bf16[2,4,2,64,8,128]{5,4,3,2,1,0:T(8,128)(2,1)S(1)}, bf16[2,4,2,64,8,128]{5,4,3,2,1,0:T(8,128)(2,1)}, u32[]{:S(2)}) copy-start(bf16[2,4,2,64,8,128]{5,4,3,2,1,0:T(8,128)(2,1)} %copy-done.6) | copy-start | bytes 6291460
  75.8 13.7 %collective-permute-start.1 = (bf16[2,64,16,128]{3,2,1,0:T(8,128)(2,1)S(1)}, bf16[2,64,16,128]{3,2,1,0:T(8,128)(2,1)S(1)}, u32[]{:S(2)}, u32[]{:S(2)}) collective-permute-start(bf16[2,64,16,128]{3,2,1,0:T(8,128)(2,1)S(1)} %get-tuple-element.35), channel_id=1, source_target_pairs={{0,64},{16,80},{32,96},{48,112},{64,0},{80,16},{96,32},{112,48},{1... | collective-permute-start | bytes 1572872 | tf_op jit(solution)/shard_map/ppermute | solution.py:216
  77.2 25.9 %collective-permute-start.2 = (bf16[2,64,16,128]{3,2,1,0:T(8,128)(2,1)S(1)}, bf16[2,64,16,128]{3,2,1,0:T(8,128)(2,1)S(1)}, u32[]{:S(2)}, u32[]{:S(2)}) collective-permute-start(bf16[2,64,16,128]{3,2,1,0:T(8,128)(2,1)S(1)} %get-tuple-element.36), channel_id=1, source_target_pairs={{0,128},{16,144},{32,160},{48,176},{64,192},{80,208},{96,224},{112... | collective-permute-start | bytes 1572872 | tf_op jit(solution)/shard_map/ppermute | solution.py:216
  79.8 25.3 %collective-permute-start.3 = (bf16[2,64,16,128]{3,2,1,0:T(8,128)(2,1)S(1)}, bf16[2,64,16,128]{3,2,1,0:T(8,128)(2,1)S(1)}, u32[]{:S(2)}, u32[]{:S(2)}) collective-permute-start(bf16[2,64,16,128]{3,2,1,0:T(8,128)(2,1)S(1)} %get-tuple-element.34), channel_id=1, source_target_pairs={{0,192},{16,208},{32,224},{48,240},{64,128},{80,144},{96,160},{112... | collective-permute-start | bytes 1572872 | tf_op jit(solution)/shard_map/ppermute | solution.py:216
  81.2 29.6 %copy-start.3 = (bf16[4,2,64,8,128]{4,3,2,1,0:T(8,128)(2,1)}, bf16[4,2,64,8,128]{4,3,2,1,0:T(8,128)(2,1)S(1)}, u32[]{:S(2)}) copy-start(bf16[4,2,64,8,128]{4,3,2,1,0:T(8,128)(2,1)S(1)} %get-tuple-element.23) | copy-start | bytes 3145732
  106.6 90.0 %collective-permute-start.5 = (bf16[3,2,64,16,128]{4,3,2,1,0:T(8,128)(2,1)}, bf16[3,2,64,16,128]{4,3,2,1,0:T(8,128)(2,1)}, u32[]{:S(2)}, u32[]{:S(2)}) collective-permute-start(bf16[3,2,64,16,128]{4,3,2,1,0:T(8,128)(2,1)} %slice.113), channel_id=1, source_target_pairs={{0,32},{16,48},{32,0},{48,16},{64,96},{80,112},{96,64},{112,80},{1... | collective-permute-start | bytes 4718600 | tf_op jit(solution)/shard_map/ppermute | solution.py:216
  112.0 11.9 %collective-permute-start.7 = (bf16[2,64,16,128]{3,2,1,0:T(8,128)(2,1)}, bf16[2,64,16,128]{3,2,1,0:T(8,128)(2,1)}, u32[]{:S(2)}, u32[]{:S(2)}) collective-permute-start(bf16[2,64,16,128]{3,2,1,0:T(8,128)(2,1)} %get-tuple-element.32), channel_id=1, source_target_pairs={{0,64},{16,80},{32,96},{48,112},{64,0},{80,16},{96,32},{112,48},{1... | collective-permute-start | bytes 1572872 | tf_op jit(solution)/shard_map/ppermute | solution.py:216
  112.0 80.7 %collective-permute-start.8 = (bf16[2,64,16,128]{3,2,1,0:T(8,128)(2,1)}, bf16[2,64,16,128]{3,2,1,0:T(8,128)(2,1)}, u32[]{:S(2)}, u32[]{:S(2)}) collective-permute-start(bf16[2,64,16,128]{3,2,1,0:T(8,128)(2,1)} %get-tuple-element.33), channel_id=1, source_target_pairs={{0,128},{16,144},{32,160},{48,176},{64,192},{80,208},{96,224},{112... | collective-permute-start | bytes 1572872 | tf_op jit(solution)/shard_map/ppermute | solution.py:216
  113.4 81.3 %collective-permute-start.9 = (bf16[2,64,16,128]{3,2,1,0:T(8,128)(2,1)}, bf16[2,64,16,128]{3,2,1,0:T(8,128)(2,1)}, u32[]{:S(2)}, u32[]{:S(2)}) collective-permute-start(bf16[2,64,16,128]{3,2,1,0:T(8,128)(2,1)} %get-tuple-element.31), channel_id=1, source_target_pairs={{0,192},{16,208},{32,224},{48,240},{64,128},{80,144},{96,160},{112... | collective-permute-start | bytes 1572872 | tf_op jit(solution)/shard_map/ppermute | solution.py:216
  118.9 7.0 %copy-start.1 = (bf16[16,2,4,64,128]{4,3,2,1,0:T(8,128)(2,1)S(1)}, bf16[16,2,4,64,128]{4,3,2,1,0:T(8,128)(2,1)}, u32[]{:S(2)}) copy-start(bf16[16,2,4,64,128]{4,3,2,1,0:T(8,128)(2,1)} %copy-done) | copy-start | bytes 6291460
  118.9 77.6 %collective-permute-start.4 = (bf16[2,64,16,128]{3,2,1,0:T(8,128)(2,1)S(1)}, bf16[2,64,16,128]{3,2,1,0:T(8,128)(2,1)S(1)}, u32[]{:S(2)}, u32[]{:S(2)}) collective-permute-start(bf16[2,64,16,128]{3,2,1,0:T(8,128)(2,1)S(1)} %slice_bitcast_fusion), channel_id=1, source_target_pairs={{32,0},{48,16},{96,64},{112,80},{160,128},{176,144},{224,192},{240... | collective-permute-start | bytes 1572872 | tf_op jit(solution)/shard_map/ppermute | solution.py:221
  188.3 109.6 %all-to-all-start.1 = ((bf16[16,2,3,64,128]{4,3,2,1,0:T(8,128)(2,1)}), bf16[16,2,3,64,128]{4,3,2,1,0:T(8,128)(2,1)}, u32[]{:S(2)}, u32[]{:S(2)}) async-start(bf16[16,2,3,64,128]{4,3,2,1,0:T(8,128)(2,1)} %copy-done.2), calls=%async_computation.1 | async-start | bytes 3145728 | tf_op jit(solution)/shard_map/all_to_all | solution.py:256
  203.6 30.0 %collective-permute-start.10 = (f32[2,64,128]{2,1,0:T(8,128)S(1)}, f32[2,64,128]{2,1,0:T(8,128)S(1)}, u32[]{:S(2)}, u32[]{:S(2)}) collective-permute-start(f32[2,64,128]{2,1,0:T(8,128)S(1)} %time_stats.1.mine_ref), channel_id=1, source_target_pairs={{0,32},{16,48},{32,0},{48,16},{64,96},{80,112},{96,64},{112,80},{1... | collective-permute-start | bytes 196616 | tf_op jit(solution)/shard_map/ppermute | solution.py:216
  251.8 11.0 %collective-permute-start.17 = (bf16[2,64,16,128]{3,2,1,0:T(8,128)(2,1)S(1)}, bf16[2,64,16,128]{3,2,1,0:T(8,128)(2,1)S(1)}, u32[]{:S(2)}, u32[]{:S(2)}) collective-permute-start(bf16[2,64,16,128]{3,2,1,0:T(8,128)(2,1)S(1)} %dynamic-slice_bitcast_fusion.4), channel_id=1, source_target_pairs={{0,64},{16,80},{32,96},{48,112},{64,0},{80,16},{96,32},{112,48},{1... | collective-permute-start | bytes 1572872 | tf_op jit(solution)/shard_map/ppermute | solution.py:216
  253.4 38.6 %collective-permute-start.12 = (bf16[3,64,16,128]{3,2,1,0:T(8,128)(2,1)S(1)}, bf16[3,64,16,128]{3,2,1,0:T(8,128)(2,1)S(1)}, u32[]{:S(2)}, u32[]{:S(2)}) collective-permute-start(bf16[3,64,16,128]{3,2,1,0:T(8,128)(2,1)S(1)} %get-tuple-element.12), channel_id=1, source_target_pairs={{0,32},{16,48},{32,0},{48,16},{64,96},{80,112},{96,64},{112,80},{1... | collective-permute-start | bytes 2359304 | tf_op jit(solution)/shard_map/ppermute | solution.py:216
  255.1 36.5 %collective-permute-start.11 = (bf16[64,16,128]{2,1,0:T(8,128)(2,1)S(1)}, bf16[64,16,128]{2,1,0:T(8,128)(2,1)S(1)}, u32[]{:S(2)}, u32[]{:S(2)}) collective-permute-start(bf16[64,16,128]{2,1,0:T(8,128)(2,1)S(1)} %get-tuple-element.11), channel_id=1, source_target_pairs={{0,32},{16,48},{64,96},{80,112},{128,160},{144,176},{192,224},{208... | collective-permute-start | bytes 786440 | tf_op jit(solution)/shard_map/ppermute | solution.py:221
  265.1 31.1 %collective-permute-start.18 = (bf16[2,64,16,128]{3,2,1,0:T(8,128)(2,1)S(1)}, bf16[2,64,16,128]{3,2,1,0:T(8,128)(2,1)S(1)}, u32[]{:S(2)}, u32[]{:S(2)}) collective-permute-start(bf16[2,64,16,128]{3,2,1,0:T(8,128)(2,1)S(1)} %get-tuple-element.29), channel_id=1, source_target_pairs={{0,128},{16,144},{32,160},{48,176},{64,192},{80,208},{96,224},{112... | collective-permute-start | bytes 1572872 | tf_op jit(solution)/shard_map/ppermute | solution.py:216
  268.2 28.8 %collective-permute-start.19 = (bf16[2,64,16,128]{3,2,1,0:T(8,128)(2,1)S(1)}, bf16[2,64,16,128]{3,2,1,0:T(8,128)(2,1)S(1)}, u32[]{:S(2)}, u32[]{:S(2)}) collective-permute-start(bf16[2,64,16,128]{3,2,1,0:T(8,128)(2,1)S(1)} %get-tuple-element.28), channel_id=1, source_target_pairs={{0,192},{16,208},{32,224},{48,240},{64,128},{80,144},{96,160},{112... | collective-permute-start | bytes 1572872 | tf_op jit(solution)/shard_map/ppermute | solution.py:216
  292.3 16.5 %collective-permute-start.13 = (bf16[1,64,16,128]{3,2,1,0:T(8,128)(2,1)S(1)}, bf16[1,64,16,128]{3,2,1,0:T(8,128)(2,1)}, u32[]{:S(2)}, u32[]{:S(2)}) collective-permute-start(bf16[1,64,16,128]{3,2,1,0:T(8,128)(2,1)S(1)} %get-tuple-element.47), channel_id=1, source_target_pairs={{0,64},{16,80},{32,96},{48,112},{64,0},{80,16},{96,32},{112,48},{1... | collective-permute-start | bytes 786440 | tf_op jit(solution)/shard_map/ppermute | solution.py:216
  292.8 17.0 %collective-permute-start.14 = (bf16[1,64,16,128]{3,2,1,0:T(8,128)(2,1)S(1)}, bf16[1,64,16,128]{3,2,1,0:T(8,128)(2,1)}, u32[]{:S(2)}, u32[]{:S(2)}) collective-permute-start(bf16[1,64,16,128]{3,2,1,0:T(8,128)(2,1)S(1)} %get-tuple-element.46), channel_id=1, source_target_pairs={{0,128},{16,144},{32,160},{48,176},{64,192},{80,208},{96,224},{112... | collective-permute-start | bytes 786440 | tf_op jit(solution)/shard_map/ppermute | solution.py:216
  295.8 15.0 %collective-permute-start.15 = (bf16[1,64,16,128]{3,2,1,0:T(8,128)(2,1)S(1)}, bf16[1,64,16,128]{3,2,1,0:T(8,128)(2,1)}, u32[]{:S(2)}, u32[]{:S(2)}) collective-permute-start(bf16[1,64,16,128]{3,2,1,0:T(8,128)(2,1)S(1)} %get-tuple-element.45), channel_id=1, source_target_pairs={{0,192},{16,208},{32,224},{48,240},{64,128},{80,144},{96,160},{112... | collective-permute-start | bytes 786440 | tf_op jit(solution)/shard_map/ppermute | solution.py:216
  297.9 44.2 %all-to-all-start.3 = ((bf16[16,2,3,64,128]{4,3,2,1,0:T(8,128)(2,1)}), bf16[16,2,3,64,128]{4,3,2,1,0:T(8,128)(2,1)S(1)}, u32[]{:S(2)}, u32[]{:S(2)}) async-start(bf16[16,2,3,64,128]{4,3,2,1,0:T(8,128)(2,1)} %space_grads.3), calls=%async_computation.3 | async-start | bytes 3145728 | tf_op jit(solution)/shard_map/all_to_all | solution.py:256
  305.6 10.0 %collective-permute-start.20 = (bf16[4,2,64,8,128]{4,3,2,1,0:T(8,128)(2,1)S(1)}, bf16[4,2,64,8,128]{4,3,2,1,0:T(8,128)(2,1)S(1)}, u32[]{:S(2)}, u32[]{:S(2)}) collective-permute-start(bf16[4,2,64,8,128]{4,3,2,1,0:T(8,128)(2,1)S(1)} %broadcast_select_fusion.2), channel_id=1, source_target_pairs={{0,16},{16,0},{32,48},{48,32},{64,80},{80,64},{96,112},{112,96},{1... | collective-permute-start | bytes 3145736 | tf_op jit(solution)/shard_map/ppermute | solution.py:216
  311.9 2.2 collective-permute-start.16
  (10 other events, 16.7 us)

commit v2 on v1

--- a/solution.py
+++ b/solution.py
@@ -81,25 +81,16 @@
     )(x)
 
 
-def frame_rows(side, count, rows, dim_of):
-    i = lax.broadcasted_iota(jnp.int32, *dim_of)
-    return (2 * (i // rows) + side) * rows + i % rows
-
-
-def time_scores(side, qg_ref, rb_ref, ra_ref, kv_ref, p, scale):
+def time_rows(qg_ref, rb_ref, ra_ref, part, p):
     slots, _, _, rows, dim = qg_ref.shape
     half = slots * rows
-    k = kv_ref[:, 0, p].reshape(half, dim)
-    v = kv_ref[:, 1, p].reshape(half, dim)
-    q = jnp.concatenate(
-        [qg_ref[:, 0, p].reshape(half, dim), rb_ref[0, p], ra_ref[:, 0, p].reshape(half - rows, dim)]
+    return jnp.concatenate(
+        [
+            qg_ref[:, part, p].reshape(half, dim),
+            rb_ref[part, p],
+            ra_ref[:, part, p].reshape(half - rows, dim),
+        ]
     )
-    g = jnp.concatenate(
-        [qg_ref[:, 1, p].reshape(half, dim), rb_ref[1, p], ra_ref[:, 1, p].reshape(half - rows, dim)]
-    )
-    s = dot(k, q, NT) * (scale * LOG2E)
-    gv = dot(v, g, NT)
-    return q, g, k, s, gv
 
 
 def time_allowed(side, slots, rows):
@@ -118,15 +109,32 @@
 def time_stats_kernel(side_ref, qg_ref, rb_ref, ra_ref, kv_ref, st_ref, *, scale):
     slots, _, count, rows, _ = qg_ref.shape
     side = side_ref[0]
+    half = slots * rows
     allowed = time_allowed(side, slots, rows)
-    for p in range(count):
-        _, _, _, s, gv = time_scores(side, qg_ref, rb_ref, ra_ref, kv_ref, p, scale)
-        s = jnp.where(allowed, s, MASKED)
-        top = jnp.max(s, axis=0, keepdims=True)
-        e = jnp.exp2(s - top)
-        total = jnp.sum(e, axis=0, keepdims=True)
-        st_ref[0, pl.ds(p, 1)] = top + jnp.log2(total)
-        st_ref[1, pl.ds(p, 1)] = jnp.sum(e * gv, axis=0, keepdims=True) / total
+    patches = range(count)
+    dim = qg_ref.shape[-1]
+    s = [dot(kv_ref[:, 0, p].reshape(half, dim), time_rows(qg_ref, rb_ref, ra_ref, 0, p), NT) for p in patches]
+    gv = [dot(kv_ref[:, 1, p].reshape(half, dim), time_rows(qg_ref, rb_ref, ra_ref, 1, p), NT) for p in patches]
+    s = [jnp.where(allowed, x * (scale * LOG2E), MASKED) for x in s]
+    top = [jnp.max(x, axis=0, keepdims=True) for x in s]
+    e = [jnp.exp2(x - t) for x, t in zip(s, top)]
+    total = [jnp.sum(x, axis=0, keepdims=True) for x in e]
+    part = [jnp.sum(x * y, axis=0, keepdims=True) for x, y in zip(e, gv)]
+    st_ref[0] = jnp.concatenate([t + jnp.log2(x) for t, x in zip(top, total)])
+    st_ref[1] = jnp.concatenate([x / y for x, y in zip(part, total)])
+
+
+def time_totals(mine_ref, other_ref):
+    lse_a, lse_b = mine_ref[0], other_ref[0]
+    top = jnp.maximum(lse_a, lse_b)
+    lse = top + jnp.log2(jnp.exp2(lse_a - top) + jnp.exp2(lse_b - top))
+    delta = jnp.exp2(lse_a - lse) * mine_ref[1] + jnp.exp2(lse_b - lse) * other_ref[1]
+    return lse, delta
+
+
+def time_weights(allowed, s, gv, lse, delta):
+    w = jnp.where(allowed, jnp.exp2(jnp.where(allowed, s - lse, 0.0)), 0.0)
+    return w, (w * (gv - delta)).astype(BF16)
 
 
 def time_grads_kernel(
@@ -134,23 +142,25 @@
 ):
     slots, _, count, rows, dim = qg_ref.shape
     half = slots * rows
-    side = side_ref[0]
-    allowed = time_allowed(side, slots, rows)
-    lse_a, lse_b = mine_ref[0], other_ref[0]
-    top = jnp.maximum(lse_a, lse_b)
-    lse = top + jnp.log2(jnp.exp2(lse_a - top) + jnp.exp2(lse_b - top))
-    delta = jnp.exp2(lse_a - lse) * mine_ref[1] + jnp.exp2(lse_b - lse) * other_ref[1]
-    for p in range(count):
-        q, g, k, s, gv = time_scores(side, qg_ref, rb_ref, ra_ref, kv_ref, p, scale)
-        w = jnp.where(allowed, jnp.exp2(jnp.where(allowed, s - lse[p : p + 1], 0.0)), 0.0)
-        ds = (w * (gv - delta[p : p + 1])).astype(BF16)
-        w = w.astype(BF16)
-        dkv_ref[:, 1, p] = dot(w, g, NN).astype(BF16).reshape(slots, rows, dim)
-        dkv_ref[:, 0, p] = (dot(ds, q, NN) * scale).astype(BF16).reshape(slots, rows, dim)
-        dq = dot(ds, k, TN) * scale
-        dq_ref[:, p] = dq[:half].reshape(slots, rows, dim)
-        db_ref[p] = dq[half : half + rows].astype(BF16)
-        da_ref[:, p] = dq[half + rows :].astype(BF16).reshape(slots - 1, rows, dim)
+    allowed = time_allowed(side_ref[0], slots, rows)
+    lse, delta = time_totals(mine_ref, other_ref)
+    patches = range(count)
+    k = [kv_ref[:, 0, p].reshape(half, dim) for p in patches]
+    q = [time_rows(qg_ref, rb_ref, ra_ref, 0, p) for p in patches]
+    g = [time_rows(qg_ref, rb_ref, ra_ref, 1, p) for p in patches]
+    s = [dot(k[p], q[p], NT) * (scale * LOG2E) for p in patches]
+    gv = [dot(kv_ref[:, 1, p].reshape(half, dim), g[p], NT) for p in patches]
+    both = [time_weights(allowed, s[p], gv[p], lse[p : p + 1], delta[p : p + 1]) for p in patches]
+    dv = [dot(both[p][0].astype(BF16), g[p], NN) for p in patches]
+    dk = [dot(both[p][1], q[p], NN) for p in patches]
+    dq = [dot(both[p][1], k[p], TN) for p in patches]
+    for p in patches:
+        dkv_ref[:, 1, p] = dv[p].astype(BF16).reshape(slots, rows, dim)
+        dkv_ref[:, 0, p] = (dk[p] * scale).astype(BF16).reshape(slots, rows, dim)
+        x = dq[p] * scale
+        dq_ref[:, p] = x[:half].reshape(slots, rows, dim)
+        db_ref[p] = x[half : half + rows].astype(BF16)
+        da_ref[:, p] = x[half + rows :].astype(BF16).reshape(slots - 1, rows, dim)
 
 
 def time_specs(group, slots, rows, dim):
@@ -242,18 +252,25 @@
 
 
 def scatter_frames(u, y, core):
-    v = y_exchange(u, y)
-    half = v.shape[-2] // 2
-    low, high = v[..., :half, :], v[..., half:, :]
-    first = core == 0
-    keep = jnp.where(first, low, high)
-    got = swap(jnp.where(first, high, low), CORE_BIT)
-    t = jnp.concatenate([jnp.where(first, keep, got), jnp.where(first, got, keep)], axis=0)
-    return [jnp.transpose(t[:, i], (2, 0, 1, 3)) for i in range(t.shape[1])]
+    slots, n, count, rows, dim = u.shape
+    t = jnp.transpose(u.reshape(slots, n, count, 2, rows // 2, dim), (0, 3, 1, 4, 2, 5))
+    out = [jnp.zeros((rows // 2, 2 * slots, count, dim), u.dtype) for _ in range(n)]
+    for j in range(slots):
+        for c in range(2):
+            piece = pick(pick(t, y ^ j), core ^ c)
+            if j or c:
+                piece = swap(piece, j * Y_BIT + c * CORE_BIT)
+            head = (core ^ c) * slots + (y ^ j)
+            out = [lax.dynamic_update_index_in_dim(o, piece[i], head, 1) for i, o in enumerate(out)]
+    return out
 
 
 def exchange_patches(x):
     return lax.all_to_all(x, "patch", split_axis=0, concat_axis=0, tiled=True)
+
+
+def after(values, done):
+    return lax.optimization_barrier(tuple(values) + (done,))
 
 
 def per_device(q_space, k_space, v_space, d_out_space, q_time, k_time, v_time, d_out_time):
@@ -265,27 +282,40 @@
 
     space = [a.reshape(seqs, rows, dim) for a in (q_space, k_space, v_space, d_out_space)]
     width = seqs // CHUNKS
-    arrived = []
-    for c in range(CHUNKS):
+
+    def space_part(c):
         x = jnp.stack([a[c * width : (c + 1) * width] for a in space], 1)
-        arrived.append(exchange_patches(x.reshape(PATCH_DEVICES, width // PATCH_DEVICES, 4, rows, dim)))
-
+        return x.reshape(PATCH_DEVICES, width // PATCH_DEVICES, 4, rows, dim)
+
+    first, second = space_part(0), space_part(1)
+    first = exchange_patches(first)
     qg = gather_frames((q_time, d_out_time), y, core)
     ra = swap(qg[1:], ZHI_BIT)
     rb = from_side(qg[0], 1)
+    k_time, v_time, first, second, qg = after((k_time, v_time, first, second), qg)
+    second = exchange_patches(second)
     kv = gather_frames((k_time, v_time), y, core)
-
-    back = [exchange_patches(space_grads(x)).reshape(width, 3, rows, dim) for x in arrived]
-
+    first = space_grads(first)
+
+    kv, rb, first, second = lax.optimization_barrier((kv, rb, first, second))
+    first, _ = after((first,), ra)
+    first = exchange_patches(first)
     mine = time_stats(side_arr, qg, rb, ra, kv)
     other = swap(mine, ZHI_BIT)
     other = jnp.roll(other, other.shape[-1] // 2, axis=-1)
+    second = space_grads(second)
+    second, other = after((second,), other)
     dq, db, da, dkv = time_grads(side_arr, qg, rb, ra, kv, mine, other)
-    da = swap(da, ZHI_BIT)
-    db = from_side(db, 0)
-    dq = (dq + jnp.concatenate([db[None], da]).astype(F32)).astype(BF16)
+    db_sent, da_sent = from_side(db, 0), swap(da, ZHI_BIT)
+    second, _ = after((second,), da)
+    second = exchange_patches(second)
+    dkv, first = after((dkv,), first)
     dk_time, dv_time = scatter_frames(dkv, y, core)
+    dq, dk_time = after((dq,), dk_time)
+    dq = (dq + jnp.concatenate([db_sent[None], da_sent]).astype(F32)).astype(BF16)
     (dq_time,) = scatter_frames(dq[:, None], y, core)
+    second, dq_time = after((second,), dq_time)
+    back = [x.reshape(width, 3, rows, dim) for x in (first, second)]
 
     shape = (frames, heads, rows, dim)
     out = [jnp.concatenate([b[:, i] for b in back]).reshape(shape) for i in range(3)]

time: 346 us -> 331 us (0.957)
  starting transfers between devices: 74 us -> 85 us
  Pallas kernels: 45.8 us -> 36.8 us
  local copies, waits for them, and re-layouts: 35.2 us -> 27.1 us
  other arithmetic: 17.6 us -> 10.1 us
    all_to_all x4, waiting for transfers between devices: 113 us -> 14.7 us  [exchange_patches(): return lax.all_to_all(x, 'patch', split_axis=0, concat_axis=0, tiled=True)]
    ppermute x2, waiting for transfers between devices: 10.7 us -> 66.2 us  [from_side(): return lax.ppermute(x, 'frame', pairs)]
    ppermute x19 -> x25, waiting for transfers between devices: 47.5 us -> 88.8 us  [swap(): lax.ppermute(x, 'frame', [(i, i ^ bits) for i in range(FRAME_DEVICES)])]
    dynamic_update_slice x11 -> x6, local copies, waits for them, and re-layouts: 10.5 us -> 0.41 us  [y_exchange(): u = lax.dynamic_update_index_in_dim(u, got[j - 1], y ^ j, 0)]
    pallas_call x1, Pallas kernels: 16.9 us -> 8.33 us  [time_grads(): pl.pallas_call(functools.partial(time_grads_kernel, scale=1.0 / math.sqrt...]
    all_to_all x4, starting transfers between devices: 23.9 us -> 29 us  [exchange_patches(): return lax.all_to_all(x, 'patch', split_axis=0, concat_axis=0, tiled=True)]
    select_n x4 -> x0, other arithmetic: 3.58 us -> none  [the longest x1 1.74 us: scatter_frames(): jnp.where(first, got, keep)]
    ppermute x19 -> x25, starting transfers between devices: 43.2 us -> 46.7 us  [swap(): lax.ppermute(x, 'frame', [(i, i ^ bits) for i in range(FRAME_DEVICES)])]
  transfers between devices with their start and end apart: 25 -> 31, of which waited for: 12 -> 20; matrix products, arithmetic and copies ran while one was open for 12% -> 6% of each run, Pallas kernels for 13% -> 11%
where the time goes in v2:
time: 331 us; the launch traced here: 330 us
  waiting for transfers between devices  170 us (51%)
  starting transfers between devices  85 us (26%)
  Pallas kernels  36.8 us (11%)
  local copies, waits for them, and re-layouts  27.1 us (8%)
  other arithmetic  10.1 us (3%)
    ppermute x25, waiting for transfers between devices, swap(): lax.ppermute(x, 'frame', [(i, i ^ bits) for i in range(FRAME_DEVICES)])  88.8 us
    ppermute x2, waiting for transfers between devices, from_side(): return lax.ppermute(x, 'frame', pairs)  66.2 us
    ppermute x25, starting transfers between devices, swap(): lax.ppermute(x, 'frame', [(i, i ^ bits) for i in range(FRAME_DEVICES)])  46.7 us
    all_to_all x4, starting transfers between devices, exchange_patches(): return lax.all_to_all(x, 'patch', split_axis=0, concat_axis=0, tiled=True)  29 us
    pallas_call x2, Pallas kernels, space_grads(): pl.pallas_call(functools.partial(space_kernel, block=256, scale=1.0 / mat...  22.1 us
    all_to_all x4, waiting for transfers between devices, exchange_patches(): return lax.all_to_all(x, 'patch', split_axis=0, concat_axis=0, tiled=True)  14.7 us
    unnamed x55, local copies, waits for them, and re-layouts  12.9 us
    ppermute x2, starting transfers between devices, from_side(): return lax.ppermute(x, 'frame', pairs)  9.26 us
  transfers between devices with their start and end apart: 31, of which 20 were waited for; matrix products, arithmetic and copies ran while one was open for 6% of the time, Pallas kernels for 11%

profile of v2, /device:TPU:1, one launch (start us, length us, event | category | flops | bytes accessed | tf_op | source)
XLA Modules:
  0.0 330.3 jit_solution(16519750415619338777)
XLA Ops:
  5.9 9.1 %all-to-all-start = ((bf16[16,2,4,64,128]{4,3,2,1,0:T(8,128)(2,1)}), bf16[16,2,4,64,128]{4,3,2,1,0:T(8,128)(2,1)}, u32[]{:S(2)}, u32[]{:S(2)}) async-start(bf16[16,2,4,64,128]{4,3,2,1,0:T(8,128)(2,1)} %pad_maximum_fusion.2), calls=%async_computation | async-start | bytes 4194304 | tf_op jit(solution)/shard_map/all_to_all | solution.py:269
  31.2 7.3 %collective-permute-done.1 = bf16[2,64,16,128]{3,2,1,0:T(8,128)(2,1)S(1)} collective-permute-done((bf16[2,64,16,128]{3,2,1,0:T(8,128)(2,1)S(1)}, bf16[2,64,16,128]{3,2,1,0:T(8,128)(2,1)S(1)}, u32[]{:S(2)}, u32[]{:S(2)}) %collective-permute-start.1) | collective-permute-done | bytes 524320 | tf_op jit(solution)/shard_map/ppermute | solution.py:226
  38.6 13.6 %collective-permute-done.2 = bf16[2,64,16,128]{3,2,1,0:T(8,128)(2,1)S(1)} collective-permute-done((bf16[2,64,16,128]{3,2,1,0:T(8,128)(2,1)S(1)}, bf16[2,64,16,128]{3,2,1,0:T(8,128)(2,1)S(1)}, u32[]{:S(2)}, u32[]{:S(2)}) %collective-permute-start.2) | collective-permute-done | bytes 524320 | tf_op jit(solution)/shard_map/ppermute | solution.py:226
  52.2 3.5 %collective-permute-done.3 = bf16[2,64,16,128]{3,2,1,0:T(8,128)(2,1)S(1)} collective-permute-done((bf16[2,64,16,128]{3,2,1,0:T(8,128)(2,1)S(1)}, bf16[2,64,16,128]{3,2,1,0:T(8,128)(2,1)S(1)}, u32[]{:S(2)}, u32[]{:S(2)}) %collective-permute-start.3) | collective-permute-done | bytes 524320 | tf_op jit(solution)/shard_map/ppermute | solution.py:226
  55.9 9.0 %all-to-all-done.x_ref = bf16[16,2,4,64,128]{4,3,2,1,0:T(8,128)(2,1)} async-done(((bf16[16,2,4,64,128]{4,3,2,1,0:T(8,128)(2,1)}), bf16[16,2,4,64,128]{4,3,2,1,0:T(8,128)(2,1)}, u32[]{:S(2)}, u32[]{:S(2)}) %all-to-all-start) | async-done | bytes 2097184 | tf_op jit(solution)/shard_map/all_to_all | solution.py:269
  64.8 4.4 %all-to-all-start.1 = ((bf16[16,2,4,64,128]{4,3,2,1,0:T(8,128)(2,1)}), bf16[16,2,4,64,128]{4,3,2,1,0:T(8,128)(2,1)}, u32[]{:S(2)}, u32[]{:S(2)}) async-start(bf16[16,2,4,64,128]{4,3,2,1,0:T(8,128)(2,1)} %pad_maximum_fusion.3), calls=%async_computation.1 | async-start | bytes 4194304 | tf_op jit(solution)/shard_map/all_to_all | solution.py:269
  74.3 4.2 %collective-permute-start.9 = (bf16[3,2,64,16,128]{4,3,2,1,0:T(8,128)(2,1)}, bf16[3,2,64,16,128]{4,3,2,1,0:T(8,128)(2,1)}, u32[]{:S(2)}, u32[]{:S(2)}) collective-permute-start(bf16[3,2,64,16,128]{4,3,2,1,0:T(8,128)(2,1)} %slice.149), channel_id=1, source_target_pairs={{0,32},{16,48},{32,0},{48,16},{64,96},{80,112},{96,64},{112,80},{1... | collective-permute-start | bytes 4718600 | tf_op jit(solution)/shard_map/ppermute | solution.py:226
  81.7 2.9 collective-permute-start.6
  84.6 11.1 %space_grads.2 = bf16[16,2,3,64,128]{4,3,2,1,0:T(8,128)(2,1)S(1)} custom-call(bf16[16,2,4,64,128]{4,3,2,1,0:T(8,128)(2,1)} %all-to-all-done.x_ref), custom_call_target="tpu_custom_call" | custom-call | flops 2684354560 | bytes 4194304 | tf_op jit(solution)/shard_map/space_grads/pallas_call | solution.py:69
  97.0 9.0 %collective-permute-done.6 = bf16[2,64,16,128]{3,2,1,0:T(8,128)(2,1)S(1)} collective-permute-done((bf16[2,64,16,128]{3,2,1,0:T(8,128)(2,1)S(1)}, bf16[2,64,16,128]{3,2,1,0:T(8,128)(2,1)S(1)}, u32[]{:S(2)}, u32[]{:S(2)}) %collective-permute-start.6) | collective-permute-done | bytes 524320 | tf_op jit(solution)/shard_map/ppermute | solution.py:226
  106.1 11.7 %collective-permute-done.7 = bf16[2,64,16,128]{3,2,1,0:T(8,128)(2,1)S(1)} collective-permute-done((bf16[2,64,16,128]{3,2,1,0:T(8,128)(2,1)S(1)}, bf16[2,64,16,128]{3,2,1,0:T(8,128)(2,1)S(1)}, u32[]{:S(2)}, u32[]{:S(2)}) %collective-permute-start.7) | collective-permute-done | bytes 524320 | tf_op jit(solution)/shard_map/ppermute | solution.py:226
  119.2 66.2 %collective-permute-done.8.rb_ref = bf16[2,64,16,128]{3,2,1,0:T(8,128)(2,1)S(1)} collective-permute-done((bf16[2,64,16,128]{3,2,1,0:T(8,128)(2,1)S(1)}, bf16[2,64,16,128]{3,2,1,0:T(8,128)(2,1)S(1)}, u32[]{:S(2)}, u32[]{:S(2)}) %collective-permute-start.8) | collective-permute-done | bytes 524320 | tf_op jit(solution)/shard_map/ppermute | solution.py:231
  185.4 5.8 %all-to-all-done.1.x_ref = bf16[16,2,4,64,128]{4,3,2,1,0:T(8,128)(2,1)} async-done(((bf16[16,2,4,64,128]{4,3,2,1,0:T(8,128)(2,1)}), bf16[16,2,4,64,128]{4,3,2,1,0:T(8,128)(2,1)}, u32[]{:S(2)}, u32[]{:S(2)}) %all-to-all-start.1) | async-done | bytes 2097184 | tf_op jit(solution)/shard_map/all_to_all | solution.py:269
  191.2 8.6 %all-to-all-start.2 = ((bf16[16,2,3,64,128]{4,3,2,1,0:T(8,128)(2,1)}), bf16[16,2,3,64,128]{4,3,2,1,0:T(8,128)(2,1)}, u32[]{:S(2)}, u32[]{:S(2)}) async-start(bf16[16,2,3,64,128]{4,3,2,1,0:T(8,128)(2,1)} %copy-done.8), calls=%async_computation.2 | async-start | bytes 3145728 | tf_op jit(solution)/shard_map/all_to_all | solution.py:269
  201.6 6.3 %time_stats.1.mine_ref = f32[2,64,128]{2,1,0:T(8,128)S(1)} custom-call(s32[1]{0:T(128)} %bitcast.side_ref, bf16[4,2,64,16,128]{4,3,2,1,0:T(8,128)(2,1)S(1)} %bitcast_dynamic-update-slice_fusion.3.qg_ref, bf16[2,64,16,128]{3,2,1,0:T(8,128)(2,1)S(1)} %collective-permute-done.8.rb_ref, bf16[3,2,64,16,128]{4,3,2,1,0:T(8,128)(2,1)} %collective-permute-done.9.ra_ref, ...), custom_call_target="tpu_custom_call" | custom-call | flops 268435456 | bytes 6291456 | tf_op jit(solution)/shard_map/time_stats/pallas_call | solution.py:179
  207.9 6.8 %collective-permute-start.10 = (f32[2,64,128]{2,1,0:T(8,128)S(1)}, f32[2,64,128]{2,1,0:T(8,128)S(1)}, u32[]{:S(2)}, u32[]{:S(2)}) collective-permute-start(f32[2,64,128]{2,1,0:T(8,128)S(1)} %time_stats.1.mine_ref), channel_id=1, source_target_pairs={{0,32},{16,48},{32,0},{48,16},{64,96},{80,112},{96,64},{112,80},{1... | collective-permute-start | bytes 196616 | tf_op jit(solution)/shard_map/ppermute | solution.py:226
  214.7 11.1 %space_grads.3 = bf16[16,2,3,64,128]{4,3,2,1,0:T(8,128)(2,1)S(1)} custom-call(bf16[16,2,4,64,128]{4,3,2,1,0:T(8,128)(2,1)} %all-to-all-done.1.x_ref), custom_call_target="tpu_custom_call" | custom-call | flops 2684354560 | bytes 4194304 | tf_op jit(solution)/shard_map/space_grads/pallas_call | solution.py:69
  227.0 6.9 %collective-permute-done.10 = f32[2,64,128]{2,1,0:T(8,128)S(1)} collective-permute-done((f32[2,64,128]{2,1,0:T(8,128)S(1)}, f32[2,64,128]{2,1,0:T(8,128)S(1)}, u32[]{:S(2)}, u32[]{:S(2)}) %collective-permute-start.10) | collective-permute-done | bytes 65568 | tf_op jit(solution)/shard_map/ppermute | solution.py:226
  234.1 8.3 %time_grads.1 = (f32[4,64,16,128]{3,2,1,0:T(8,128)S(1)}, bf16[64,16,128]{2,1,0:T(8,128)(2,1)}, bf16[3,64,16,128]{3,2,1,0:T(8,128)(2,1)S(1)}, bf16[4,2,64,16,128]{4,3,2,1,0:T(8,128)(2,1)S(1)}) custom-call(s32[1]{0:T(128)} %bitcast.side_ref, bf16[4,2,64,16,128]{4,3,2,1,0:T(8,128)(2,1)S(1)} %bitcast_dynamic-update-slice_fusion.3.qg_ref, ...), custom_call_target="tpu_custom_call" | custom-call | flops 671088640 | bytes 10485760 | tf_op jit(solution)/shard_map/time_grads/pallas_call | solution.py:199
  245.0 8.0 %collective-permute-start.18 = (bf16[64,16,128]{2,1,0:T(8,128)(2,1)}, bf16[64,16,128]{2,1,0:T(8,128)(2,1)}, u32[]{:S(2)}, u32[]{:S(2)}) collective-permute-start(bf16[64,16,128]{2,1,0:T(8,128)(2,1)} %get-tuple-element.48), channel_id=1, source_target_pairs={{0,32},{16,48},{64,96},{80,112},{128,160},{144,176},{192,224},{208... | collective-permute-start | bytes 786440 | tf_op jit(solution)/shard_map/ppermute | solution.py:231
  253.0 6.9 %all-to-all-start.3 = ((bf16[16,2,3,64,128]{4,3,2,1,0:T(8,128)(2,1)}), bf16[16,2,3,64,128]{4,3,2,1,0:T(8,128)(2,1)}, u32[]{:S(2)}, u32[]{:S(2)}) async-start(bf16[16,2,3,64,128]{4,3,2,1,0:T(8,128)(2,1)} %copy-done.7), calls=%async_computation.3 | async-start | bytes 3145728 | tf_op jit(solution)/shard_map/all_to_all | solution.py:269
  260.4 3.5 %collective-permute-start.11 = (bf16[2,8,64,128]{3,2,1,0:T(8,128)(2,1)S(1)}, bf16[2,8,64,128]{3,2,1,0:T(8,128)(2,1)S(1)}, u32[]{:S(2)}, u32[]{:S(2)}) collective-permute-start(bf16[2,8,64,128]{3,2,1,0:T(8,128)(2,1)S(1)} %bitcast.281), channel_id=1, source_target_pairs={{0,16},{16,0},{32,48},{48,32},{64,80},{80,64},{96,112},{112,96},{1... | collective-permute-start | bytes 786440 | tf_op jit(solution)/shard_map/ppermute | solution.py:226
  268.1 3.0 collective-permute-start.14
  272.1 3.9 %collective-permute-start.15 = (bf16[2,8,64,128]{3,2,1,0:T(8,128)(2,1)S(1)}, bf16[2,8,64,128]{3,2,1,0:T(8,128)(2,1)S(1)}, u32[]{:S(2)}, u32[]{:S(2)}) collective-permute-start(bf16[2,8,64,128]{3,2,1,0:T(8,128)(2,1)S(1)} %bitcast.277), channel_id=1, source_target_pairs={{0,144},{16,128},{32,176},{48,160},{64,208},{80,192},{96,240},{112... | collective-permute-start | bytes 786440 | tf_op jit(solution)/shard_map/ppermute | solution.py:226
  281.3 4.4 %collective-permute-done.14 = bf16[2,8,64,128]{3,2,1,0:T(8,128)(2,1)S(1)} collective-permute-done((bf16[2,8,64,128]{3,2,1,0:T(8,128)(2,1)S(1)}, bf16[2,8,64,128]{3,2,1,0:T(8,128)(2,1)S(1)}, u32[]{:S(2)}, u32[]{:S(2)}) %collective-permute-start.14) | collective-permute-done | bytes 262176 | tf_op jit(solution)/shard_map/ppermute | solution.py:226
  286.8 4.7 %collective-permute-done.15 = bf16[2,8,64,128]{3,2,1,0:T(8,128)(2,1)S(1)} collective-permute-done((bf16[2,8,64,128]{3,2,1,0:T(8,128)(2,1)S(1)}, bf16[2,8,64,128]{3,2,1,0:T(8,128)(2,1)S(1)}, u32[]{:S(2)}, u32[]{:S(2)}) %collective-permute-start.15) | collective-permute-done | bytes 262176 | tf_op jit(solution)/shard_map/ppermute | solution.py:226
  291.5 5.9 %collective-permute-done.16 = bf16[2,8,64,128]{3,2,1,0:T(8,128)(2,1)S(1)} collective-permute-done((bf16[2,8,64,128]{3,2,1,0:T(8,128)(2,1)S(1)}, bf16[2,8,64,128]{3,2,1,0:T(8,128)(2,1)S(1)}, u32[]{:S(2)}, u32[]{:S(2)}) %collective-permute-start.16) | collective-permute-done | bytes 262176 | tf_op jit(solution)/shard_map/ppermute | solution.py:226
  297.4 5.6 %collective-permute-done.17 = bf16[2,8,64,128]{3,2,1,0:T(8,128)(2,1)S(1)} collective-permute-done((bf16[2,8,64,128]{3,2,1,0:T(8,128)(2,1)S(1)}, bf16[2,8,64,128]{3,2,1,0:T(8,128)(2,1)S(1)}, u32[]{:S(2)}, u32[]{:S(2)}) %collective-permute-start.17) | collective-permute-done | bytes 262176 | tf_op jit(solution)/shard_map/ppermute | solution.py:226
  309.1 2.9 collective-permute-start.24
  312.4 3.1 collective-permute-start.26
  316.8 3.2 collective-permute-done.24
  320.1 3.0 collective-permute-done.25
  (142 shorter events, 65.0 us)
Async XLA Ops:
  5.9 58.9 %all-to-all-start = ((bf16[16,2,4,64,128]{4,3,2,1,0:T(8,128)(2,1)}), bf16[16,2,4,64,128]{4,3,2,1,0:T(8,128)(2,1)}, u32[]{:S(2)}, u32[]{:S(2)}) async-start(bf16[16,2,4,64,128]{4,3,2,1,0:T(8,128)(2,1)} %pad_maximum_fusion.2), calls=%async_computation | async-start | bytes 4194304 | tf_op jit(solution)/shard_map/all_to_all | solution.py:269
  19.9 3.6 %collective-permute-start = (bf16[4,2,64,8,128]{4,3,2,1,0:T(8,128)(2,1)}, bf16[4,2,64,8,128]{4,3,2,1,0:T(8,128)(2,1)}, u32[]{:S(2)}, u32[]{:S(2)}) collective-permute-start(bf16[4,2,64,8,128]{4,3,2,1,0:T(8,128)(2,1)} %dynamic-slice_bitcast_fusion.1), channel_id=1, source_target_pairs={{0,16},{16,0},{32,48},{48,32},{64,80},{80,64},{96,112},{112,96},{1... | collective-permute-start | bytes 3145736 | tf_op jit(solution)/shard_map/ppermute | solution.py:226
  25.2 13.3 %collective-permute-start.1 = (bf16[2,64,16,128]{3,2,1,0:T(8,128)(2,1)S(1)}, bf16[2,64,16,128]{3,2,1,0:T(8,128)(2,1)S(1)}, u32[]{:S(2)}, u32[]{:S(2)}) collective-permute-start(bf16[2,64,16,128]{3,2,1,0:T(8,128)(2,1)S(1)} %get-tuple-element.68), channel_id=1, source_target_pairs={{0,64},{16,80},{32,96},{48,112},{64,0},{80,16},{96,32},{112,48},{1... | collective-permute-start | bytes 1572872 | tf_op jit(solution)/shard_map/ppermute | solution.py:226
  26.6 25.6 %collective-permute-start.2 = (bf16[2,64,16,128]{3,2,1,0:T(8,128)(2,1)S(1)}, bf16[2,64,16,128]{3,2,1,0:T(8,128)(2,1)S(1)}, u32[]{:S(2)}, u32[]{:S(2)}) collective-permute-start(bf16[2,64,16,128]{3,2,1,0:T(8,128)(2,1)S(1)} %get-tuple-element.69), channel_id=1, source_target_pairs={{0,128},{16,144},{32,160},{48,176},{64,192},{80,208},{96,224},{112... | collective-permute-start | bytes 1572872 | tf_op jit(solution)/shard_map/ppermute | solution.py:226
  30.8 24.9 %collective-permute-start.3 = (bf16[2,64,16,128]{3,2,1,0:T(8,128)(2,1)S(1)}, bf16[2,64,16,128]{3,2,1,0:T(8,128)(2,1)S(1)}, u32[]{:S(2)}, u32[]{:S(2)}) collective-permute-start(bf16[2,64,16,128]{3,2,1,0:T(8,128)(2,1)S(1)} %get-tuple-element.67), channel_id=1, source_target_pairs={{0,192},{16,208},{32,224},{48,240},{64,128},{80,144},{96,160},{112... | collective-permute-start | bytes 1572872 | tf_op jit(solution)/shard_map/ppermute | solution.py:226
  64.8 126.4 %all-to-all-start.1 = ((bf16[16,2,4,64,128]{4,3,2,1,0:T(8,128)(2,1)}), bf16[16,2,4,64,128]{4,3,2,1,0:T(8,128)(2,1)}, u32[]{:S(2)}, u32[]{:S(2)}) async-start(bf16[16,2,4,64,128]{4,3,2,1,0:T(8,128)(2,1)} %pad_maximum_fusion.3), calls=%async_computation.1 | async-start | bytes 4194304 | tf_op jit(solution)/shard_map/all_to_all | solution.py:269
  71.3 7.2 %collective-permute-start.4 = (bf16[4,2,64,8,128]{4,3,2,1,0:T(8,128)(2,1)S(1)}, bf16[4,2,64,8,128]{4,3,2,1,0:T(8,128)(2,1)S(1)}, u32[]{:S(2)}, u32[]{:S(2)}) collective-permute-start(bf16[4,2,64,8,128]{4,3,2,1,0:T(8,128)(2,1)S(1)} %dynamic-slice_bitcast_fusion), channel_id=1, source_target_pairs={{0,16},{16,0},{32,48},{48,32},{64,80},{80,64},{96,112},{112,96},{1... | collective-permute-start | bytes 3145736 | tf_op jit(solution)/shard_map/ppermute | solution.py:226
  74.3 116.9 %collective-permute-start.9 = (bf16[3,2,64,16,128]{4,3,2,1,0:T(8,128)(2,1)}, bf16[3,2,64,16,128]{4,3,2,1,0:T(8,128)(2,1)}, u32[]{:S(2)}, u32[]{:S(2)}) collective-permute-start(bf16[3,2,64,16,128]{4,3,2,1,0:T(8,128)(2,1)} %slice.149), channel_id=1, source_target_pairs={{0,32},{16,48},{32,0},{48,16},{64,96},{80,112},{96,64},{112,80},{1... | collective-permute-start | bytes 4718600 | tf_op jit(solution)/shard_map/ppermute | solution.py:226
  79.0 17.9 %collective-permute-start.5 = (bf16[2,64,16,128]{3,2,1,0:T(8,128)(2,1)S(1)}, bf16[2,64,16,128]{3,2,1,0:T(8,128)(2,1)S(1)}, u32[]{:S(2)}, u32[]{:S(2)}) collective-permute-start(bf16[2,64,16,128]{3,2,1,0:T(8,128)(2,1)S(1)} %get-tuple-element.65), channel_id=1, source_target_pairs={{0,64},{16,80},{32,96},{48,112},{64,0},{80,16},{96,32},{112,48},{1... | collective-permute-start | bytes 1572872 | tf_op jit(solution)/shard_map/ppermute | solution.py:226
  80.4 105.1 %collective-permute-start.8 = (bf16[2,64,16,128]{3,2,1,0:T(8,128)(2,1)S(1)}, bf16[2,64,16,128]{3,2,1,0:T(8,128)(2,1)S(1)}, u32[]{:S(2)}, u32[]{:S(2)}) collective-permute-start(bf16[2,64,16,128]{3,2,1,0:T(8,128)(2,1)S(1)} %slice_bitcast_fusion.6), channel_id=1, source_target_pairs={{32,0},{48,16},{96,64},{112,80},{160,128},{176,144},{224,192},{240... | collective-permute-start | bytes 1572872 | tf_op jit(solution)/shard_map/ppermute | solution.py:231
  81.7 24.3 %collective-permute-start.6 = (bf16[2,64,16,128]{3,2,1,0:T(8,128)(2,1)S(1)}, bf16[2,64,16,128]{3,2,1,0:T(8,128)(2,1)S(1)}, u32[]{:S(2)}, u32[]{:S(2)}) collective-permute-start(bf16[2,64,16,128]{3,2,1,0:T(8,128)(2,1)S(1)} %get-tuple-element.66), channel_id=1, source_target_pairs={{0,128},{16,144},{32,160},{48,176},{64,192},{80,208},{96,224},{112... | collective-permute-start | bytes 1572872 | tf_op jit(solution)/shard_map/ppermute | solution.py:226
  95.6 22.2 %collective-permute-start.7 = (bf16[2,64,16,128]{3,2,1,0:T(8,128)(2,1)S(1)}, bf16[2,64,16,128]{3,2,1,0:T(8,128)(2,1)S(1)}, u32[]{:S(2)}, u32[]{:S(2)}) collective-permute-start(bf16[2,64,16,128]{3,2,1,0:T(8,128)(2,1)S(1)} %get-tuple-element.64), channel_id=1, source_target_pairs={{0,192},{16,208},{32,224},{48,240},{64,128},{80,144},{96,160},{112... | collective-permute-start | bytes 1572872 | tf_op jit(solution)/shard_map/ppermute | solution.py:226
  191.2 61.8 %all-to-all-start.2 = ((bf16[16,2,3,64,128]{4,3,2,1,0:T(8,128)(2,1)}), bf16[16,2,3,64,128]{4,3,2,1,0:T(8,128)(2,1)}, u32[]{:S(2)}, u32[]{:S(2)}) async-start(bf16[16,2,3,64,128]{4,3,2,1,0:T(8,128)(2,1)} %copy-done.8), calls=%async_computation.2 | async-start | bytes 3145728 | tf_op jit(solution)/shard_map/all_to_all | solution.py:269
  207.9 25.9 %collective-permute-start.10 = (f32[2,64,128]{2,1,0:T(8,128)S(1)}, f32[2,64,128]{2,1,0:T(8,128)S(1)}, u32[]{:S(2)}, u32[]{:S(2)}) collective-permute-start(f32[2,64,128]{2,1,0:T(8,128)S(1)} %time_stats.1.mine_ref), channel_id=1, source_target_pairs={{0,32},{16,48},{32,0},{48,16},{64,96},{80,112},{96,64},{112,80},{1... | collective-permute-start | bytes 196616 | tf_op jit(solution)/shard_map/ppermute | solution.py:226
  245.0 58.0 %collective-permute-start.19 = (bf16[3,64,16,128]{3,2,1,0:T(8,128)(2,1)S(1)}, bf16[3,64,16,128]{3,2,1,0:T(8,128)(2,1)}, u32[]{:S(2)}, u32[]{:S(2)}) collective-permute-start(bf16[3,64,16,128]{3,2,1,0:T(8,128)(2,1)S(1)} %get-tuple-element.43), channel_id=1, source_target_pairs={{0,32},{16,48},{32,0},{48,16},{64,96},{80,112},{96,64},{112,80},{1... | collective-permute-start | bytes 2359304 | tf_op jit(solution)/shard_map/ppermute | solution.py:226
  245.0 58.0 %collective-permute-start.18 = (bf16[64,16,128]{2,1,0:T(8,128)(2,1)}, bf16[64,16,128]{2,1,0:T(8,128)(2,1)}, u32[]{:S(2)}, u32[]{:S(2)}) collective-permute-start(bf16[64,16,128]{2,1,0:T(8,128)(2,1)} %get-tuple-element.48), channel_id=1, source_target_pairs={{0,32},{16,48},{64,96},{80,112},{128,160},{144,176},{192,224},{208... | collective-permute-start | bytes 786440 | tf_op jit(solution)/shard_map/ppermute | solution.py:231
  253.0 72.8 %all-to-all-start.3 = ((bf16[16,2,3,64,128]{4,3,2,1,0:T(8,128)(2,1)}), bf16[16,2,3,64,128]{4,3,2,1,0:T(8,128)(2,1)}, u32[]{:S(2)}, u32[]{:S(2)}) async-start(bf16[16,2,3,64,128]{4,3,2,1,0:T(8,128)(2,1)} %copy-done.7), calls=%async_computation.3 | async-start | bytes 3145728 | tf_op jit(solution)/shard_map/all_to_all | solution.py:269
  260.4 7.7 %collective-permute-start.11 = (bf16[2,8,64,128]{3,2,1,0:T(8,128)(2,1)S(1)}, bf16[2,8,64,128]{3,2,1,0:T(8,128)(2,1)S(1)}, u32[]{:S(2)}, u32[]{:S(2)}) collective-permute-start(bf16[2,8,64,128]{3,2,1,0:T(8,128)(2,1)S(1)} %bitcast.281), channel_id=1, source_target_pairs={{0,16},{16,0},{32,48},{48,32},{64,80},{80,64},{96,112},{112,96},{1... | collective-permute-start | bytes 786440 | tf_op jit(solution)/shard_map/ppermute | solution.py:226
  264.0 8.1 %collective-permute-start.12 = (bf16[2,8,64,128]{3,2,1,0:T(8,128)(2,1)S(1)}, bf16[2,8,64,128]{3,2,1,0:T(8,128)(2,1)S(1)}, u32[]{:S(2)}, u32[]{:S(2)}) collective-permute-start(bf16[2,8,64,128]{3,2,1,0:T(8,128)(2,1)S(1)} %bitcast.280), channel_id=1, source_target_pairs={{0,64},{16,80},{32,96},{48,112},{64,0},{80,16},{96,32},{112,48},{1... | collective-permute-start | bytes 786440 | tf_op jit(solution)/shard_map/ppermute | solution.py:226
  265.4 13.1 %collective-permute-start.13 = (bf16[2,8,64,128]{3,2,1,0:T(8,128)(2,1)S(1)}, bf16[2,8,64,128]{3,2,1,0:T(8,128)(2,1)S(1)}, u32[]{:S(2)}, u32[]{:S(2)}) collective-permute-start(bf16[2,8,64,128]{3,2,1,0:T(8,128)(2,1)S(1)} %bitcast.278), channel_id=1, source_target_pairs={{0,80},{16,64},{32,112},{48,96},{64,16},{80,0},{96,48},{112,32},{1... | collective-permute-start | bytes 786440 | tf_op jit(solution)/shard_map/ppermute | solution.py:226
  268.1 36.3 %copy-start.4 = (f32[4,64,16,128]{3,2,1,0:T(8,128)S(1)}, f32[4,64,16,128]{3,2,1,0:T(8,128)}, u32[]{:S(2)}) copy-start(f32[4,64,16,128]{3,2,1,0:T(8,128)} %copy-done.3) | copy-start | bytes 6291460
  268.1 17.6 %collective-permute-start.14 = (bf16[2,8,64,128]{3,2,1,0:T(8,128)(2,1)S(1)}, bf16[2,8,64,128]{3,2,1,0:T(8,128)(2,1)S(1)}, u32[]{:S(2)}, u32[]{:S(2)}) collective-permute-start(bf16[2,8,64,128]{3,2,1,0:T(8,128)(2,1)S(1)} %bitcast.279), channel_id=1, source_target_pairs={{0,128},{16,144},{32,160},{48,176},{64,192},{80,208},{96,224},{112... | collective-permute-start | bytes 786440 | tf_op jit(solution)/shard_map/ppermute | solution.py:226
  272.1 19.4 %collective-permute-start.15 = (bf16[2,8,64,128]{3,2,1,0:T(8,128)(2,1)S(1)}, bf16[2,8,64,128]{3,2,1,0:T(8,128)(2,1)S(1)}, u32[]{:S(2)}, u32[]{:S(2)}) collective-permute-start(bf16[2,8,64,128]{3,2,1,0:T(8,128)(2,1)S(1)} %bitcast.277), channel_id=1, source_target_pairs={{0,144},{16,128},{32,176},{48,160},{64,208},{80,192},{96,240},{112... | collective-permute-start | bytes 786440 | tf_op jit(solution)/shard_map/ppermute | solution.py:226
  278.5 18.9 %collective-permute-start.16 = (bf16[2,8,64,128]{3,2,1,0:T(8,128)(2,1)S(1)}, bf16[2,8,64,128]{3,2,1,0:T(8,128)(2,1)S(1)}, u32[]{:S(2)}, u32[]{:S(2)}) collective-permute-start(bf16[2,8,64,128]{3,2,1,0:T(8,128)(2,1)S(1)} %bitcast.276), channel_id=1, source_target_pairs={{0,192},{16,208},{32,224},{48,240},{64,128},{80,144},{96,160},{112... | collective-permute-start | bytes 786440 | tf_op jit(solution)/shard_map/ppermute | solution.py:226
  285.7 17.3 %collective-permute-start.17 = (bf16[2,8,64,128]{3,2,1,0:T(8,128)(2,1)S(1)}, bf16[2,8,64,128]{3,2,1,0:T(8,128)(2,1)S(1)}, u32[]{:S(2)}, u32[]{:S(2)}) collective-permute-start(bf16[2,8,64,128]{3,2,1,0:T(8,128)(2,1)S(1)} %bitcast.275), channel_id=1, source_target_pairs={{0,208},{16,192},{32,240},{48,224},{64,144},{80,128},{96,176},{112... | collective-permute-start | bytes 786440 | tf_op jit(solution)/shard_map/ppermute | solution.py:226
  306.1 6.2 %collective-permute-start.20 = (bf16[1,8,64,128]{3,2,1,0:T(8,128)(2,1)S(1)}, bf16[1,8,64,128]{3,2,1,0:T(8,128)(2,1)S(1)}, u32[]{:S(2)}, u32[]{:S(2)}) collective-permute-start(bf16[1,8,64,128]{3,2,1,0:T(8,128)(2,1)S(1)} %bitcast.288), channel_id=1, source_target_pairs={{0,16},{16,0},{32,48},{48,32},{64,80},{80,64},{96,112},{112,96},{1... | collective-permute-start | bytes 393224 | tf_op jit(solution)/shard_map/ppermute | solution.py:226
  306.5 5.9 %collective-permute-start.21 = (bf16[1,8,64,128]{3,2,1,0:T(8,128)(2,1)S(1)}, bf16[1,8,64,128]{3,2,1,0:T(8,128)(2,1)S(1)}, u32[]{:S(2)}, u32[]{:S(2)}) collective-permute-start(bf16[1,8,64,128]{3,2,1,0:T(8,128)(2,1)S(1)} %bitcast.287), channel_id=1, source_target_pairs={{0,64},{16,80},{32,96},{48,112},{64,0},{80,16},{96,32},{112,48},{1... | collective-permute-start | bytes 393224 | tf_op jit(solution)/shard_map/ppermute | solution.py:226
  306.7 8.9 %collective-permute-start.22 = (bf16[1,8,64,128]{3,2,1,0:T(8,128)(2,1)S(1)}, bf16[1,8,64,128]{3,2,1,0:T(8,128)(2,1)S(1)}, u32[]{:S(2)}, u32[]{:S(2)}) collective-permute-start(bf16[1,8,64,128]{3,2,1,0:T(8,128)(2,1)S(1)} %bitcast.286), channel_id=1, source_target_pairs={{0,80},{16,64},{32,112},{48,96},{64,16},{80,0},{96,48},{112,32},{1... | collective-permute-start | bytes 393224 | tf_op jit(solution)/shard_map/ppermute | solution.py:226
  308.6 8.2 %collective-permute-start.23 = (bf16[1,8,64,128]{3,2,1,0:T(8,128)(2,1)S(1)}, bf16[1,8,64,128]{3,2,1,0:T(8,128)(2,1)S(1)}, u32[]{:S(2)}, u32[]{:S(2)}) collective-permute-start(bf16[1,8,64,128]{3,2,1,0:T(8,128)(2,1)S(1)} %bitcast.285), channel_id=1, source_target_pairs={{0,128},{16,144},{32,160},{48,176},{64,192},{80,208},{96,224},{112... | collective-permute-start | bytes 393224 | tf_op jit(solution)/shard_map/ppermute | solution.py:226
  309.1 11.0 %collective-permute-start.24 = (bf16[1,8,64,128]{3,2,1,0:T(8,128)(2,1)S(1)}, bf16[1,8,64,128]{3,2,1,0:T(8,128)(2,1)S(1)}, u32[]{:S(2)}, u32[]{:S(2)}) collective-permute-start(bf16[1,8,64,128]{3,2,1,0:T(8,128)(2,1)S(1)} %bitcast.284), channel_id=1, source_target_pairs={{0,144},{16,128},{32,176},{48,160},{64,208},{80,192},{96,240},{112... | collective-permute-start | bytes 393224 | tf_op jit(solution)/shard_map/ppermute | solution.py:226
  312.3 10.8 %collective-permute-start.25 = (bf16[1,8,64,128]{3,2,1,0:T(8,128)(2,1)S(1)}, bf16[1,8,64,128]{3,2,1,0:T(8,128)(2,1)S(1)}, u32[]{:S(2)}, u32[]{:S(2)}) collective-permute-start(bf16[1,8,64,128]{3,2,1,0:T(8,128)(2,1)S(1)} %bitcast.283), channel_id=1, source_target_pairs={{0,192},{16,208},{32,224},{48,240},{64,128},{80,144},{96,160},{112... | collective-permute-start | bytes 393224 | tf_op jit(solution)/shard_map/ppermute | solution.py:226
  312.4 13.3 %collective-permute-start.26 = (bf16[1,8,64,128]{3,2,1,0:T(8,128)(2,1)S(1)}, bf16[1,8,64,128]{3,2,1,0:T(8,128)(2,1)S(1)}, u32[]{:S(2)}, u32[]{:S(2)}) collective-permute-start(bf16[1,8,64,128]{3,2,1,0:T(8,128)(2,1)S(1)} %bitcast.282), channel_id=1, source_target_pairs={{0,208},{16,192},{32,240},{48,224},{64,144},{80,128},{96,176},{112... | collective-permute-start | bytes 393224 | tf_op jit(solution)/shard_map/ppermute | solution.py:226
  (18 other events, 82.3 us)

commit v3 on v2

--- a/solution.py
+++ b/solution.py
@@ -81,6 +81,44 @@
     )(x)
 
 
+def stack_kernel(q_ref, k_ref, v_ref, g_ref, o_ref):
+    for i, x in enumerate((q_ref, k_ref, v_ref, g_ref)):
+        o_ref[:, i] = x[...]
+
+
+def stack_seqs(arrays, start, count, group=16):
+    _, rows, dim = arrays[0].shape
+    return pl.pallas_call(
+        stack_kernel,
+        grid=(count // group,),
+        in_specs=[pl.BlockSpec((group, rows, dim), lambda i: (i + start // group, 0, 0))] * 4,
+        out_specs=pl.BlockSpec((group, 4, rows, dim), lambda i: (i, 0, 0, 0)),
+        out_shape=jax.ShapeDtypeStruct((count, 4, rows, dim), BF16),
+        cost_estimate=pl.CostEstimate(flops=0, bytes_accessed=count * rows * dim * 16, transcendentals=0),
+        name="stack_seqs",
+    )(*arrays)
+
+
+def unstack_kernel(x_ref, *refs):
+    for i, o in enumerate(refs[-3:]):
+        o[...] = x_ref[:, i]
+
+
+def unstack_seqs(x, start, total, into=(), group=16):
+    count, _, rows, dim = x.shape
+    return pl.pallas_call(
+        unstack_kernel,
+        grid=(count // group,),
+        in_specs=[pl.BlockSpec((group, 3, rows, dim), lambda i: (i, 0, 0, 0))]
+        + [pl.BlockSpec(memory_space=pl.ANY)] * len(into),
+        out_specs=[pl.BlockSpec((group, rows, dim), lambda i: (i + start // group, 0, 0))] * 3,
+        out_shape=[jax.ShapeDtypeStruct((total, rows, dim), BF16)] * 3,
+        input_output_aliases={i + 1: i for i in range(len(into))},
+        cost_estimate=pl.CostEstimate(flops=0, bytes_accessed=count * rows * dim * 12, transcendentals=0),
+        name="unstack_seqs",
+    )(x, *into)
+
+
 def time_rows(qg_ref, rb_ref, ra_ref, part, p):
     slots, _, _, rows, dim = qg_ref.shape
     half = slots * rows
@@ -284,7 +322,7 @@
     width = seqs // CHUNKS
 
     def space_part(c):
-        x = jnp.stack([a[c * width : (c + 1) * width] for a in space], 1)
+        x = stack_seqs(space, c * width, width)
         return x.reshape(PATCH_DEVICES, width // PATCH_DEVICES, 4, rows, dim)
 
     first, second = space_part(0), space_part(1)
@@ -309,16 +347,15 @@
     db_sent, da_sent = from_side(db, 0), swap(da, ZHI_BIT)
     second, _ = after((second,), da)
     second = exchange_patches(second)
-    dkv, first = after((dkv,), first)
+    dkv, first, db_sent = lax.optimization_barrier((dkv, first, db_sent))
     dk_time, dv_time = scatter_frames(dkv, y, core)
     dq, dk_time = after((dq,), dk_time)
     dq = (dq + jnp.concatenate([db_sent[None], da_sent]).astype(F32)).astype(BF16)
     (dq_time,) = scatter_frames(dq[:, None], y, core)
     second, dq_time = after((second,), dq_time)
-    back = [x.reshape(width, 3, rows, dim) for x in (first, second)]
-
-    shape = (frames, heads, rows, dim)
-    out = [jnp.concatenate([b[:, i] for b in back]).reshape(shape) for i in range(3)]
+    out = unstack_seqs(first.reshape(width, 3, rows, dim), 0, seqs)
+    out = unstack_seqs(second.reshape(width, 3, rows, dim), width, seqs, out)
+    out = [o.reshape(frames, heads, rows, dim) for o in out]
     return (out[0], out[1], out[2], dq_time, dk_time, dv_time)
 
 

time: 331 us -> 334 us (level)
  starting transfers between devices: 85 us -> 72.4 us
  Pallas kernels: 36.8 us -> 47.1 us
  waiting for transfers between devices: 170 us -> 174 us
    ppermute x2, waiting for transfers between devices: 66.2 us -> 80.1 us  [from_side(): return lax.ppermute(x, 'frame', pairs)]
    pallas_call x0 -> x4, Pallas kernels: none -> 10.3 us  [the longest x2 5.25 us: stack_seqs(): pl.pallas_call(stack_kernel, grid=(count // group,), in_specs=[pl.BlockSp...]
    ppermute x25, waiting for transfers between devices: 88.8 us -> 81.4 us  [swap(): lax.ppermute(x, 'frame', [(i, i ^ bits) for i in range(FRAME_DEVICES)])]
    ppermute x25, starting transfers between devices: 46.7 us -> 40.2 us  [swap(): lax.ppermute(x, 'frame', [(i, i ^ bits) for i in range(FRAME_DEVICES)])]
    ppermute x2, starting transfers between devices: 9.26 us -> 2.89 us  [from_side(): return lax.ppermute(x, 'frame', pairs)]
    dynamic_update_slice x17, local copies, waits for them, and re-layouts: 0.47 us -> 4.51 us  [scatter_frames(): lax.dynamic_update_index_in_dim(o, piece[i], head, 1)]
    squeeze x2 -> x0, local copies, waits for them, and re-layouts: 3.35 us -> none  [per_device(): b[:, i]]
    unnamed x55 -> x51, local copies, waits for them, and re-layouts: 12.9 us -> 15.5 us
  transfers between devices with their start and end apart: 31 -> 31, of which waited for: 20 -> 19; matrix products, arithmetic and copies ran while one was open for 6% -> 9% of each run, Pallas kernels for 11% -> 13%
where the time goes in v3:
time: 334 us; the launch traced here: 333 us
  waiting for transfers between devices  174 us (52%)
  starting transfers between devices  72.4 us (22%)
  Pallas kernels  47.1 us (14%)
  local copies, waits for them, and re-layouts  28.4 us (9%)
  other arithmetic  9.18 us (3%)
    ppermute x25, waiting for transfers between devices, swap(): lax.ppermute(x, 'frame', [(i, i ^ bits) for i in range(FRAME_DEVICES)])  81.4 us
    ppermute x2, waiting for transfers between devices, from_side(): return lax.ppermute(x, 'frame', pairs)  80.1 us
    ppermute x25, starting transfers between devices, swap(): lax.ppermute(x, 'frame', [(i, i ^ bits) for i in range(FRAME_DEVICES)])  40.2 us
    all_to_all x4, starting transfers between devices, exchange_patches(): return lax.all_to_all(x, 'patch', split_axis=0, concat_axis=0, tiled=True)  29.3 us
    pallas_call x2, Pallas kernels, space_grads(): pl.pallas_call(functools.partial(space_kernel, block=256, scale=1.0 / mat...  22.1 us
    unnamed x51, local copies, waits for them, and re-layouts  15.5 us
    all_to_all x4, waiting for transfers between devices, exchange_patches(): return lax.all_to_all(x, 'patch', split_axis=0, concat_axis=0, tiled=True)  12.9 us
    pallas_call x1, Pallas kernels, time_grads(): pl.pallas_call(functools.partial(time_grads_kernel, scale=1.0 / math.sqrt...  8.33 us
  transfers between devices with their start and end apart: 31, of which 19 were waited for; matrix products, arithmetic and copies ran while one was open for 9% of the time, Pallas kernels for 13%

profile of v3, /device:TPU:1, one launch (start us, length us, event | category | flops | bytes accessed | tf_op | source)
XLA Modules:
  0.0 332.8 jit_solution(7914356857248615332)
XLA Ops:
  3.3 9.2 %all-to-all-start = ((bf16[16,2,4,64,128]{4,3,2,1,0:T(8,128)(2,1)}), bf16[16,2,4,64,128]{4,3,2,1,0:T(8,128)(2,1)}, u32[]{:S(2)}, u32[]{:S(2)}) async-start(bf16[16,2,4,64,128]{4,3,2,1,0:T(8,128)(2,1)} %bitcast.238), calls=%async_computation | async-start | bytes 4194304 | tf_op jit(solution)/shard_map/all_to_all | solution.py:307
  31.5 5.3 %collective-permute-done.1 = bf16[2,64,16,128]{3,2,1,0:T(8,128)(2,1)} collective-permute-done((bf16[2,64,16,128]{3,2,1,0:T(8,128)(2,1)}, bf16[2,64,16,128]{3,2,1,0:T(8,128)(2,1)}, u32[]{:S(2)}, u32[]{:S(2)}) %collective-permute-start.1) | collective-permute-done | bytes 524320 | tf_op jit(solution)/shard_map/ppermute | solution.py:264
  38.0 12.6 %collective-permute-done.2 = bf16[2,64,16,128]{3,2,1,0:T(8,128)(2,1)} collective-permute-done((bf16[2,64,16,128]{3,2,1,0:T(8,128)(2,1)}, bf16[2,64,16,128]{3,2,1,0:T(8,128)(2,1)}, u32[]{:S(2)}, u32[]{:S(2)}) %collective-permute-start.2) | collective-permute-done | bytes 524320 | tf_op jit(solution)/shard_map/ppermute | solution.py:264
  51.7 3.4 %collective-permute-done.3 = bf16[2,64,16,128]{3,2,1,0:T(8,128)(2,1)S(1)} collective-permute-done((bf16[2,64,16,128]{3,2,1,0:T(8,128)(2,1)}, bf16[2,64,16,128]{3,2,1,0:T(8,128)(2,1)S(1)}, u32[]{:S(2)}, u32[]{:S(2)}) %collective-permute-start.3) | collective-permute-done | bytes 524320 | tf_op jit(solution)/shard_map/ppermute | solution.py:264
  55.2 7.2 %all-to-all-done.x_ref = bf16[16,2,4,64,128]{4,3,2,1,0:T(8,128)(2,1)} async-done(((bf16[16,2,4,64,128]{4,3,2,1,0:T(8,128)(2,1)}), bf16[16,2,4,64,128]{4,3,2,1,0:T(8,128)(2,1)}, u32[]{:S(2)}, u32[]{:S(2)}) %all-to-all-start) | async-done | bytes 2097184 | tf_op jit(solution)/shard_map/all_to_all | solution.py:307
  62.3 4.6 %all-to-all-start.1 = ((bf16[16,2,4,64,128]{4,3,2,1,0:T(8,128)(2,1)}), bf16[16,2,4,64,128]{4,3,2,1,0:T(8,128)(2,1)}, u32[]{:S(2)}, u32[]{:S(2)}) async-start(bf16[16,2,4,64,128]{4,3,2,1,0:T(8,128)(2,1)} %bitcast.239), calls=%async_computation.1 | async-start | bytes 4194304 | tf_op jit(solution)/shard_map/all_to_all | solution.py:307
  72.1 4.2 %collective-permute-start.9 = (bf16[3,2,64,16,128]{4,3,2,1,0:T(8,128)(2,1)}, bf16[3,2,64,16,128]{4,3,2,1,0:T(8,128)(2,1)}, u32[]{:S(2)}, u32[]{:S(2)}) collective-permute-start(bf16[3,2,64,16,128]{4,3,2,1,0:T(8,128)(2,1)} %slice.85), channel_id=1, source_target_pairs={{0,32},{16,48},{32,0},{48,16},{64,96},{80,112},{96,64},{112,80},{1... | collective-permute-start | bytes 4718600 | tf_op jit(solution)/shard_map/ppermute | solution.py:264
  79.4 2.9 collective-permute-start.6
  82.3 11.1 %space_grads.2 = bf16[16,2,3,64,128]{4,3,2,1,0:T(8,128)(2,1)S(1)} custom-call(bf16[16,2,4,64,128]{4,3,2,1,0:T(8,128)(2,1)} %all-to-all-done.x_ref), custom_call_target="tpu_custom_call" | custom-call | flops 2684354560 | bytes 4194304 | tf_op jit(solution)/shard_map/space_grads/pallas_call | solution.py:69
  94.6 9.1 %collective-permute-done.6 = bf16[2,64,16,128]{3,2,1,0:T(8,128)(2,1)S(1)} collective-permute-done((bf16[2,64,16,128]{3,2,1,0:T(8,128)(2,1)S(1)}, bf16[2,64,16,128]{3,2,1,0:T(8,128)(2,1)S(1)}, u32[]{:S(2)}, u32[]{:S(2)}) %collective-permute-start.6) | collective-permute-done | bytes 524320 | tf_op jit(solution)/shard_map/ppermute | solution.py:264
  103.8 11.7 %collective-permute-done.7 = bf16[2,64,16,128]{3,2,1,0:T(8,128)(2,1)S(1)} collective-permute-done((bf16[2,64,16,128]{3,2,1,0:T(8,128)(2,1)S(1)}, bf16[2,64,16,128]{3,2,1,0:T(8,128)(2,1)S(1)}, u32[]{:S(2)}, u32[]{:S(2)}) %collective-permute-start.7) | collective-permute-done | bytes 524320 | tf_op jit(solution)/shard_map/ppermute | solution.py:264
  117.0 66.1 %collective-permute-done.8.rb_ref = bf16[2,64,16,128]{3,2,1,0:T(8,128)(2,1)S(1)} collective-permute-done((bf16[2,64,16,128]{3,2,1,0:T(8,128)(2,1)S(1)}, bf16[2,64,16,128]{3,2,1,0:T(8,128)(2,1)S(1)}, u32[]{:S(2)}, u32[]{:S(2)}) %collective-permute-start.8) | collective-permute-done | bytes 524320 | tf_op jit(solution)/shard_map/ppermute | solution.py:269
  183.1 5.8 %all-to-all-done.1.x_ref = bf16[16,2,4,64,128]{4,3,2,1,0:T(8,128)(2,1)} async-done(((bf16[16,2,4,64,128]{4,3,2,1,0:T(8,128)(2,1)}), bf16[16,2,4,64,128]{4,3,2,1,0:T(8,128)(2,1)}, u32[]{:S(2)}, u32[]{:S(2)}) %all-to-all-start.1) | async-done | bytes 2097184 | tf_op jit(solution)/shard_map/all_to_all | solution.py:307
  188.9 8.6 %all-to-all-start.3 = ((bf16[16,2,3,64,128]{4,3,2,1,0:T(8,128)(2,1)}), bf16[16,2,3,64,128]{4,3,2,1,0:T(8,128)(2,1)}, u32[]{:S(2)}, u32[]{:S(2)}) async-start(bf16[16,2,3,64,128]{4,3,2,1,0:T(8,128)(2,1)} %copy-done.8), calls=%async_computation.3 | async-start | bytes 3145728 | tf_op jit(solution)/shard_map/all_to_all | solution.py:307
  199.1 6.3 %time_stats.1.mine_ref = f32[2,64,128]{2,1,0:T(8,128)S(1)} custom-call(s32[1]{0:T(128)} %bitcast.31.side_ref, bf16[4,2,64,16,128]{4,3,2,1,0:T(8,128)(2,1)S(1)} %bitcast_dynamic-update-slice_fusion.3.qg_ref, bf16[2,64,16,128]{3,2,1,0:T(8,128)(2,1)S(1)} %collective-permute-done.8.rb_ref, bf16[3,2,64,16,128]{4,3,2,1,0:T(8,128)(2,1)} %collective-permute-done.9.ra_ref, ...), custom_call_target="tpu_custom_call" | custom-call | flops 268435456 | bytes 6291456 | tf_op jit(solution)/shard_map/time_stats/pallas_call | solution.py:217
  205.5 6.8 %collective-permute-start.10 = (f32[2,64,128]{2,1,0:T(8,128)S(1)}, f32[2,64,128]{2,1,0:T(8,128)S(1)}, u32[]{:S(2)}, u32[]{:S(2)}) collective-permute-start(f32[2,64,128]{2,1,0:T(8,128)S(1)} %time_stats.1.mine_ref), channel_id=1, source_target_pairs={{0,32},{16,48},{32,0},{48,16},{64,96},{80,112},{96,64},{112,80},{1... | collective-permute-start | bytes 196616 | tf_op jit(solution)/shard_map/ppermute | solution.py:264
  212.2 11.1 %space_grads.3 = bf16[16,2,3,64,128]{4,3,2,1,0:T(8,128)(2,1)S(1)} custom-call(bf16[16,2,4,64,128]{4,3,2,1,0:T(8,128)(2,1)} %all-to-all-done.1.x_ref), custom_call_target="tpu_custom_call" | custom-call | flops 2684354560 | bytes 4194304 | tf_op jit(solution)/shard_map/space_grads/pallas_call | solution.py:69
  224.5 7.0 %collective-permute-done.10 = f32[2,64,128]{2,1,0:T(8,128)S(1)} collective-permute-done((f32[2,64,128]{2,1,0:T(8,128)S(1)}, f32[2,64,128]{2,1,0:T(8,128)S(1)}, u32[]{:S(2)}, u32[]{:S(2)}) %collective-permute-start.10) | collective-permute-done | bytes 65568 | tf_op jit(solution)/shard_map/ppermute | solution.py:264
  231.7 8.3 %time_grads.1 = (f32[4,64,16,128]{3,2,1,0:T(8,128)S(1)}, bf16[64,16,128]{2,1,0:T(8,128)(2,1)}, bf16[3,64,16,128]{3,2,1,0:T(8,128)(2,1)S(1)}, bf16[4,2,64,16,128]{4,3,2,1,0:T(8,128)(2,1)S(1)}) custom-call(s32[1]{0:T(128)} %bitcast.31.side_ref, bf16[4,2,64,16,128]{4,3,2,1,0:T(8,128)(2,1)S(1)} %bitcast_dynamic-update-slice_fusion.3.qg_ref, ...), custom_call_target="tpu_custom_call" | custom-call | flops 671088640 | bytes 10485760 | tf_op jit(solution)/shard_map/time_grads/pallas_call | solution.py:237
  244.5 6.9 %all-to-all-start.2 = ((bf16[16,2,3,64,128]{4,3,2,1,0:T(8,128)(2,1)}), bf16[16,2,3,64,128]{4,3,2,1,0:T(8,128)(2,1)}, u32[]{:S(2)}, u32[]{:S(2)}) async-start(bf16[16,2,3,64,128]{4,3,2,1,0:T(8,128)(2,1)} %copy-done.7), calls=%async_computation.2 | async-start | bytes 3145728 | tf_op jit(solution)/shard_map/all_to_all | solution.py:307
  251.4 13.9 %collective-permute-done.11 = bf16[64,16,128]{2,1,0:T(8,128)(2,1)S(1)} collective-permute-done((bf16[64,16,128]{2,1,0:T(8,128)(2,1)}, bf16[64,16,128]{2,1,0:T(8,128)(2,1)S(1)}, u32[]{:S(2)}, u32[]{:S(2)}) %collective-permute-start.11) | collective-permute-done | bytes 262176 | tf_op jit(solution)/shard_map/ppermute | solution.py:269
  272.6 2.9 collective-permute-start.15
  281.8 2.7 collective-permute-start.17
  287.2 3.7 %collective-permute-done.15 = bf16[2,8,64,128]{3,2,1,0:T(8,128)(2,1)} collective-permute-done((bf16[2,8,64,128]{3,2,1,0:T(8,128)(2,1)}, bf16[2,8,64,128]{3,2,1,0:T(8,128)(2,1)}, u32[]{:S(2)}, u32[]{:S(2)}) %collective-permute-start.15) | collective-permute-done | bytes 262176 | tf_op jit(solution)/shard_map/ppermute | solution.py:264
  291.9 5.0 %collective-permute-done.16 = bf16[2,8,64,128]{3,2,1,0:T(8,128)(2,1)S(1)} collective-permute-done((bf16[2,8,64,128]{3,2,1,0:T(8,128)(2,1)}, bf16[2,8,64,128]{3,2,1,0:T(8,128)(2,1)S(1)}, u32[]{:S(2)}, u32[]{:S(2)}) %collective-permute-start.16) | collective-permute-done | bytes 262176 | tf_op jit(solution)/shard_map/ppermute | solution.py:264
  296.9 5.5 %collective-permute-done.17 = bf16[2,8,64,128]{3,2,1,0:T(8,128)(2,1)S(1)} collective-permute-done((bf16[2,8,64,128]{3,2,1,0:T(8,128)(2,1)}, bf16[2,8,64,128]{3,2,1,0:T(8,128)(2,1)S(1)}, u32[]{:S(2)}, u32[]{:S(2)}) %collective-permute-start.17) | collective-permute-done | bytes 262176 | tf_op jit(solution)/shard_map/ppermute | solution.py:264
  302.5 5.6 %collective-permute-done.18 = bf16[2,8,64,128]{3,2,1,0:T(8,128)(2,1)S(1)} collective-permute-done((bf16[2,8,64,128]{3,2,1,0:T(8,128)(2,1)}, bf16[2,8,64,128]{3,2,1,0:T(8,128)(2,1)S(1)}, u32[]{:S(2)}, u32[]{:S(2)}) %collective-permute-start.18) | collective-permute-done | bytes 262176 | tf_op jit(solution)/shard_map/ppermute | solution.py:264
  313.4 2.8 collective-permute-start.24
  316.7 3.2 collective-permute-start.26
  321.0 3.6 %collective-permute-done.24 = bf16[1,8,64,128]{3,2,1,0:T(8,128)(2,1)S(1)} collective-permute-done((bf16[1,8,64,128]{3,2,1,0:T(8,128)(2,1)S(1)}, bf16[1,8,64,128]{3,2,1,0:T(8,128)(2,1)S(1)}, u32[]{:S(2)}, u32[]{:S(2)}) %collective-permute-start.24) | collective-permute-done | bytes 131104 | tf_op jit(solution)/shard_map/ppermute | solution.py:264
  327.3 2.8 collective-permute-done.26
  330.1 2.7 unstack_seqs.3
  (132 shorter events, 68.8 us)
Async XLA Ops:
  3.3 59.0 %all-to-all-start = ((bf16[16,2,4,64,128]{4,3,2,1,0:T(8,128)(2,1)}), bf16[16,2,4,64,128]{4,3,2,1,0:T(8,128)(2,1)}, u32[]{:S(2)}, u32[]{:S(2)}) async-start(bf16[16,2,4,64,128]{4,3,2,1,0:T(8,128)(2,1)} %bitcast.238), calls=%async_computation | async-start | bytes 4194304 | tf_op jit(solution)/shard_map/all_to_all | solution.py:307
  15.3 3.5 %collective-permute-start = (bf16[4,2,64,8,128]{4,3,2,1,0:T(8,128)(2,1)S(1)}, bf16[4,2,64,8,128]{4,3,2,1,0:T(8,128)(2,1)}, u32[]{:S(2)}, u32[]{:S(2)}) collective-permute-start(bf16[4,2,64,8,128]{4,3,2,1,0:T(8,128)(2,1)S(1)} %dynamic-slice_bitcast_fusion.1), channel_id=1, source_target_pairs={{0,16},{16,0},{32,48},{48,32},{64,80},{80,64},{96,112},{112,96},{1... | collective-permute-start | bytes 3145736 | tf_op jit(solution)/shard_map/ppermute | solution.py:264
  23.4 13.5 %collective-permute-start.1 = (bf16[2,64,16,128]{3,2,1,0:T(8,128)(2,1)}, bf16[2,64,16,128]{3,2,1,0:T(8,128)(2,1)}, u32[]{:S(2)}, u32[]{:S(2)}) collective-permute-start(bf16[2,64,16,128]{3,2,1,0:T(8,128)(2,1)} %get-tuple-element.82), channel_id=1, source_target_pairs={{0,64},{16,80},{32,96},{48,112},{64,0},{80,16},{96,32},{112,48},{1... | collective-permute-start | bytes 1572872 | tf_op jit(solution)/shard_map/ppermute | solution.py:264
  24.7 25.9 %collective-permute-start.2 = (bf16[2,64,16,128]{3,2,1,0:T(8,128)(2,1)}, bf16[2,64,16,128]{3,2,1,0:T(8,128)(2,1)}, u32[]{:S(2)}, u32[]{:S(2)}) collective-permute-start(bf16[2,64,16,128]{3,2,1,0:T(8,128)(2,1)} %get-tuple-element.83), channel_id=1, source_target_pairs={{0,128},{16,144},{32,160},{48,176},{64,192},{80,208},{96,224},{112... | collective-permute-start | bytes 1572872 | tf_op jit(solution)/shard_map/ppermute | solution.py:264
  29.9 25.1 %collective-permute-start.3 = (bf16[2,64,16,128]{3,2,1,0:T(8,128)(2,1)}, bf16[2,64,16,128]{3,2,1,0:T(8,128)(2,1)S(1)}, u32[]{:S(2)}, u32[]{:S(2)}) collective-permute-start(bf16[2,64,16,128]{3,2,1,0:T(8,128)(2,1)} %get-tuple-element.81), channel_id=1, source_target_pairs={{0,192},{16,208},{32,224},{48,240},{64,128},{80,144},{96,160},{112... | collective-permute-start | bytes 1572872 | tf_op jit(solution)/shard_map/ppermute | solution.py:264
  62.3 126.5 %all-to-all-start.1 = ((bf16[16,2,4,64,128]{4,3,2,1,0:T(8,128)(2,1)}), bf16[16,2,4,64,128]{4,3,2,1,0:T(8,128)(2,1)}, u32[]{:S(2)}, u32[]{:S(2)}) async-start(bf16[16,2,4,64,128]{4,3,2,1,0:T(8,128)(2,1)} %bitcast.239), calls=%async_computation.1 | async-start | bytes 4194304 | tf_op jit(solution)/shard_map/all_to_all | solution.py:307
  69.0 7.3 %collective-permute-start.4 = (bf16[4,2,64,8,128]{4,3,2,1,0:T(8,128)(2,1)S(1)}, bf16[4,2,64,8,128]{4,3,2,1,0:T(8,128)(2,1)S(1)}, u32[]{:S(2)}, u32[]{:S(2)}) collective-permute-start(bf16[4,2,64,8,128]{4,3,2,1,0:T(8,128)(2,1)S(1)} %dynamic-slice_bitcast_fusion), channel_id=1, source_target_pairs={{0,16},{16,0},{32,48},{48,32},{64,80},{80,64},{96,112},{112,96},{1... | collective-permute-start | bytes 3145736 | tf_op jit(solution)/shard_map/ppermute | solution.py:264
  72.1 116.8 %collective-permute-start.9 = (bf16[3,2,64,16,128]{4,3,2,1,0:T(8,128)(2,1)}, bf16[3,2,64,16,128]{4,3,2,1,0:T(8,128)(2,1)}, u32[]{:S(2)}, u32[]{:S(2)}) collective-permute-start(bf16[3,2,64,16,128]{4,3,2,1,0:T(8,128)(2,1)} %slice.85), channel_id=1, source_target_pairs={{0,32},{16,48},{32,0},{48,16},{64,96},{80,112},{96,64},{112,80},{1... | collective-permute-start | bytes 4718600 | tf_op jit(solution)/shard_map/ppermute | solution.py:264
  76.7 17.8 %collective-permute-start.5 = (bf16[2,64,16,128]{3,2,1,0:T(8,128)(2,1)S(1)}, bf16[2,64,16,128]{3,2,1,0:T(8,128)(2,1)S(1)}, u32[]{:S(2)}, u32[]{:S(2)}) collective-permute-start(bf16[2,64,16,128]{3,2,1,0:T(8,128)(2,1)S(1)} %get-tuple-element.79), channel_id=1, source_target_pairs={{0,64},{16,80},{32,96},{48,112},{64,0},{80,16},{96,32},{112,48},{1... | collective-permute-start | bytes 1572872 | tf_op jit(solution)/shard_map/ppermute | solution.py:264
  78.1 105.0 %collective-permute-start.8 = (bf16[2,64,16,128]{3,2,1,0:T(8,128)(2,1)S(1)}, bf16[2,64,16,128]{3,2,1,0:T(8,128)(2,1)S(1)}, u32[]{:S(2)}, u32[]{:S(2)}) collective-permute-start(bf16[2,64,16,128]{3,2,1,0:T(8,128)(2,1)S(1)} %slice_bitcast_fusion), channel_id=1, source_target_pairs={{32,0},{48,16},{96,64},{112,80},{160,128},{176,144},{224,192},{240... | collective-permute-start | bytes 1572872 | tf_op jit(solution)/shard_map/ppermute | solution.py:269
  79.4 24.3 %collective-permute-start.6 = (bf16[2,64,16,128]{3,2,1,0:T(8,128)(2,1)S(1)}, bf16[2,64,16,128]{3,2,1,0:T(8,128)(2,1)S(1)}, u32[]{:S(2)}, u32[]{:S(2)}) collective-permute-start(bf16[2,64,16,128]{3,2,1,0:T(8,128)(2,1)S(1)} %get-tuple-element.80), channel_id=1, source_target_pairs={{0,128},{16,144},{32,160},{48,176},{64,192},{80,208},{96,224},{112... | collective-permute-start | bytes 1572872 | tf_op jit(solution)/shard_map/ppermute | solution.py:264
  93.4 22.2 %collective-permute-start.7 = (bf16[2,64,16,128]{3,2,1,0:T(8,128)(2,1)S(1)}, bf16[2,64,16,128]{3,2,1,0:T(8,128)(2,1)S(1)}, u32[]{:S(2)}, u32[]{:S(2)}) collective-permute-start(bf16[2,64,16,128]{3,2,1,0:T(8,128)(2,1)S(1)} %get-tuple-element.78), channel_id=1, source_target_pairs={{0,192},{16,208},{32,224},{48,240},{64,128},{80,144},{96,160},{112... | collective-permute-start | bytes 1572872 | tf_op jit(solution)/shard_map/ppermute | solution.py:264
  188.9 55.6 %all-to-all-start.3 = ((bf16[16,2,3,64,128]{4,3,2,1,0:T(8,128)(2,1)}), bf16[16,2,3,64,128]{4,3,2,1,0:T(8,128)(2,1)}, u32[]{:S(2)}, u32[]{:S(2)}) async-start(bf16[16,2,3,64,128]{4,3,2,1,0:T(8,128)(2,1)} %copy-done.8), calls=%async_computation.3 | async-start | bytes 3145728 | tf_op jit(solution)/shard_map/all_to_all | solution.py:307
  205.5 26.0 %collective-permute-start.10 = (f32[2,64,128]{2,1,0:T(8,128)S(1)}, f32[2,64,128]{2,1,0:T(8,128)S(1)}, u32[]{:S(2)}, u32[]{:S(2)}) collective-permute-start(f32[2,64,128]{2,1,0:T(8,128)S(1)} %time_stats.1.mine_ref), channel_id=1, source_target_pairs={{0,32},{16,48},{32,0},{48,16},{64,96},{80,112},{96,64},{112,80},{1... | collective-permute-start | bytes 196616 | tf_op jit(solution)/shard_map/ppermute | solution.py:264
  242.7 22.6 %collective-permute-start.11 = (bf16[64,16,128]{2,1,0:T(8,128)(2,1)}, bf16[64,16,128]{2,1,0:T(8,128)(2,1)S(1)}, u32[]{:S(2)}, u32[]{:S(2)}) collective-permute-start(bf16[64,16,128]{2,1,0:T(8,128)(2,1)} %get-tuple-element.52), channel_id=1, source_target_pairs={{0,32},{16,48},{64,96},{80,112},{128,160},{144,176},{192,224},{208... | collective-permute-start | bytes 786440 | tf_op jit(solution)/shard_map/ppermute | solution.py:269
  244.4 63.8 %collective-permute-start.19 = (bf16[3,64,16,128]{3,2,1,0:T(8,128)(2,1)S(1)}, bf16[3,64,16,128]{3,2,1,0:T(8,128)(2,1)}, u32[]{:S(2)}, u32[]{:S(2)}) collective-permute-start(bf16[3,64,16,128]{3,2,1,0:T(8,128)(2,1)S(1)} %get-tuple-element.46), channel_id=1, source_target_pairs={{0,32},{16,48},{32,0},{48,16},{64,96},{80,112},{96,64},{112,80},{1... | collective-permute-start | bytes 2359304 | tf_op jit(solution)/shard_map/ppermute | solution.py:264
  244.5 85.6 %all-to-all-start.2 = ((bf16[16,2,3,64,128]{4,3,2,1,0:T(8,128)(2,1)}), bf16[16,2,3,64,128]{4,3,2,1,0:T(8,128)(2,1)}, u32[]{:S(2)}, u32[]{:S(2)}) async-start(bf16[16,2,3,64,128]{4,3,2,1,0:T(8,128)(2,1)} %copy-done.7), calls=%async_computation.2 | async-start | bytes 3145728 | tf_op jit(solution)/shard_map/all_to_all | solution.py:307
  267.2 12.9 %collective-permute-start.12 = (bf16[2,8,64,128]{3,2,1,0:T(8,128)(2,1)}, bf16[2,8,64,128]{3,2,1,0:T(8,128)(2,1)}, u32[]{:S(2)}, u32[]{:S(2)}) collective-permute-start(bf16[2,8,64,128]{3,2,1,0:T(8,128)(2,1)} %bitcast.228), channel_id=1, source_target_pairs={{0,16},{16,0},{32,48},{48,32},{64,80},{80,64},{96,112},{112,96},{1... | collective-permute-start | bytes 786440 | tf_op jit(solution)/shard_map/ppermute | solution.py:264
  268.9 12.9 %collective-permute-start.13 = (bf16[2,8,64,128]{3,2,1,0:T(8,128)(2,1)}, bf16[2,8,64,128]{3,2,1,0:T(8,128)(2,1)}, u32[]{:S(2)}, u32[]{:S(2)}) collective-permute-start(bf16[2,8,64,128]{3,2,1,0:T(8,128)(2,1)} %bitcast.227), channel_id=1, source_target_pairs={{0,64},{16,80},{32,96},{48,112},{64,0},{80,16},{96,32},{112,48},{1... | collective-permute-start | bytes 786440 | tf_op jit(solution)/shard_map/ppermute | solution.py:264
  271.5 14.0 %collective-permute-start.14 = (bf16[2,8,64,128]{3,2,1,0:T(8,128)(2,1)}, bf16[2,8,64,128]{3,2,1,0:T(8,128)(2,1)}, u32[]{:S(2)}, u32[]{:S(2)}) collective-permute-start(bf16[2,8,64,128]{3,2,1,0:T(8,128)(2,1)} %bitcast.226), channel_id=1, source_target_pairs={{0,80},{16,64},{32,112},{48,96},{64,16},{80,0},{96,48},{112,32},{1... | collective-permute-start | bytes 786440 | tf_op jit(solution)/shard_map/ppermute | solution.py:264
  272.6 18.3 %collective-permute-start.15 = (bf16[2,8,64,128]{3,2,1,0:T(8,128)(2,1)}, bf16[2,8,64,128]{3,2,1,0:T(8,128)(2,1)}, u32[]{:S(2)}, u32[]{:S(2)}) collective-permute-start(bf16[2,8,64,128]{3,2,1,0:T(8,128)(2,1)} %bitcast.225), channel_id=1, source_target_pairs={{0,128},{16,144},{32,160},{48,176},{64,192},{80,208},{96,224},{112... | collective-permute-start | bytes 786440 | tf_op jit(solution)/shard_map/ppermute | solution.py:264
  280.1 28.1 %copy-start.16 = (bf16[64,16,128]{2,1,0:T(8,128)(2,1)S(1)}, bf16[64,16,128]{2,1,0:T(8,128)(2,1)}, u32[]{:S(2)}) copy-start(bf16[64,16,128]{2,1,0:T(8,128)(2,1)} %copy-done.15) | copy-start | bytes 786436
  280.1 16.8 %collective-permute-start.16 = (bf16[2,8,64,128]{3,2,1,0:T(8,128)(2,1)}, bf16[2,8,64,128]{3,2,1,0:T(8,128)(2,1)S(1)}, u32[]{:S(2)}, u32[]{:S(2)}) collective-permute-start(bf16[2,8,64,128]{3,2,1,0:T(8,128)(2,1)} %bitcast.260), channel_id=1, source_target_pairs={{0,144},{16,128},{32,176},{48,160},{64,208},{80,192},{96,240},{112... | collective-permute-start | bytes 786440 | tf_op jit(solution)/shard_map/ppermute | solution.py:264
  281.8 20.6 %collective-permute-start.17 = (bf16[2,8,64,128]{3,2,1,0:T(8,128)(2,1)}, bf16[2,8,64,128]{3,2,1,0:T(8,128)(2,1)S(1)}, u32[]{:S(2)}, u32[]{:S(2)}) collective-permute-start(bf16[2,8,64,128]{3,2,1,0:T(8,128)(2,1)} %bitcast.259), channel_id=1, source_target_pairs={{0,192},{16,208},{32,224},{48,240},{64,128},{80,144},{96,160},{112... | collective-permute-start | bytes 786440 | tf_op jit(solution)/shard_map/ppermute | solution.py:264
  285.5 22.6 %collective-permute-start.18 = (bf16[2,8,64,128]{3,2,1,0:T(8,128)(2,1)}, bf16[2,8,64,128]{3,2,1,0:T(8,128)(2,1)S(1)}, u32[]{:S(2)}, u32[]{:S(2)}) collective-permute-start(bf16[2,8,64,128]{3,2,1,0:T(8,128)(2,1)} %bitcast.258), channel_id=1, source_target_pairs={{0,208},{16,192},{32,240},{48,224},{64,144},{80,128},{96,176},{112... | collective-permute-start | bytes 786440 | tf_op jit(solution)/shard_map/ppermute | solution.py:264
  310.5 6.1 %collective-permute-start.20 = (bf16[1,8,64,128]{3,2,1,0:T(8,128)(2,1)S(1)}, bf16[1,8,64,128]{3,2,1,0:T(8,128)(2,1)S(1)}, u32[]{:S(2)}, u32[]{:S(2)}) collective-permute-start(bf16[1,8,64,128]{3,2,1,0:T(8,128)(2,1)S(1)} %bitcast.267), channel_id=1, source_target_pairs={{0,16},{16,0},{32,48},{48,32},{64,80},{80,64},{96,112},{112,96},{1... | collective-permute-start | bytes 393224 | tf_op jit(solution)/shard_map/ppermute | solution.py:264
  310.8 5.9 %collective-permute-start.21 = (bf16[1,8,64,128]{3,2,1,0:T(8,128)(2,1)S(1)}, bf16[1,8,64,128]{3,2,1,0:T(8,128)(2,1)S(1)}, u32[]{:S(2)}, u32[]{:S(2)}) collective-permute-start(bf16[1,8,64,128]{3,2,1,0:T(8,128)(2,1)S(1)} %bitcast.266), channel_id=1, source_target_pairs={{0,64},{16,80},{32,96},{48,112},{64,0},{80,16},{96,32},{112,48},{1... | collective-permute-start | bytes 393224 | tf_op jit(solution)/shard_map/ppermute | solution.py:264
  311.0 9.0 %collective-permute-start.22 = (bf16[1,8,64,128]{3,2,1,0:T(8,128)(2,1)S(1)}, bf16[1,8,64,128]{3,2,1,0:T(8,128)(2,1)S(1)}, u32[]{:S(2)}, u32[]{:S(2)}) collective-permute-start(bf16[1,8,64,128]{3,2,1,0:T(8,128)(2,1)S(1)} %bitcast.265), channel_id=1, source_target_pairs={{0,80},{16,64},{32,112},{48,96},{64,16},{80,0},{96,48},{112,32},{1... | collective-permute-start | bytes 393224 | tf_op jit(solution)/shard_map/ppermute | solution.py:264
  313.0 8.1 %collective-permute-start.23 = (bf16[1,8,64,128]{3,2,1,0:T(8,128)(2,1)S(1)}, bf16[1,8,64,128]{3,2,1,0:T(8,128)(2,1)S(1)}, u32[]{:S(2)}, u32[]{:S(2)}) collective-permute-start(bf16[1,8,64,128]{3,2,1,0:T(8,128)(2,1)S(1)} %bitcast.264), channel_id=1, source_target_pairs={{0,128},{16,144},{32,160},{48,176},{64,192},{80,208},{96,224},{112... | collective-permute-start | bytes 393224 | tf_op jit(solution)/shard_map/ppermute | solution.py:264
  313.4 11.3 %collective-permute-start.24 = (bf16[1,8,64,128]{3,2,1,0:T(8,128)(2,1)S(1)}, bf16[1,8,64,128]{3,2,1,0:T(8,128)(2,1)S(1)}, u32[]{:S(2)}, u32[]{:S(2)}) collective-permute-start(bf16[1,8,64,128]{3,2,1,0:T(8,128)(2,1)S(1)} %bitcast.263), channel_id=1, source_target_pairs={{0,144},{16,128},{32,176},{48,160},{64,208},{80,192},{96,240},{112... | collective-permute-start | bytes 393224 | tf_op jit(solution)/shard_map/ppermute | solution.py:264
  316.6 10.7 %collective-permute-start.25 = (bf16[1,8,64,128]{3,2,1,0:T(8,128)(2,1)S(1)}, bf16[1,8,64,128]{3,2,1,0:T(8,128)(2,1)S(1)}, u32[]{:S(2)}, u32[]{:S(2)}) collective-permute-start(bf16[1,8,64,128]{3,2,1,0:T(8,128)(2,1)S(1)} %bitcast.262), channel_id=1, source_target_pairs={{0,192},{16,208},{32,224},{48,240},{64,128},{80,144},{96,160},{112... | collective-permute-start | bytes 393224 | tf_op jit(solution)/shard_map/ppermute | solution.py:264
  316.7 13.3 %collective-permute-start.26 = (bf16[1,8,64,128]{3,2,1,0:T(8,128)(2,1)S(1)}, bf16[1,8,64,128]{3,2,1,0:T(8,128)(2,1)S(1)}, u32[]{:S(2)}, u32[]{:S(2)}) collective-permute-start(bf16[1,8,64,128]{3,2,1,0:T(8,128)(2,1)S(1)} %bitcast.261), channel_id=1, source_target_pairs={{0,208},{16,192},{32,240},{48,224},{64,144},{80,128},{96,176},{112... | collective-permute-start | bytes 393224 | tf_op jit(solution)/shard_map/ppermute | solution.py:264
  (16 other events, 108.2 us)

commit v4 on v3

--- a/solution.py
+++ b/solution.py
@@ -293,13 +293,12 @@
     slots, n, count, rows, dim = u.shape
     t = jnp.transpose(u.reshape(slots, n, count, 2, rows // 2, dim), (0, 3, 1, 4, 2, 5))
     out = [jnp.zeros((rows // 2, 2 * slots, count, dim), u.dtype) for _ in range(n)]
-    for j in range(slots):
-        for c in range(2):
-            piece = pick(pick(t, y ^ j), core ^ c)
-            if j or c:
-                piece = swap(piece, j * Y_BIT + c * CORE_BIT)
-            head = (core ^ c) * slots + (y ^ j)
-            out = [lax.dynamic_update_index_in_dim(o, piece[i], head, 1) for i, o in enumerate(out)]
+    for j, c in ((0, 0), (1, 0), (3, 0), (2, 0), (1, 1), (3, 1), (2, 1), (0, 1)):
+        piece = pick(pick(t, y ^ j), core ^ c)
+        if j or c:
+            piece = swap(piece, j * Y_BIT + c * CORE_BIT)
+        head = (core ^ c) * slots + (y ^ j)
+        out = [lax.dynamic_update_index_in_dim(o, piece[i], head, 1) for i, o in enumerate(out)]
     return out
 
 
@@ -347,7 +346,7 @@
     db_sent, da_sent = from_side(db, 0), swap(da, ZHI_BIT)
     second, _ = after((second,), da)
     second = exchange_patches(second)
-    dkv, first, db_sent = lax.optimization_barrier((dkv, first, db_sent))
+    dkv, first = after((dkv,), first)
     dk_time, dv_time = scatter_frames(dkv, y, core)
     dq, dk_time = after((dq,), dk_time)
     dq = (dq + jnp.concatenate([db_sent[None], da_sent]).astype(F32)).astype(BF16)

time: 334 us -> 326 us (0.976)
  waiting for transfers between devices: 174 us -> 160 us
  starting transfers between devices: 72.4 us -> 82.3 us
    ppermute x25, waiting for transfers between devices: 81.4 us -> 66.8 us  [swap(): lax.ppermute(x, 'frame', [(i, i ^ bits) for i in range(FRAME_DEVICES)])]
    ppermute x2, waiting for transfers between devices: 80.1 us -> 66.2 us  [from_side(): return lax.ppermute(x, 'frame', pairs)]
    all_to_all x4, waiting for transfers between devices: 12.9 us -> 26.8 us  [exchange_patches(): return lax.all_to_all(x, 'patch', split_axis=0, concat_axis=0, tiled=True)]
    ppermute x2, starting transfers between devices: 2.89 us -> 9.26 us  [from_side(): return lax.ppermute(x, 'frame', pairs)]
    ppermute x25, starting transfers between devices: 40.2 us -> 43.7 us  [swap(): lax.ppermute(x, 'frame', [(i, i ^ bits) for i in range(FRAME_DEVICES)])]
    unnamed x51 -> x49, local copies, waits for them, and re-layouts: 15.5 us -> 15.8 us
  transfers between devices with their start and end apart: 31 -> 31, of which waited for: 19 -> 16; matrix products, arithmetic and copies ran while one was open for 9% -> 8% of each run, Pallas kernels for 13% -> 13%
where the time goes in v4:
time: 326 us; the launch traced here: 325 us
  waiting for transfers between devices  160 us (49%)
  starting transfers between devices  82.3 us (25%)
  Pallas kernels  46.7 us (14%)
  local copies, waits for them, and re-layouts  27.5 us (8%)
  other arithmetic  7.3 us (2%)
    ppermute x25, waiting for transfers between devices, swap(): lax.ppermute(x, 'frame', [(i, i ^ bits) for i in range(FRAME_DEVICES)])  66.8 us
    ppermute x2, waiting for transfers between devices, from_side(): return lax.ppermute(x, 'frame', pairs)  66.2 us
    ppermute x25, starting transfers between devices, swap(): lax.ppermute(x, 'frame', [(i, i ^ bits) for i in range(FRAME_DEVICES)])  43.7 us
    all_to_all x4, starting transfers between devices, exchange_patches(): return lax.all_to_all(x, 'patch', split_axis=0, concat_axis=0, tiled=True)  29.3 us
    all_to_all x4, waiting for transfers between devices, exchange_patches(): return lax.all_to_all(x, 'patch', split_axis=0, concat_axis=0, tiled=True)  26.8 us
    pallas_call x2, Pallas kernels, space_grads(): pl.pallas_call(functools.partial(space_kernel, block=256, scale=1.0 / mat...  22.1 us
    unnamed x49, local copies, waits for them, and re-layouts  15.8 us
    ppermute x2, starting transfers between devices, from_side(): return lax.ppermute(x, 'frame', pairs)  9.26 us
  transfers between devices with their start and end apart: 31, of which 16 were waited for; matrix products, arithmetic and copies ran while one was open for 8% of the time, Pallas kernels for 13%

profile of v4, /device:TPU:1, one launch (start us, length us, event | category | flops | bytes accessed | tf_op | source)
XLA Modules:
  0.0 324.9 jit_solution(15526162874037053169)
XLA Ops:
  0.6 2.6 stack_seqs.2
  3.3 9.2 %all-to-all-start = ((bf16[16,2,4,64,128]{4,3,2,1,0:T(8,128)(2,1)}), bf16[16,2,4,64,128]{4,3,2,1,0:T(8,128)(2,1)}, u32[]{:S(2)}, u32[]{:S(2)}) async-start(bf16[16,2,4,64,128]{4,3,2,1,0:T(8,128)(2,1)} %bitcast.238), calls=%async_computation | async-start | bytes 4194304 | tf_op jit(solution)/shard_map/all_to_all | solution.py:306
  16.3 2.4 collective-permute-done
  23.6 2.6 collective-permute-start.2
  26.2 2.6 stack_seqs.3
  30.4 5.3 %collective-permute-done.1 = bf16[2,64,16,128]{3,2,1,0:T(8,128)(2,1)} collective-permute-done((bf16[2,64,16,128]{3,2,1,0:T(8,128)(2,1)}, bf16[2,64,16,128]{3,2,1,0:T(8,128)(2,1)}, u32[]{:S(2)}, u32[]{:S(2)}) %collective-permute-start.1) | collective-permute-done | bytes 524320 | tf_op jit(solution)/shard_map/ppermute | solution.py:264
  36.9 12.6 %collective-permute-done.2 = bf16[2,64,16,128]{3,2,1,0:T(8,128)(2,1)} collective-permute-done((bf16[2,64,16,128]{3,2,1,0:T(8,128)(2,1)}, bf16[2,64,16,128]{3,2,1,0:T(8,128)(2,1)}, u32[]{:S(2)}, u32[]{:S(2)}) %collective-permute-start.2) | collective-permute-done | bytes 524320 | tf_op jit(solution)/shard_map/ppermute | solution.py:264
  50.6 3.4 %collective-permute-done.3 = bf16[2,64,16,128]{3,2,1,0:T(8,128)(2,1)S(1)} collective-permute-done((bf16[2,64,16,128]{3,2,1,0:T(8,128)(2,1)}, bf16[2,64,16,128]{3,2,1,0:T(8,128)(2,1)S(1)}, u32[]{:S(2)}, u32[]{:S(2)}) %collective-permute-start.3) | collective-permute-done | bytes 524320 | tf_op jit(solution)/shard_map/ppermute | solution.py:264
  54.0 8.3 %all-to-all-done.x_ref = bf16[16,2,4,64,128]{4,3,2,1,0:T(8,128)(2,1)} async-done(((bf16[16,2,4,64,128]{4,3,2,1,0:T(8,128)(2,1)}), bf16[16,2,4,64,128]{4,3,2,1,0:T(8,128)(2,1)}, u32[]{:S(2)}, u32[]{:S(2)}) %all-to-all-start) | async-done | bytes 2097184 | tf_op jit(solution)/shard_map/all_to_all | solution.py:306
  62.3 4.6 %all-to-all-start.1 = ((bf16[16,2,4,64,128]{4,3,2,1,0:T(8,128)(2,1)}), bf16[16,2,4,64,128]{4,3,2,1,0:T(8,128)(2,1)}, u32[]{:S(2)}, u32[]{:S(2)}) async-start(bf16[16,2,4,64,128]{4,3,2,1,0:T(8,128)(2,1)} %bitcast.239), calls=%async_computation.1 | async-start | bytes 4194304 | tf_op jit(solution)/shard_map/all_to_all | solution.py:306
  72.0 4.2 %collective-permute-start.9 = (bf16[3,2,64,16,128]{4,3,2,1,0:T(8,128)(2,1)}, bf16[3,2,64,16,128]{4,3,2,1,0:T(8,128)(2,1)}, u32[]{:S(2)}, u32[]{:S(2)}) collective-permute-start(bf16[3,2,64,16,128]{4,3,2,1,0:T(8,128)(2,1)} %slice.85), channel_id=1, source_target_pairs={{0,32},{16,48},{32,0},{48,16},{64,96},{80,112},{96,64},{112,80},{1... | collective-permute-start | bytes 4718600 | tf_op jit(solution)/shard_map/ppermute | solution.py:264
  79.4 2.9 collective-permute-start.6
  82.3 11.1 %space_grads.2 = bf16[16,2,3,64,128]{4,3,2,1,0:T(8,128)(2,1)S(1)} custom-call(bf16[16,2,4,64,128]{4,3,2,1,0:T(8,128)(2,1)} %all-to-all-done.x_ref), custom_call_target="tpu_custom_call" | custom-call | flops 2684354560 | bytes 4194304 | tf_op jit(solution)/shard_map/space_grads/pallas_call | solution.py:69
  94.6 9.1 %collective-permute-done.6 = bf16[2,64,16,128]{3,2,1,0:T(8,128)(2,1)S(1)} collective-permute-done((bf16[2,64,16,128]{3,2,1,0:T(8,128)(2,1)S(1)}, bf16[2,64,16,128]{3,2,1,0:T(8,128)(2,1)S(1)}, u32[]{:S(2)}, u32[]{:S(2)}) %collective-permute-start.6) | collective-permute-done | bytes 524320 | tf_op jit(solution)/shard_map/ppermute | solution.py:264
  103.8 11.7 %collective-permute-done.7 = bf16[2,64,16,128]{3,2,1,0:T(8,128)(2,1)S(1)} collective-permute-done((bf16[2,64,16,128]{3,2,1,0:T(8,128)(2,1)S(1)}, bf16[2,64,16,128]{3,2,1,0:T(8,128)(2,1)S(1)}, u32[]{:S(2)}, u32[]{:S(2)}) %collective-permute-start.7) | collective-permute-done | bytes 524320 | tf_op jit(solution)/shard_map/ppermute | solution.py:264
  116.9 66.2 %collective-permute-done.8.rb_ref = bf16[2,64,16,128]{3,2,1,0:T(8,128)(2,1)S(1)} collective-permute-done((bf16[2,64,16,128]{3,2,1,0:T(8,128)(2,1)S(1)}, bf16[2,64,16,128]{3,2,1,0:T(8,128)(2,1)S(1)}, u32[]{:S(2)}, u32[]{:S(2)}) %collective-permute-start.8) | collective-permute-done | bytes 524320 | tf_op jit(solution)/shard_map/ppermute | solution.py:269
  183.1 5.8 %all-to-all-done.1.x_ref = bf16[16,2,4,64,128]{4,3,2,1,0:T(8,128)(2,1)} async-done(((bf16[16,2,4,64,128]{4,3,2,1,0:T(8,128)(2,1)}), bf16[16,2,4,64,128]{4,3,2,1,0:T(8,128)(2,1)}, u32[]{:S(2)}, u32[]{:S(2)}) %all-to-all-start.1) | async-done | bytes 2097184 | tf_op jit(solution)/shard_map/all_to_all | solution.py:306
  188.9 8.6 %all-to-all-start.3 = ((bf16[16,2,3,64,128]{4,3,2,1,0:T(8,128)(2,1)}), bf16[16,2,3,64,128]{4,3,2,1,0:T(8,128)(2,1)}, u32[]{:S(2)}, u32[]{:S(2)}) async-start(bf16[16,2,3,64,128]{4,3,2,1,0:T(8,128)(2,1)} %copy-done.8), calls=%async_computation.3 | async-start | bytes 3145728 | tf_op jit(solution)/shard_map/all_to_all | solution.py:306
  199.2 6.3 %time_stats.1.mine_ref = f32[2,64,128]{2,1,0:T(8,128)S(1)} custom-call(s32[1]{0:T(128)} %bitcast.31.side_ref, bf16[4,2,64,16,128]{4,3,2,1,0:T(8,128)(2,1)S(1)} %bitcast_dynamic-update-slice_fusion.3.qg_ref, bf16[2,64,16,128]{3,2,1,0:T(8,128)(2,1)S(1)} %collective-permute-done.8.rb_ref, bf16[3,2,64,16,128]{4,3,2,1,0:T(8,128)(2,1)} %collective-permute-done.9.ra_ref, ...), custom_call_target="tpu_custom_call" | custom-call | flops 268435456 | bytes 6291456 | tf_op jit(solution)/shard_map/time_stats/pallas_call | solution.py:217
  205.6 6.8 %collective-permute-start.10 = (f32[2,64,128]{2,1,0:T(8,128)S(1)}, f32[2,64,128]{2,1,0:T(8,128)S(1)}, u32[]{:S(2)}, u32[]{:S(2)}) collective-permute-start(f32[2,64,128]{2,1,0:T(8,128)S(1)} %time_stats.1.mine_ref), channel_id=1, source_target_pairs={{0,32},{16,48},{32,0},{48,16},{64,96},{80,112},{96,64},{112,80},{1... | collective-permute-start | bytes 196616 | tf_op jit(solution)/shard_map/ppermute | solution.py:264
  212.3 11.1 %space_grads.3 = bf16[16,2,3,64,128]{4,3,2,1,0:T(8,128)(2,1)S(1)} custom-call(bf16[16,2,4,64,128]{4,3,2,1,0:T(8,128)(2,1)} %all-to-all-done.1.x_ref), custom_call_target="tpu_custom_call" | custom-call | flops 2684354560 | bytes 4194304 | tf_op jit(solution)/shard_map/space_grads/pallas_call | solution.py:69
  224.6 6.9 %collective-permute-done.10 = f32[2,64,128]{2,1,0:T(8,128)S(1)} collective-permute-done((f32[2,64,128]{2,1,0:T(8,128)S(1)}, f32[2,64,128]{2,1,0:T(8,128)S(1)}, u32[]{:S(2)}, u32[]{:S(2)}) %collective-permute-start.10) | collective-permute-done | bytes 65568 | tf_op jit(solution)/shard_map/ppermute | solution.py:264
  231.7 8.3 %time_grads.1 = (f32[4,64,16,128]{3,2,1,0:T(8,128)S(1)}, bf16[64,16,128]{2,1,0:T(8,128)(2,1)}, bf16[3,64,16,128]{3,2,1,0:T(8,128)(2,1)S(1)}, bf16[4,2,64,16,128]{4,3,2,1,0:T(8,128)(2,1)S(1)}) custom-call(s32[1]{0:T(128)} %bitcast.31.side_ref, bf16[4,2,64,16,128]{4,3,2,1,0:T(8,128)(2,1)S(1)} %bitcast_dynamic-update-slice_fusion.3.qg_ref, ...), custom_call_target="tpu_custom_call" | custom-call | flops 671088640 | bytes 10485760 | tf_op jit(solution)/shard_map/time_grads/pallas_call | solution.py:237
  242.7 8.0 %collective-permute-start.18 = (bf16[64,16,128]{2,1,0:T(8,128)(2,1)}, bf16[64,16,128]{2,1,0:T(8,128)(2,1)}, u32[]{:S(2)}, u32[]{:S(2)}) collective-permute-start(bf16[64,16,128]{2,1,0:T(8,128)(2,1)} %get-tuple-element.53), channel_id=1, source_target_pairs={{0,32},{16,48},{64,96},{80,112},{128,160},{144,176},{192,224},{208... | collective-permute-start | bytes 786440 | tf_op jit(solution)/shard_map/ppermute | solution.py:269
  250.7 6.9 %all-to-all-start.2 = ((bf16[16,2,3,64,128]{4,3,2,1,0:T(8,128)(2,1)}), bf16[16,2,3,64,128]{4,3,2,1,0:T(8,128)(2,1)}, u32[]{:S(2)}, u32[]{:S(2)}) async-start(bf16[16,2,3,64,128]{4,3,2,1,0:T(8,128)(2,1)} %copy-done.7), calls=%async_computation.2 | async-start | bytes 3145728 | tf_op jit(solution)/shard_map/all_to_all | solution.py:306
  267.8 2.3 unstack_seqs.2
  270.1 4.8 %collective-permute-start.14 = (bf16[2,8,64,128]{3,2,1,0:T(8,128)(2,1)}, bf16[2,8,64,128]{3,2,1,0:T(8,128)(2,1)S(1)}, u32[]{:S(2)}, u32[]{:S(2)}) collective-permute-start(bf16[2,8,64,128]{3,2,1,0:T(8,128)(2,1)} %bitcast.225), channel_id=1, source_target_pairs={{0,80},{16,64},{32,112},{48,96},{64,16},{80,0},{96,48},{112,32},{1... | collective-permute-start | bytes 786440 | tf_op jit(solution)/shard_map/ppermute | solution.py:264
  276.0 3.0 collective-permute-start.15
  282.8 8.4 %collective-permute-done.15 = bf16[2,8,64,128]{3,2,1,0:T(8,128)(2,1)S(1)} collective-permute-done((bf16[2,8,64,128]{3,2,1,0:T(8,128)(2,1)}, bf16[2,8,64,128]{3,2,1,0:T(8,128)(2,1)S(1)}, u32[]{:S(2)}, u32[]{:S(2)}) %collective-permute-start.15) | collective-permute-done | bytes 262176 | tf_op jit(solution)/shard_map/ppermute | solution.py:264
  294.1 2.5 collective-permute-start.21
  309.8 12.8 %all-to-all-done.2 = bf16[16,2,3,64,128]{4,3,2,1,0:T(8,128)(2,1)} async-done(((bf16[16,2,3,64,128]{4,3,2,1,0:T(8,128)(2,1)}), bf16[16,2,3,64,128]{4,3,2,1,0:T(8,128)(2,1)}, u32[]{:S(2)}, u32[]{:S(2)}) %all-to-all-start.2) | async-done | bytes 1572896 | tf_op jit(solution)/shard_map/all_to_all | solution.py:306
  322.6 2.3 unstack_seqs.3
  (130 shorter events, 60.0 us)
Async XLA Ops:
  3.3 59.0 %all-to-all-start = ((bf16[16,2,4,64,128]{4,3,2,1,0:T(8,128)(2,1)}), bf16[16,2,4,64,128]{4,3,2,1,0:T(8,128)(2,1)}, u32[]{:S(2)}, u32[]{:S(2)}) async-start(bf16[16,2,4,64,128]{4,3,2,1,0:T(8,128)(2,1)} %bitcast.238), calls=%async_computation | async-start | bytes 4194304 | tf_op jit(solution)/shard_map/all_to_all | solution.py:306
  15.3 3.5 %collective-permute-start = (bf16[4,2,64,8,128]{4,3,2,1,0:T(8,128)(2,1)S(1)}, bf16[4,2,64,8,128]{4,3,2,1,0:T(8,128)(2,1)}, u32[]{:S(2)}, u32[]{:S(2)}) collective-permute-start(bf16[4,2,64,8,128]{4,3,2,1,0:T(8,128)(2,1)S(1)} %dynamic-slice_bitcast_fusion.1), channel_id=1, source_target_pairs={{0,16},{16,0},{32,48},{48,32},{64,80},{80,64},{96,112},{112,96},{1... | collective-permute-start | bytes 3145736 | tf_op jit(solution)/shard_map/ppermute | solution.py:264
  22.3 13.5 %collective-permute-start.1 = (bf16[2,64,16,128]{3,2,1,0:T(8,128)(2,1)}, bf16[2,64,16,128]{3,2,1,0:T(8,128)(2,1)}, u32[]{:S(2)}, u32[]{:S(2)}) collective-permute-start(bf16[2,64,16,128]{3,2,1,0:T(8,128)(2,1)} %get-tuple-element.80), channel_id=1, source_target_pairs={{0,64},{16,80},{32,96},{48,112},{64,0},{80,16},{96,32},{112,48},{1... | collective-permute-start | bytes 1572872 | tf_op jit(solution)/shard_map/ppermute | solution.py:264
  23.6 25.9 %collective-permute-start.2 = (bf16[2,64,16,128]{3,2,1,0:T(8,128)(2,1)}, bf16[2,64,16,128]{3,2,1,0:T(8,128)(2,1)}, u32[]{:S(2)}, u32[]{:S(2)}) collective-permute-start(bf16[2,64,16,128]{3,2,1,0:T(8,128)(2,1)} %get-tuple-element.81), channel_id=1, source_target_pairs={{0,128},{16,144},{32,160},{48,176},{64,192},{80,208},{96,224},{112... | collective-permute-start | bytes 1572872 | tf_op jit(solution)/shard_map/ppermute | solution.py:264
  28.8 25.1 %collective-permute-start.3 = (bf16[2,64,16,128]{3,2,1,0:T(8,128)(2,1)}, bf16[2,64,16,128]{3,2,1,0:T(8,128)(2,1)S(1)}, u32[]{:S(2)}, u32[]{:S(2)}) collective-permute-start(bf16[2,64,16,128]{3,2,1,0:T(8,128)(2,1)} %get-tuple-element.79), channel_id=1, source_target_pairs={{0,192},{16,208},{32,224},{48,240},{64,128},{80,144},{96,160},{112... | collective-permute-start | bytes 1572872 | tf_op jit(solution)/shard_map/ppermute | solution.py:264
  62.3 126.5 %all-to-all-start.1 = ((bf16[16,2,4,64,128]{4,3,2,1,0:T(8,128)(2,1)}), bf16[16,2,4,64,128]{4,3,2,1,0:T(8,128)(2,1)}, u32[]{:S(2)}, u32[]{:S(2)}) async-start(bf16[16,2,4,64,128]{4,3,2,1,0:T(8,128)(2,1)} %bitcast.239), calls=%async_computation.1 | async-start | bytes 4194304 | tf_op jit(solution)/shard_map/all_to_all | solution.py:306
  69.0 7.3 %collective-permute-start.4 = (bf16[4,2,64,8,128]{4,3,2,1,0:T(8,128)(2,1)S(1)}, bf16[4,2,64,8,128]{4,3,2,1,0:T(8,128)(2,1)S(1)}, u32[]{:S(2)}, u32[]{:S(2)}) collective-permute-start(bf16[4,2,64,8,128]{4,3,2,1,0:T(8,128)(2,1)S(1)} %dynamic-slice_bitcast_fusion), channel_id=1, source_target_pairs={{0,16},{16,0},{32,48},{48,32},{64,80},{80,64},{96,112},{112,96},{1... | collective-permute-start | bytes 3145736 | tf_op jit(solution)/shard_map/ppermute | solution.py:264
  72.0 116.8 %collective-permute-start.9 = (bf16[3,2,64,16,128]{4,3,2,1,0:T(8,128)(2,1)}, bf16[3,2,64,16,128]{4,3,2,1,0:T(8,128)(2,1)}, u32[]{:S(2)}, u32[]{:S(2)}) collective-permute-start(bf16[3,2,64,16,128]{4,3,2,1,0:T(8,128)(2,1)} %slice.85), channel_id=1, source_target_pairs={{0,32},{16,48},{32,0},{48,16},{64,96},{80,112},{96,64},{112,80},{1... | collective-permute-start | bytes 4718600 | tf_op jit(solution)/shard_map/ppermute | solution.py:264
  76.7 17.8 %collective-permute-start.5 = (bf16[2,64,16,128]{3,2,1,0:T(8,128)(2,1)S(1)}, bf16[2,64,16,128]{3,2,1,0:T(8,128)(2,1)S(1)}, u32[]{:S(2)}, u32[]{:S(2)}) collective-permute-start(bf16[2,64,16,128]{3,2,1,0:T(8,128)(2,1)S(1)} %get-tuple-element.77), channel_id=1, source_target_pairs={{0,64},{16,80},{32,96},{48,112},{64,0},{80,16},{96,32},{112,48},{1... | collective-permute-start | bytes 1572872 | tf_op jit(solution)/shard_map/ppermute | solution.py:264
  78.1 105.0 %collective-permute-start.8 = (bf16[2,64,16,128]{3,2,1,0:T(8,128)(2,1)S(1)}, bf16[2,64,16,128]{3,2,1,0:T(8,128)(2,1)S(1)}, u32[]{:S(2)}, u32[]{:S(2)}) collective-permute-start(bf16[2,64,16,128]{3,2,1,0:T(8,128)(2,1)S(1)} %slice_bitcast_fusion), channel_id=1, source_target_pairs={{32,0},{48,16},{96,64},{112,80},{160,128},{176,144},{224,192},{240... | collective-permute-start | bytes 1572872 | tf_op jit(solution)/shard_map/ppermute | solution.py:269
  79.4 24.3 %collective-permute-start.6 = (bf16[2,64,16,128]{3,2,1,0:T(8,128)(2,1)S(1)}, bf16[2,64,16,128]{3,2,1,0:T(8,128)(2,1)S(1)}, u32[]{:S(2)}, u32[]{:S(2)}) collective-permute-start(bf16[2,64,16,128]{3,2,1,0:T(8,128)(2,1)S(1)} %get-tuple-element.78), channel_id=1, source_target_pairs={{0,128},{16,144},{32,160},{48,176},{64,192},{80,208},{96,224},{112... | collective-permute-start | bytes 1572872 | tf_op jit(solution)/shard_map/ppermute | solution.py:264
  93.4 22.2 %collective-permute-start.7 = (bf16[2,64,16,128]{3,2,1,0:T(8,128)(2,1)S(1)}, bf16[2,64,16,128]{3,2,1,0:T(8,128)(2,1)S(1)}, u32[]{:S(2)}, u32[]{:S(2)}) collective-permute-start(bf16[2,64,16,128]{3,2,1,0:T(8,128)(2,1)S(1)} %get-tuple-element.76), channel_id=1, source_target_pairs={{0,192},{16,208},{32,224},{48,240},{64,128},{80,144},{96,160},{112... | collective-permute-start | bytes 1572872 | tf_op jit(solution)/shard_map/ppermute | solution.py:264
  188.9 61.8 %all-to-all-start.3 = ((bf16[16,2,3,64,128]{4,3,2,1,0:T(8,128)(2,1)}), bf16[16,2,3,64,128]{4,3,2,1,0:T(8,128)(2,1)}, u32[]{:S(2)}, u32[]{:S(2)}) async-start(bf16[16,2,3,64,128]{4,3,2,1,0:T(8,128)(2,1)} %copy-done.8), calls=%async_computation.3 | async-start | bytes 3145728 | tf_op jit(solution)/shard_map/all_to_all | solution.py:306
  205.6 26.1 %copy-start.2 = (bf16[4,2,64,16,128]{4,3,2,1,0:T(8,128)(2,1)S(1)}, bf16[4,2,64,16,128]{4,3,2,1,0:T(8,128)(2,1)}, u32[]{:S(2)}) copy-start(bf16[4,2,64,16,128]{4,3,2,1,0:T(8,128)(2,1)} %copy-done) | copy-start | bytes 6291460
  205.6 25.9 %collective-permute-start.10 = (f32[2,64,128]{2,1,0:T(8,128)S(1)}, f32[2,64,128]{2,1,0:T(8,128)S(1)}, u32[]{:S(2)}, u32[]{:S(2)}) collective-permute-start(f32[2,64,128]{2,1,0:T(8,128)S(1)} %time_stats.1.mine_ref), channel_id=1, source_target_pairs={{0,32},{16,48},{32,0},{48,16},{64,96},{80,112},{96,64},{112,80},{1... | collective-permute-start | bytes 196616 | tf_op jit(solution)/shard_map/ppermute | solution.py:264
  242.7 48.6 %collective-permute-start.19 = (bf16[3,64,16,128]{3,2,1,0:T(8,128)(2,1)S(1)}, bf16[3,64,16,128]{3,2,1,0:T(8,128)(2,1)}, u32[]{:S(2)}, u32[]{:S(2)}) collective-permute-start(bf16[3,64,16,128]{3,2,1,0:T(8,128)(2,1)S(1)} %get-tuple-element.45), channel_id=1, source_target_pairs={{0,32},{16,48},{32,0},{48,16},{64,96},{80,112},{96,64},{112,80},{1... | collective-permute-start | bytes 2359304 | tf_op jit(solution)/shard_map/ppermute | solution.py:264
  242.7 48.6 %collective-permute-start.18 = (bf16[64,16,128]{2,1,0:T(8,128)(2,1)}, bf16[64,16,128]{2,1,0:T(8,128)(2,1)}, u32[]{:S(2)}, u32[]{:S(2)}) collective-permute-start(bf16[64,16,128]{2,1,0:T(8,128)(2,1)} %get-tuple-element.53), channel_id=1, source_target_pairs={{0,32},{16,48},{64,96},{80,112},{128,160},{144,176},{192,224},{208... | collective-permute-start | bytes 786440 | tf_op jit(solution)/shard_map/ppermute | solution.py:269
  250.7 71.9 %all-to-all-start.2 = ((bf16[16,2,3,64,128]{4,3,2,1,0:T(8,128)(2,1)}), bf16[16,2,3,64,128]{4,3,2,1,0:T(8,128)(2,1)}, u32[]{:S(2)}, u32[]{:S(2)}) async-start(bf16[16,2,3,64,128]{4,3,2,1,0:T(8,128)(2,1)} %copy-done.7), calls=%async_computation.2 | async-start | bytes 3145728 | tf_op jit(solution)/shard_map/all_to_all | solution.py:306
  258.8 11.3 %collective-permute-start.11 = (bf16[2,8,64,128]{3,2,1,0:T(8,128)(2,1)}, bf16[2,8,64,128]{3,2,1,0:T(8,128)(2,1)}, u32[]{:S(2)}, u32[]{:S(2)}) collective-permute-start(bf16[2,8,64,128]{3,2,1,0:T(8,128)(2,1)} %bitcast.228), channel_id=1, source_target_pairs={{0,64},{16,80},{32,96},{48,112},{64,0},{80,16},{96,32},{112,48},{1... | collective-permute-start | bytes 786440 | tf_op jit(solution)/shard_map/ppermute | solution.py:264
  260.9 15.1 %collective-permute-start.12 = (bf16[2,8,64,128]{3,2,1,0:T(8,128)(2,1)}, bf16[2,8,64,128]{3,2,1,0:T(8,128)(2,1)}, u32[]{:S(2)}, u32[]{:S(2)}) collective-permute-start(bf16[2,8,64,128]{3,2,1,0:T(8,128)(2,1)} %bitcast.227), channel_id=1, source_target_pairs={{0,192},{16,208},{32,224},{48,240},{64,128},{80,144},{96,160},{112... | collective-permute-start | bytes 786440 | tf_op jit(solution)/shard_map/ppermute | solution.py:264
  264.1 15.9 %collective-permute-start.13 = (bf16[2,8,64,128]{3,2,1,0:T(8,128)(2,1)}, bf16[2,8,64,128]{3,2,1,0:T(8,128)(2,1)}, u32[]{:S(2)}, u32[]{:S(2)}) collective-permute-start(bf16[2,8,64,128]{3,2,1,0:T(8,128)(2,1)} %bitcast.226), channel_id=1, source_target_pairs={{0,128},{16,144},{32,160},{48,176},{64,192},{80,208},{96,224},{112... | collective-permute-start | bytes 786440 | tf_op jit(solution)/shard_map/ppermute | solution.py:264
  270.1 11.9 %collective-permute-start.14 = (bf16[2,8,64,128]{3,2,1,0:T(8,128)(2,1)}, bf16[2,8,64,128]{3,2,1,0:T(8,128)(2,1)S(1)}, u32[]{:S(2)}, u32[]{:S(2)}) collective-permute-start(bf16[2,8,64,128]{3,2,1,0:T(8,128)(2,1)} %bitcast.225), channel_id=1, source_target_pairs={{0,80},{16,64},{32,112},{48,96},{64,16},{80,0},{96,48},{112,32},{1... | collective-permute-start | bytes 786440 | tf_op jit(solution)/shard_map/ppermute | solution.py:264
  276.0 15.2 %collective-permute-start.15 = (bf16[2,8,64,128]{3,2,1,0:T(8,128)(2,1)}, bf16[2,8,64,128]{3,2,1,0:T(8,128)(2,1)S(1)}, u32[]{:S(2)}, u32[]{:S(2)}) collective-permute-start(bf16[2,8,64,128]{3,2,1,0:T(8,128)(2,1)} %bitcast.259), channel_id=1, source_target_pairs={{0,208},{16,192},{32,240},{48,224},{64,144},{80,128},{96,176},{112... | collective-permute-start | bytes 786440 | tf_op jit(solution)/shard_map/ppermute | solution.py:264
  280.0 11.2 %collective-permute-start.16 = (bf16[2,8,64,128]{3,2,1,0:T(8,128)(2,1)}, bf16[2,8,64,128]{3,2,1,0:T(8,128)(2,1)S(1)}, u32[]{:S(2)}, u32[]{:S(2)}) collective-permute-start(bf16[2,8,64,128]{3,2,1,0:T(8,128)(2,1)} %bitcast.258), channel_id=1, source_target_pairs={{0,144},{16,128},{32,176},{48,160},{64,208},{80,192},{96,240},{112... | collective-permute-start | bytes 786440 | tf_op jit(solution)/shard_map/ppermute | solution.py:264
  282.1 9.2 %collective-permute-start.17 = (bf16[2,8,64,128]{3,2,1,0:T(8,128)(2,1)}, bf16[2,8,64,128]{3,2,1,0:T(8,128)(2,1)S(1)}, u32[]{:S(2)}, u32[]{:S(2)}) collective-permute-start(bf16[2,8,64,128]{3,2,1,0:T(8,128)(2,1)} %bitcast.257), channel_id=1, source_target_pairs={{0,16},{16,0},{32,48},{48,32},{64,80},{80,64},{96,112},{112,96},{1... | collective-permute-start | bytes 786440 | tf_op jit(solution)/shard_map/ppermute | solution.py:264
  293.8 8.0 %collective-permute-start.20 = (bf16[1,8,64,128]{3,2,1,0:T(8,128)(2,1)S(1)}, bf16[1,8,64,128]{3,2,1,0:T(8,128)(2,1)S(1)}, u32[]{:S(2)}, u32[]{:S(2)}) collective-permute-start(bf16[1,8,64,128]{3,2,1,0:T(8,128)(2,1)S(1)} %bitcast.266), channel_id=1, source_target_pairs={{0,64},{16,80},{32,96},{48,112},{64,0},{80,16},{96,32},{112,48},{1... | collective-permute-start | bytes 393224 | tf_op jit(solution)/shard_map/ppermute | solution.py:264
  294.1 9.5 %collective-permute-start.21 = (bf16[1,8,64,128]{3,2,1,0:T(8,128)(2,1)S(1)}, bf16[1,8,64,128]{3,2,1,0:T(8,128)(2,1)S(1)}, u32[]{:S(2)}, u32[]{:S(2)}) collective-permute-start(bf16[1,8,64,128]{3,2,1,0:T(8,128)(2,1)S(1)} %bitcast.265), channel_id=1, source_target_pairs={{0,192},{16,208},{32,224},{48,240},{64,128},{80,144},{96,160},{112... | collective-permute-start | bytes 393224 | tf_op jit(solution)/shard_map/ppermute | solution.py:264
  296.6 7.2 %collective-permute-start.22 = (bf16[1,8,64,128]{3,2,1,0:T(8,128)(2,1)S(1)}, bf16[1,8,64,128]{3,2,1,0:T(8,128)(2,1)S(1)}, u32[]{:S(2)}, u32[]{:S(2)}) collective-permute-start(bf16[1,8,64,128]{3,2,1,0:T(8,128)(2,1)S(1)} %bitcast.264), channel_id=1, source_target_pairs={{0,128},{16,144},{32,160},{48,176},{64,192},{80,208},{96,224},{112... | collective-permute-start | bytes 393224 | tf_op jit(solution)/shard_map/ppermute | solution.py:264
  297.8 7.9 %collective-permute-start.23 = (bf16[1,8,64,128]{3,2,1,0:T(8,128)(2,1)S(1)}, bf16[1,8,64,128]{3,2,1,0:T(8,128)(2,1)S(1)}, u32[]{:S(2)}, u32[]{:S(2)}) collective-permute-start(bf16[1,8,64,128]{3,2,1,0:T(8,128)(2,1)S(1)} %bitcast.263), channel_id=1, source_target_pairs={{0,80},{16,64},{32,112},{48,96},{64,16},{80,0},{96,48},{112,32},{1... | collective-permute-start | bytes 393224 | tf_op jit(solution)/shard_map/ppermute | solution.py:264
  299.2 8.7 %collective-permute-start.24 = (bf16[1,8,64,128]{3,2,1,0:T(8,128)(2,1)S(1)}, bf16[1,8,64,128]{3,2,1,0:T(8,128)(2,1)S(1)}, u32[]{:S(2)}, u32[]{:S(2)}) collective-permute-start(bf16[1,8,64,128]{3,2,1,0:T(8,128)(2,1)S(1)} %bitcast.262), channel_id=1, source_target_pairs={{0,208},{16,192},{32,240},{48,224},{64,144},{80,128},{96,176},{112... | collective-permute-start | bytes 393224 | tf_op jit(solution)/shard_map/ppermute | solution.py:264
  301.9 7.9 %collective-permute-start.25 = (bf16[1,8,64,128]{3,2,1,0:T(8,128)(2,1)S(1)}, bf16[1,8,64,128]{3,2,1,0:T(8,128)(2,1)S(1)}, u32[]{:S(2)}, u32[]{:S(2)}) collective-permute-start(bf16[1,8,64,128]{3,2,1,0:T(8,128)(2,1)S(1)} %bitcast.261), channel_id=1, source_target_pairs={{0,144},{16,128},{32,176},{48,160},{64,208},{80,192},{96,240},{112... | collective-permute-start | bytes 393224 | tf_op jit(solution)/shard_map/ppermute | solution.py:264
  303.6 6.2 %collective-permute-start.26 = (bf16[1,8,64,128]{3,2,1,0:T(8,128)(2,1)S(1)}, bf16[1,8,64,128]{3,2,1,0:T(8,128)(2,1)S(1)}, u32[]{:S(2)}, u32[]{:S(2)}) collective-permute-start(bf16[1,8,64,128]{3,2,1,0:T(8,128)(2,1)S(1)} %bitcast.260), channel_id=1, source_target_pairs={{0,16},{16,0},{32,48},{48,32},{64,80},{80,64},{96,112},{112,96},{1... | collective-permute-start | bytes 393224 | tf_op jit(solution)/shard_map/ppermute | solution.py:264
  (15 other events, 79.7 us)
